TPU v7x, 32 devices: a whole 2x2x4 slice. The times are simulated.
32 devices in a mesh: rep: 2 (over y), seq: 4 (over z), mp: 2 (over x), sub: 2 (over core).
Axes of the slice: x: 2, y: 2, z: 4, core: 2. Of those that a mesh axis runs over, the one named last changes fastest.
Arguments:
- normed_inputs: bfloat16 [4096, 5120], P(('rep', 'seq', 'sub'), 'mp'), parts along dimension 0, may hold values from -6 to 6
- base_queries: bfloat16 [4096, 8192], P(('rep', 'seq', 'sub'), 'mp'), parts along dimension 0, may hold values from -8 to 8
- base_keys: bfloat16 [4096, 1024], P(('rep', 'seq', 'sub'), 'mp'), parts along dimension 0, may hold values from -8 to 8
- base_values: bfloat16 [4096, 1024], P(('rep', 'seq', 'sub'), 'mp'), parts along dimension 0, may hold values from -6 to 6
- adapter_down: bfloat16 [8, 5120, 16], P(None, 'mp'), may hold values from -0.078125 to 0.078125
- adapter_up: bfloat16 [8, 16, 8192], P(None, None, 'mp'), may hold values from -0.75 to 0.75
- position_document: int32 [4096], P(('rep', 'seq', 'sub')), parts along dimension 0, may hold values from 0 to 15, never falling along the last dimension, each value on 1 to 768 neighbouring positions
- document_tenant: int32 [32], P('rep'), parts along dimension 0, may hold values from 0 to 7, as said below
- output_gradient: bfloat16 [4096, 8192], P(('rep', 'seq', 'sub'), 'mp'), parts along dimension 0, may hold values from -6 to 6
Outputs:
- attn_out: bfloat16 [4096, 8192], P(('rep', 'seq', 'sub'), 'mp'), parts along dimension 0
- grad_a: float32 [16, 5120, 16], P('rep', 'mp'), parts along dimension 0
- grad_b: float32 [16, 16, 8192], P('rep', None, 'mp'), parts along dimension 0
There are 2 independent parts, one for each index of `rep`. A program takes and returns all parts, laid end to end along the dimension named above; an argument that names none is the same for every part. Nothing has to cross between parts.
Inputs may be any that keep to these rules, and one draw needn't show every extreme that they name: `position_document`: Non-decreasing along the row; each document spans 1 to 768 positions, and one spans exactly that many. `document_tenant`: every tenant owns exactly 2 documents.
All inputs are finite; a program needn't handle non-finite values.
Results may differ from a plain program's by a relative error of at most 0.035.
Values may be sent and summed in bfloat16 or wider, within the bound.
No kernel may reach another device: no remote copies, remote signals or barrier semaphores. Data moves between devices by JAX's collectives and lax.ppermute only.
A program may use at most 192 MiB of HBM per device.

v0:
```python
import functools

import jax
import jax.numpy as jnp
from jax import lax
from jax.experimental import pallas as pl
from jax.experimental.pallas import tpu as pltpu
from jax.sharding import PartitionSpec as P

HEAD = 128
REACH = 3
NEG = -1e30
LIFT = 2.0
LOG2E = 1.4426950408889634
TAIL = 16
VMEM_BYTES = 48 * 1024 * 1024
VMEM_MOST = 60 * 1024 * 1024
VMEM_HEADS = 57 * 1024 * 1024

VM = pl.BlockSpec(memory_space=pltpu.VMEM)
SM = pl.BlockSpec(memory_space=pltpu.SMEM)
ANY = pl.BlockSpec(memory_space=pl.ANY)


def nt(a, b):
    return lax.dot_general(a, b, (((1,), (1,)), ((), ())), preferred_element_type=jnp.float32)


def nn(a, b):
    return jnp.dot(a, b, preferred_element_type=jnp.float32)


def params(limit=VMEM_BYTES):
    return pltpu.CompilerParams(vmem_limit_bytes=limit)


def fetch(pairs, sems):
    copies = [pltpu.make_async_copy(src, dst, sems.at[i]) for i, (src, dst) in enumerate(pairs)]
    for copy in copies:
        copy.start()
    return copies


def pack_kernel(keys, values, doc, *rest):
    outs, (ids, blocks, sems) = rest[:-3], rest[-3:]
    rows, width = keys.shape
    part = width // len(outs)
    pairs = [(doc, ids)]
    for c in range(len(outs)):
        cols = pl.ds(c * part, part)
        pairs.append((keys.at[:, cols], blocks.at[c, pl.ds(0, rows), pl.ds(0, part)]))
        pairs.append((values.at[:, cols], blocks.at[c, pl.ds(0, rows), pl.ds(part, part)]))
    loads = fetch(pairs, sems.at[pl.ds(0, len(pairs))])
    loads[0].wait()
    tail = jnp.broadcast_to((ids[...] + 1).astype(jnp.float32), (TAIL, rows)).astype(jnp.bfloat16)
    stores = []
    for c, out in enumerate(outs):
        blocks[c, rows:, :] = jnp.zeros((TAIL, 2 * part), jnp.bfloat16)
        blocks[c, rows:, 0:rows] = tail
        loads[1 + 2 * c].wait()
        loads[2 + 2 * c].wait()
        stores += fetch([(blocks.at[c], out)], sems.at[pl.ds(len(pairs) + c, 1)])
    for store in stores:
        store.wait()


def pack(keys, values, doc, chunks):
    rows, width = keys.shape
    shape = (rows + TAIL, 2 * width // chunks)
    return pl.pallas_call(
        pack_kernel,
        out_shape=[jax.ShapeDtypeStruct(shape, jnp.bfloat16)] * chunks,
        in_specs=[ANY] * 3,
        out_specs=[ANY] * chunks,
        scratch_shapes=[
            pltpu.VMEM((1, rows), jnp.int32),
            pltpu.VMEM((chunks, *shape), jnp.bfloat16),
            pltpu.SemaphoreType.DMA((1 + 3 * chunks,)),
        ],
        compiler_params=params(VMEM_MOST),
        cost_estimate=pl.CostEstimate(flops=0, bytes_accessed=8 * rows * width, transcendentals=0),
        name="pack_keys_values",
    )(keys, values, doc)


def relay_kernel(own, got, after, out, got_out, held, sems):
    sub = lax.axis_index("sub")

    def move(source):
        load = pltpu.make_async_copy(source, held, sems.at[0])
        load.start()
        load.wait()

    @pl.when(sub == 0)
    def _():
        move(own)

    @pl.when(sub != 0)
    def _():
        move(got)

    store = pltpu.make_async_copy(held, out, sems.at[1])
    store.start()
    store.wait()


def relay(own, got, after):
    shape = jax.ShapeDtypeStruct(own.shape, own.dtype)
    return pl.pallas_call(
        relay_kernel,
        out_shape=[shape, shape],
        in_specs=[ANY, ANY, ANY],
        out_specs=[ANY, ANY],
        input_output_aliases={1: 1},
        scratch_shapes=[pltpu.VMEM(own.shape, own.dtype), pltpu.SemaphoreType.DMA((2,))],
        compiler_params=params(),
        cost_estimate=pl.CostEstimate(flops=0, bytes_accessed=4 * own.size, transcendentals=0),
        name="relay_block",
    )(own, got, after)


def selector_of(owner, tenants, rank):
    rows = owner.shape[1]
    tenant = lax.broadcasted_iota(jnp.int32, (tenants * rank, rows), 0) // rank
    return tenant == owner


def fold(full, owner, tenants, rank):
    kept = jnp.where(selector_of(owner, tenants, rank), full, 0.0)
    total = kept[0:rank]
    for t in range(1, tenants):
        total = total + kept[t * rank : (t + 1) * rank]
    return total


def unfold(compact, owner, tenants, rank):
    spread = jnp.concatenate([compact] * tenants, axis=0)
    return jnp.where(selector_of(owner, tenants, rank), spread, 0.0)


def down_kernel(tenants, rank, x_hbm, adapter_hbm, doc_hbm, tenant_of, info, x, adapter, doc, sems):
    copies = fetch([(doc_hbm, doc), (x_hbm, x), (adapter_hbm, adapter)], sems)
    copies[0].wait()
    ids = doc[...]
    found = jnp.zeros(ids.shape, jnp.int32)
    for s in range(tenant_of.shape[0]):
        found = jnp.where(ids == s, tenant_of[s], found)
    info[rank:, :] = jnp.broadcast_to(found.astype(jnp.float32), (info.shape[0] - rank, ids.shape[1]))
    copies[1].wait()
    copies[2].wait()
    info[0:rank, :] = fold(nt(x[...], adapter[...]).T, found, tenants, rank)


def down_project(x, adapter, doc, tenant_of, tenants, rank):
    rows, width = x.shape
    return pl.pallas_call(
        functools.partial(down_kernel, tenants, rank),
        out_shape=jax.ShapeDtypeStruct((rank + 8, rows), jnp.float32),
        in_specs=[ANY, ANY, ANY, SM],
        out_specs=VM,
        scratch_shapes=[
            pltpu.VMEM(x.shape, x.dtype),
            pltpu.VMEM(adapter.shape, adapter.dtype),
            pltpu.VMEM(doc.shape, doc.dtype),
            pltpu.SemaphoreType.DMA((3,)),
        ],
        compiler_params=params(VMEM_MOST),
        cost_estimate=pl.CostEstimate(
            flops=2 * rows * width * tenants * rank,
            bytes_accessed=2 * width * (rows + tenants * rank),
            transcendentals=0,
        ),
        name="down_project",
    )(x, adapter, doc, tenant_of)


def owner_of(info, rank):
    return info[rank : rank + 1, :].astype(jnp.int32)


def turn(x):
    return x.astype(jnp.float32).T.astype(jnp.bfloat16)


def attention(
    head, at, count, group, base, grad, up, blocks, with_ids, info, terms, before, tenants, rank
):
    rows, width = base.shape
    window = (REACH + 1) * rows
    tall = tenants * rank
    half = tall // 2
    span = group * HEAD
    pair = min(4, group)
    scale = HEAD**-0.5
    wide = lambda r: pl.BlockSpec((r, span), lambda i: (0, i + head))
    narrow = pl.BlockSpec((half, span), lambda i: (0, i))
    keys = pl.BlockSpec((rows, HEAD), lambda i: (0, i + at))
    skip = blocks[0].shape[1] // (2 * HEAD)
    values = pl.BlockSpec((rows, HEAD), lambda i: (0, i + at + skip))
    ids = pl.BlockSpec((TAIL, rows), lambda i: (rows // TAIL, 0))
    same = lambda a: pl.BlockSpec(a.shape, lambda i: (0, 0))
    operands, specs = [base, grad, up], [wide(rows), wide(rows), wide(tall)]
    for block in blocks:
        operands += [block, block]
        specs += [keys, values]
    operands += [*with_ids, info, *terms]
    specs += [ids] * 4 + [same(info)] * 3
    if before is not None:
        operands += [before[1], before[0]]
        specs += [same(before[1]), ANY]
    held = dict(
        kw=pltpu.VMEM((window, HEAD), jnp.bfloat16),
        vw=pltpu.VMEM((window, HEAD), jnp.bfloat16),
        kt=pltpu.VMEM((HEAD, window), jnp.bfloat16),
        vt=pltpu.VMEM((HEAD + TAIL, window), jnp.bfloat16),
        bottle=pltpu.VMEM((rows, tall), jnp.bfloat16),
        bottle_t=pltpu.VMEM((tall, rows), jnp.bfloat16),
        bias=pltpu.VMEM((window, rows), jnp.float32),
        query=pltpu.VMEM((span, rows), jnp.bfloat16),
        gt=pltpu.VMEM((span, rows), jnp.bfloat16),
        gquery=pltpu.VMEM((span, rows), jnp.bfloat16),
        scores=pltpu.VMEM((pair, window, rows), jnp.float32),
        part=pltpu.VMEM((tall, span), jnp.bfloat16),
        total=pltpu.VMEM((tall, rows), jnp.float32),
        reach=pltpu.SMEM((1,), jnp.int32),
    )

    def kernel(*refs):
        base, grad, up = refs[0:3]
        kv, tails, info, terms = refs[3:11], refs[11:15], refs[15], refs[16:18]
        out, keep, send, projected = refs[len(operands) : len(operands) + 4]
        r = dict(zip(held, refs[len(operands) + 4 :]))
        kw, vw, kt, vt = (r[n] for n in ("kw", "vw", "kt", "vt"))
        bias, query, gt, gquery, scores = (
            r[n] for n in ("bias", "query", "gt", "gquery", "scores")
        )
        sub = lax.axis_index("sub")
        step = pl.program_id(0)

        @pl.when(step == 0)
        def _():
            owner = owner_of(info, rank)
            lifted = unfold((terms[0][...] + terms[1][...])[0:rank], owner, tenants, rank)
            r["bottle_t"][...] = lifted.astype(jnp.bfloat16)
            r["bottle"][...] = lifted.T.astype(jnp.bfloat16)
            r["total"][...] = jnp.zeros((tall, rows), jnp.float32)
            vt[HEAD:, :] = jnp.ones((TAIL, window), jnp.bfloat16)
            own, two, swap, passed = (ref[...].astype(jnp.float32) for ref in tails)
            near = jnp.where(sub == 0, swap, passed)
            far = jnp.where(sub == 0, passed, swap)
            mine = own[0:1, :]
            lowest = jnp.min(mine)
            reach = 0
            for slot, block in ((REACH, own), (2, near), (1, two), (0, far)):
                same = block.T[:, 0:1] == mine
                if slot == REACH:
                    same = same & (
                        lax.broadcasted_iota(jnp.int32, (rows, rows), 0)
                        <= lax.broadcasted_iota(jnp.int32, (rows, rows), 1)
                    )
                else:
                    reach = jnp.where(jnp.max(block[0:1, :]) == lowest, REACH - slot, reach)
                bias[slot * rows : (slot + 1) * rows, :] = jnp.where(same, 0.0, NEG)
            r["reach"][0] = reach

        def place(slot, k_ref, v_ref):
            at = slice(slot * rows, (slot + 1) * rows)
            k, v = k_ref[...], v_ref[...]
            kw[at, :] = k
            vw[at, :] = v
            kt[:, at] = turn(k)
            vt[0:HEAD, at] = turn(v)

        place(REACH, *kv[0:2])
        place(1, *kv[2:4])

        @pl.when(sub == 0)
        def _():
            place(2, *kv[4:6])
            place(0, *kv[6:8])

        @pl.when(sub != 0)
        def _():
            place(2, *kv[6:8])
            place(0, *kv[4:6])

        lift = LIFT * nn(r["bottle"][...], up[...])
        query[...] = (base[...].astype(jnp.float32) + lift).T.astype(jnp.bfloat16)
        gt[...] = turn(grad[...])

        def run(reached, numbers):
            chunks = [slice(c * rows, (c + 1) * rows) for c in range(REACH - reached, REACH + 1)]
            spans = [pl.ds(pl.multiple_of(h * HEAD, HEAD), HEAD) for h in numbers]
            peaks = []
            for i, span_i in enumerate(spans):
                q, peak = query[span_i, :], None
                for c in chunks:
                    s = nn(kw[c, :], q) + bias[c, :]
                    scores[i, c, :] = s
                    top = jnp.max(s, axis=0, keepdims=True)
                    peak = top if peak is None else jnp.maximum(peak, top)
                peaks.append(peak)
            inverses, rowdots = [], []
            for i, span_i in enumerate(spans):
                total = None
                for c in chunks:
                    w = jnp.exp2((scores[i, c, :] - peaks[i]) * (scale * LOG2E))
                    scores[i, c, :] = w
                    o = nn(vt[:, c], w.astype(jnp.bfloat16))
                    total = o if total is None else total + o
                inverse = 1.0 / total[HEAD : HEAD + 1, :]
                attn = total[0:HEAD, :] * inverse
                out[:, span_i] = attn.T.astype(jnp.bfloat16)
                attn = attn.astype(jnp.bfloat16)
                product = gt[span_i, :].astype(jnp.float32) * attn.astype(jnp.float32)
                rowdots.append(jnp.sum(product, axis=0, keepdims=True))
                inverses.append(inverse)
            for i, span_i in enumerate(spans):
                g, moved = gt[span_i, :], None
                for c in chunks:
                    dprob = nn(vw[c, :], g)
                    ds = (scores[i, c, :] * (dprob - rowdots[i])).astype(jnp.bfloat16)
                    dq = nn(kt[:, c], ds)
                    moved = dq if moved is None else moved + dq
                gquery[span_i, :] = (moved * (inverses[i] * (LIFT * scale))).astype(jnp.bfloat16)

        for reached in range(REACH + 1):

            @pl.when(r["reach"][0] == reached)
            def _():
                @pl.loop(0, group // pair)
                def _(i):
                    run(reached, [i * pair + k for k in range(pair)])

        r["part"][...] = nt(r["bottle_t"][...], gquery[...]).astype(jnp.bfloat16)
        keep[...] = r["part"][pl.ds(pl.multiple_of(sub * half, half), half), :]
        send[...] = r["part"][pl.ds(pl.multiple_of((1 - sub) * half, half), half), :]
        r["total"][...] += nn(up[...], gquery[...])

        @pl.when(step == count - 1)
        def _():
            folded = fold(r["total"][...], owner_of(info, rank), tenants, rank)
            projected[...] = folded if before is None else folded + refs[18][...]

    return pl.pallas_call(
        kernel,
        grid=(count,),
        out_shape=[
            jax.ShapeDtypeStruct((rows, width), jnp.bfloat16),
            *halves_of(tall, count * span),
            jax.ShapeDtypeStruct((rank, rows), jnp.float32),
        ],
        in_specs=specs,
        out_specs=[wide(rows), narrow, narrow, pl.BlockSpec((rank, rows), lambda i: (0, 0))],
        scratch_shapes=list(held.values()),
        input_output_aliases={19: 0} if before is not None else {},
        compiler_params=params(VMEM_HEADS),
        cost_estimate=pl.CostEstimate(
            flops=8 * rows * window * span * count,
            bytes_accessed=6 * rows * span * count,
            transcendentals=rows * window * group * count,
        ),
        name="attention",
    )(*operands)


def small_call(kernel, name, shapes, *operands, after=(), through=(), scratch=()):
    size = sum(2 * a.size for a in operands)
    count, results = len(operands), jax.tree.leaves(shapes)
    given = (*operands, *after, *through)
    outs = len(given) + len(results)
    calls = pl.pallas_call(
        lambda *refs: kernel(
            *refs[:count], *refs[len(given) : outs], *refs[outs + len(through) :]
        ),
        out_shape=results + [jax.ShapeDtypeStruct(a.shape, a.dtype) for a in through],
        in_specs=[VM] * count + [ANY] * (len(after) + len(through)),
        out_specs=[VM] * len(results) + [ANY] * len(through),
        scratch_shapes=list(scratch),
        input_output_aliases={
            count + len(after) + i: len(results) + i for i in range(len(through))
        },
        compiler_params=params(),
        cost_estimate=pl.CostEstimate(flops=size, bytes_accessed=2 * size, transcendentals=0),
        name=name,
    )(*given)
    return calls if isinstance(shapes, list) or through else calls[0]


def grad_a_of(tenants, rank, one, other, info, x):
    g = unfold((one[...] + other[...]), owner_of(info[...], rank), tenants, rank)
    return nn(g.astype(jnp.bfloat16), x[...]).astype(jnp.bfloat16)


def grad_a_kernel(tenants, rank, one, other, info, x, out):
    out[...] = grad_a_of(tenants, rank, one, other, info, x)


def split_kernel(tenants, rank, one, other, info, x, keep, send):
    part = grad_a_of(tenants, rank, one, other, info, x)
    half = keep.shape[0]
    sub = lax.axis_index("sub")

    @pl.when(sub == 0)
    def _():
        keep[...] = part[0:half, :]
        send[...] = part[half:, :]

    @pl.when(sub != 0)
    def _():
        keep[...] = part[half:, :]
        send[...] = part[0:half, :]


def scatter_kernel(size, count, *refs):
    mine, *sends, total = refs[2 * count :]
    col = 0
    for keep, got in zip(refs[0 : 2 * count : 2], refs[1 : 2 * count : 2]):
        both = keep[...].astype(jnp.float32) + got[...].astype(jnp.float32)
        total[:, col : col + keep.shape[1]] = both.astype(jnp.bfloat16)
        col += keep.shape[1]
    me = lax.axis_index("seq")
    rows = mine.shape[0]
    for d, out in enumerate((mine, *sends)):
        at = pl.multiple_of(lax.rem(me + d, size) * rows, rows)
        out[...] = total[pl.ds(at, rows), :]


def sum_kernel(*refs):
    total = refs[0][...].astype(jnp.float32)
    for ref in refs[1:-1]:
        total = total + ref[...].astype(jnp.float32)
    refs[-1][...] = total.astype(jnp.bfloat16)


def gather_kernel(size, *refs):
    pieces, out = refs[:-1], refs[-1]
    me = lax.axis_index("seq")
    rows = pieces[0].shape[0]
    for d, piece in enumerate(pieces):
        at = pl.multiple_of(lax.rem(me + size - d, size) * rows, rows)
        out[pl.ds(at, rows), :] = piece[...]


def gather(pieces, after=()):
    size, (rows, width) = len(pieces), pieces[0].shape
    return small_call(
        functools.partial(gather_kernel, size), "gather_grads",
        jax.ShapeDtypeStruct((rows * size, width), jnp.bfloat16), *pieces, after=after,
    )


def finish_kernel(count, *refs):
    grad_b, grad_a = refs[2 * count :]
    sub = lax.axis_index("sub")
    half, wide = refs[0].shape[0], grad_b.shape[1]
    here = pl.ds(pl.multiple_of(sub * half, half), half)
    there = pl.ds(pl.multiple_of((1 - sub) * half, half), half)
    for at, group in ((here, refs[0 : 2 * count : 2]), (there, refs[1 : 2 * count : 2])):
        col = 0
        for ref in group:
            width = ref.shape[1]
            first = min(width, wide - col)
            grad_b[at, col : col + first] = ref[:, 0:first].astype(jnp.float32)
            if first < width:
                grad_a[at, :] = ref[:, first:].astype(jnp.float32)
            col += width


def finish(pairs, wide):
    rows, width = pairs[0][0].shape[0] * 2, sum(half.shape[1] for half, _ in pairs)
    return small_call(
        functools.partial(finish_kernel, len(pairs)), "finish_grads",
        [
            jax.ShapeDtypeStruct((rows, wide), jnp.float32),
            jax.ShapeDtypeStruct((rows, width - wide), jnp.float32),
        ],
        *[block for pair in pairs for block in pair],
    )


def halves_of(rows, width):
    return [jax.ShapeDtypeStruct((rows // 2, width), jnp.bfloat16)] * 2


def scatter(*pairs, after=()):
    size = lax.axis_size("seq")
    rows, width = pairs[0][0].shape[0], sum(keep.shape[1] for keep, _ in pairs)
    shard = jax.ShapeDtypeStruct((rows // size, width), jnp.bfloat16)
    return small_call(
        functools.partial(scatter_kernel, size, len(pairs)), "scatter_grads", [shard] * size,
        *[block for pair in pairs for block in pair],
        after=after, scratch=[pltpu.VMEM((rows, width), jnp.bfloat16)],
    )


def exchange(shards):
    return [shards[0]] + [rotate_over(block, "seq", d + 1) for d, block in enumerate(shards[1:])]


def add_up(pieces, after=(), through=()):
    shape = jax.ShapeDtypeStruct(pieces[0].shape, pieces[0].dtype)
    return small_call(sum_kernel, "sum_grads", shape, *pieces, after=after, through=through)


def spread(shard):
    return [shard] + [rotate_over(shard, "seq", d) for d in range(1, lax.axis_size("seq"))]


def swap_over(block, axis):
    return lax.ppermute(block, axis, [(0, 1), (1, 0)])


def rotate_over(block, axis, d):
    size = lax.axis_size(axis)
    return lax.ppermute(block, axis, [(i, (i + d) % size) for i in range(size)])


def terms_over(block, axis):
    if lax.axis_size(axis) == 2:
        return block, swap_over(block, axis)
    return lax.psum(block, axis), jnp.zeros_like(block)


def shift_over(block, axis):
    size = lax.axis_size(axis)
    return lax.ppermute(block, axis, [(i, i + 1) for i in range(size - 1)])


def body(
    normed_inputs, base_queries, base_keys, base_values, adapter_down, adapter_up,
    position_document, document_tenant, output_gradient,
):
    rows, width = normed_inputs.shape
    tenants, _, rank = adapter_down.shape
    tall, up_width = tenants * rank, adapter_up.shape[2]
    doc = position_document.reshape(1, rows)
    adapter = jnp.transpose(adapter_down, (0, 2, 1)).reshape(tall, width)
    up = adapter_up.reshape(tall, up_width)
    key_heads = base_keys.shape[1] // HEAD
    chunks = 2 if key_heads % 4 == 0 else 1
    size = lax.axis_size("seq")
    by_hand = chunks == 2 and tall % (2 * TAIL * size) == 0

    own = pack(base_keys, base_values, doc, chunks)
    info = down_project(normed_inputs, adapter, doc, document_tenant, tenants, rank)
    terms = terms_over(info, "mp")
    group = base_queries.shape[1] // HEAD // key_heads
    per = key_heads // chunks
    counts = [1, per - 1, per] if chunks == 2 else [1] * per
    state, pairs, held, with_ids, head = None, [], [], None, 0
    for i, count in enumerate(counts):
        chunk = head // per
        if len(held) < chunks and i < 2:
            two = shift_over(own[i], "seq")
            passing, two = relay(own[i], two, terms[1] if i == 0 else state[1])
            held.append((own[i], two, swap_over(two, "sub"), shift_over(passing, ("seq", "sub"))))
        with_ids = held[0]
        out, keep, send, gdown = attention(
            head, head % per, count, group, base_queries, output_gradient, up, held[chunk],
            with_ids, info, terms, state, tenants, rank,
        )
        state = (out, gdown)
        pairs.append((keep, send))
        head += count
    if by_hand:
        keep_late, send_late = pairs[-1]
        one, other = terms_over(gdown, "mp")
        swapped = [(keep, swap_over(send, "sub")) for keep, send in pairs[:-1]]
        pieces = exchange(scatter(*swapped, after=[keep_late]))
        early = add_up(pieces)
        keep_a, send_a = small_call(
            functools.partial(split_kernel, tenants, rank), "split_grads", halves_of(tall, width),
            one, other, info, normed_inputs, after=pieces[1:2],
        )
        shards = scatter(
            (keep_late, swap_over(send_late, "sub")), (keep_a, swap_over(send_a, "sub")), after=[early]
        )
        late = add_up(exchange(shards))
        half_early = gather(spread(early), after=[late])
        other_early = swap_over(half_early, "sub")
        half_late = gather(spread(late), after=[other_early])
        grad_b, grad_a = finish(
            [(half_early, other_early), (half_late, swap_over(half_late, "sub"))], up_width
        )
    else:
        one, other = terms_over(gdown, "mp")
        part_a = small_call(
            functools.partial(grad_a_kernel, tenants, rank), "grad_a_part",
            jax.ShapeDtypeStruct((tall, width), jnp.bfloat16), one, other, info, normed_inputs,
        )
        grad_a = lax.psum(part_a, ("seq", "sub")).astype(jnp.float32)
        keeps = jnp.concatenate([keep for keep, _ in pairs], axis=1)
        sends = jnp.concatenate([send for _, send in pairs], axis=1)
        low = lax.axis_index("sub") == 0
        part_b = jnp.concatenate([jnp.where(low, keeps, sends), jnp.where(low, sends, keeps)])
        grad_b = lax.psum(part_b, ("seq", "sub")).astype(jnp.float32)
    grad_a = jnp.transpose(grad_a.reshape(tenants, rank, width), (0, 2, 1))
    return out, grad_a, grad_b.reshape(tenants, rank, up_width)


def solution(mesh):
    split = P(("rep", "seq", "sub"), "mp")
    in_specs = (
        split, split, split, split, P(None, "mp", None), P(None, None, "mp"),
        P(("rep", "seq", "sub")), P("rep"), split,
    )
    out_specs = (split, P("rep", "mp", None), P("rep", None, "mp"))
    return jax.shard_map(body, mesh=mesh, in_specs=in_specs, out_specs=out_specs, check_vma=False)
```

profile of v0, /device:TPU:0, one launch (start us, length us, event | category | flops | bytes accessed | tf_op | source)
XLA Modules:
  0.0 120.3 jit_solution(4697967672121770445)
XLA Ops:
  0.6 1.9 %pack_keys_values.1 = (bf16[272,512]{1,0:T(8,128)(2,1)}, bf16[272,512]{1,0:T(8,128)(2,1)}) custom-call(bf16[256,512]{1,0:T(8,128)(2,1)} %keys.1, bf16[256,512]{1,0:T(8,128)(2,1)} %values.1, s32[1,256]{1,0:T(1,128)} %bitcast.13), custom_call_target="tpu_custom_call" | custom-call | bytes 1048576 | tf_op jit(solution)/shard_map/pack_keys_values/pallas_call | solution.py:70
  2.5 5.1 %collective-permute-start.1 = (bf16[272,512]{1,0:T(8,128)(2,1)}, bf16[272,512]{1,0:T(8,128)(2,1)S(1)}, u32[]{:S(2)}, u32[]{:S(2)}) collective-permute-start(bf16[272,512]{1,0:T(8,128)(2,1)} %get-tuple-element.34.own.refs_3_.refs_4_.refs_11_), channel_id=1, source_target_pairs={{0,4},{4,8},{8,12},{1,5},{5,9},{9,13},{2,6},{6,10},{10,14},{3,7},{... | collective-permute-start | bytes 835592 | tf_op jit(solution)/shard_map/ppermute | solution.py:527
  7.6 3.4 %down_project.1.refs_15_.refs_16_.refs_2_ = f32[24,256]{1,0:T(8,128)} custom-call(bf16[256,2560]{1,0:T(8,128)(2,1)} %refs_3_.1, bf16[128,2560]{1,0:T(8,128)(2,1)} %bitcast.12, s32[1,256]{1,0:T(1,128)} %bitcast.14, s32[16]{0:T(128)} %tenant_of.1), custom_call_target="tpu_custom_call" | custom-call | flops 167772160 | bytes 1966080 | tf_op jit(solution)/shard_map/down_project/pallas_call | solution.py:156
  11.0 1.6 %collective-permute-start.2 = (f32[24,256]{1,0:T(8,128)}, f32[24,256]{1,0:T(8,128)S(1)}, u32[]{:S(2)}, u32[]{:S(2)}) collective-permute-start(f32[24,256]{1,0:T(8,128)} %down_project.1.refs_15_.refs_16_.refs_2_), channel_id=1, source_target_pairs={{0,2},{2,0},{1,3},{3,1},{4,6},{6,4},{5,7},{7,5},{8,10},{10,8},{9,1... | collective-permute-start | bytes 73736 | tf_op jit(solution)/shard_map/ppermute | solution.py:511
  12.5 2.5 %collective-permute-done.2.after.refs_17_ = f32[24,256]{1,0:T(8,128)S(1)} collective-permute-done((f32[24,256]{1,0:T(8,128)}, f32[24,256]{1,0:T(8,128)S(1)}, u32[]{:S(2)}, u32[]{:S(2)}) %collective-permute-start.2) | collective-permute-done | bytes 24608 | tf_op jit(solution)/shard_map/ppermute | solution.py:511
  15.1 0.1 relay_block.2
  15.2 1.3 %collective-permute-start.4 = (bf16[272,512]{1,0:T(8,128)(2,1)S(1)}, bf16[272,512]{1,0:T(8,128)(2,1)S(1)}, u32[]{:S(2)}, u32[]{:S(2)}) collective-permute-start(bf16[272,512]{1,0:T(8,128)(2,1)S(1)} %get-tuple-element.36), channel_id=1, source_target_pairs={{0,1},{1,4},{4,5},{5,8},{8,9},{9,12},{12,13},{2,3},{3,6},{6,7},{7,... | collective-permute-start | bytes 835592 | tf_op jit(solution)/shard_map/ppermute | solution.py:527
  16.5 2.3 %collective-permute-start.3 = (bf16[272,512]{1,0:T(8,128)(2,1)S(1)}, bf16[272,512]{1,0:T(8,128)(2,1)S(1)}, u32[]{:S(2)}, u32[]{:S(2)}) collective-permute-start(bf16[272,512]{1,0:T(8,128)(2,1)S(1)} %get-tuple-element.35.refs_5_.refs_6_.refs_12_), channel_id=1, source_target_pairs={{0,1},{1,0},{2,3},{3,2},{4,5},{5,4},{6,7},{7,6},{8,9},{9,8},{10,11... | collective-permute-start | bytes 835592 | tf_op jit(solution)/shard_map/ppermute | solution.py:511
  18.9 3.5 %collective-permute-start = (bf16[272,512]{1,0:T(8,128)(2,1)S(1)}, bf16[272,512]{1,0:T(8,128)(2,1)S(1)}, u32[]{:S(2)}, u32[]{:S(2)}) collective-permute-start(bf16[272,512]{1,0:T(8,128)(2,1)S(1)} %copy-done.6), channel_id=1, source_target_pairs={{0,4},{4,8},{8,12},{1,5},{5,9},{9,13},{2,6},{6,10},{10,14},{3,7},{... | collective-permute-start | bytes 835592 | tf_op jit(solution)/shard_map/ppermute | solution.py:527
  22.5 0.7 copy-done.13
  23.1 0.1 copy-done.14
  23.2 6.6 %attention.3 = (bf16[256,4096]{1,0:T(8,128)(2,1)}, bf16[64,1024]{1,0:T(8,128)(2,1)}, bf16[64,1024]{1,0:T(8,128)(2,1)}, f32[16,256]{1,0:T(8,128)}) custom-call(bf16[256,4096]{1,0:T(8,128)(2,1)} %refs_0_.5, bf16[256,4096]{1,0:T(8,128)(2,1)} %refs_1_.5, bf16[128,4096]{1,0:T(8,128)(2,1)} %bitcast.9, ...), custom_call_target="tpu_custom_call" | custom-call | flops 2147483648 | bytes 1572864 | tf_op jit(solution)/shard_map/attention/pallas_call | solution.py:345
  29.8 0.7 copy-done.11
  30.7 3.0 %collective-permute-start.6 = (bf16[272,512]{1,0:T(8,128)(2,1)S(1)}, bf16[272,512]{1,0:T(8,128)(2,1)S(1)}, u32[]{:S(2)}, u32[]{:S(2)}) collective-permute-start(bf16[272,512]{1,0:T(8,128)(2,1)S(1)} %get-tuple-element.39), channel_id=1, source_target_pairs={{0,1},{1,4},{4,5},{5,8},{8,9},{9,12},{12,13},{2,3},{3,6},{6,7},{7,... | collective-permute-start | bytes 835592 | tf_op jit(solution)/shard_map/ppermute | solution.py:527
  33.6 2.5 %collective-permute-start.5 = (bf16[272,512]{1,0:T(8,128)(2,1)S(1)}, bf16[272,512]{1,0:T(8,128)(2,1)S(1)}, u32[]{:S(2)}, u32[]{:S(2)}) collective-permute-start(bf16[272,512]{1,0:T(8,128)(2,1)S(1)} %get-tuple-element.38.refs_5_.refs_6_), channel_id=1, source_target_pairs={{0,1},{1,0},{2,3},{3,2},{4,5},{5,4},{6,7},{7,6},{8,9},{9,8},{10,11... | collective-permute-start | bytes 835592 | tf_op jit(solution)/shard_map/ppermute | solution.py:511
  36.3 7.0 %attention.4 = (bf16[256,4096]{1,0:T(8,128)(2,1)}, bf16[64,1024]{1,0:T(8,128)(2,1)}, bf16[64,1024]{1,0:T(8,128)(2,1)}, f32[16,256]{1,0:T(8,128)}) custom-call(bf16[256,4096]{1,0:T(8,128)(2,1)} %refs_0_.5, bf16[256,4096]{1,0:T(8,128)(2,1)} %refs_1_.5, bf16[128,4096]{1,0:T(8,128)(2,1)} %bitcast.10, ...), custom_call_target="tpu_custom_call", output_to_operand_aliasing={{0}: (19, {})} | custom-call | flops 2147483648 | bytes 1572864 | tf_op jit(solution)/shard_map/attention/pallas_call | solution.py:345
  43.3 1.6 %collective-permute-start.8 = (bf16[64,1024]{1,0:T(8,128)(2,1)}, bf16[64,1024]{1,0:T(8,128)(2,1)S(1)}, u32[]{:S(2)}, u32[]{:S(2)}) collective-permute-start(bf16[64,1024]{1,0:T(8,128)(2,1)} %get-tuple-element.47), channel_id=1, source_target_pairs={{0,1},{1,0},{2,3},{3,2},{4,5},{5,4},{6,7},{7,6},{8,9},{9,8},{10,11... | collective-permute-start | bytes 393224 | tf_op jit(solution)/shard_map/ppermute | solution.py:511
  45.0 0.7 copy-done.15
  45.7 0.1 copy-done.16
  45.8 11.7 %attention.5 = (bf16[256,4096]{1,0:T(8,128)(2,1)}, bf16[64,2048]{1,0:T(8,128)(2,1)}, bf16[64,2048]{1,0:T(8,128)(2,1)}, f32[16,256]{1,0:T(8,128)}) custom-call(bf16[256,4096]{1,0:T(8,128)(2,1)} %refs_0_.5, bf16[256,4096]{1,0:T(8,128)(2,1)} %refs_1_.5, bf16[128,4096]{1,0:T(8,128)(2,1)} %bitcast.11, ...), custom_call_target="tpu_custom_call", output_to_operand_aliasing={{0}: (19, {})} | custom-call | flops 4294967296 | bytes 3145728 | tf_op jit(solution)/shard_map/attention/pallas_call | solution.py:345
  57.5 0.9 copy-done.3
  58.5 0.1 scatter_grads.2
  58.6 3.5 %collective-permute-start.9 = (bf16[16,2048]{1,0:T(8,128)(2,1)S(1)}, bf16[16,2048]{1,0:T(8,128)(2,1)S(1)}, u32[]{:S(2)}, u32[]{:S(2)}) collective-permute-start(bf16[16,2048]{1,0:T(8,128)(2,1)S(1)} %get-tuple-element.50), channel_id=1, source_target_pairs={{0,4},{4,8},{8,12},{12,0},{1,5},{5,9},{9,13},{13,1},{2,6},{6,10},{... | collective-permute-start | bytes 196616 | tf_op jit(solution)/shard_map/ppermute | solution.py:516
  62.1 1.5 %collective-permute-start.16 = (f32[16,256]{1,0:T(8,128)}, f32[16,256]{1,0:T(8,128)S(1)}, u32[]{:S(2)}, u32[]{:S(2)}) collective-permute-start(f32[16,256]{1,0:T(8,128)} %get-tuple-element.54.refs_0_), channel_id=1, source_target_pairs={{0,2},{2,0},{1,3},{3,1},{4,6},{6,4},{5,7},{7,5},{8,10},{10,8},{9,1... | collective-permute-start | bytes 49160 | tf_op jit(solution)/shard_map/ppermute | solution.py:511
  63.6 2.5 %collective-permute-done.16.refs_1_ = f32[16,256]{1,0:T(8,128)S(1)} collective-permute-done((f32[16,256]{1,0:T(8,128)}, f32[16,256]{1,0:T(8,128)S(1)}, u32[]{:S(2)}, u32[]{:S(2)}) %collective-permute-start.16) | collective-permute-done | bytes 16416 | tf_op jit(solution)/shard_map/ppermute | solution.py:511
  66.1 3.2 %collective-permute-done.9.refs_1_.refs_4_ = bf16[16,2048]{1,0:T(8,128)(2,1)S(1)} collective-permute-done((bf16[16,2048]{1,0:T(8,128)(2,1)S(1)}, bf16[16,2048]{1,0:T(8,128)(2,1)S(1)}, u32[]{:S(2)}, u32[]{:S(2)}) %collective-permute-start.9) | collective-permute-done | bytes 65568 | tf_op jit(solution)/shard_map/ppermute | solution.py:516
  69.3 0.7 copy-done.12
  70.0 0.4 split_grads.1
  70.4 0.8 collective-permute-start.17
  71.3 1.9 %collective-permute-start.10 = (bf16[16,2048]{1,0:T(8,128)(2,1)S(1)}, bf16[16,2048]{1,0:T(8,128)(2,1)S(1)}, u32[]{:S(2)}, u32[]{:S(2)}) collective-permute-start(bf16[16,2048]{1,0:T(8,128)(2,1)S(1)} %get-tuple-element.51), channel_id=1, source_target_pairs={{0,8},{4,12},{8,0},{12,4},{1,9},{5,13},{9,1},{13,5},{2,10},{6,14},... | collective-permute-start | bytes 196616 | tf_op jit(solution)/shard_map/ppermute | solution.py:516
  73.3 4.0 %collective-permute-done.10.refs_2_ = bf16[16,2048]{1,0:T(8,128)(2,1)S(1)} collective-permute-done((bf16[16,2048]{1,0:T(8,128)(2,1)S(1)}, bf16[16,2048]{1,0:T(8,128)(2,1)S(1)}, u32[]{:S(2)}, u32[]{:S(2)}) %collective-permute-start.10) | collective-permute-done | bytes 65568 | tf_op jit(solution)/shard_map/ppermute | solution.py:516
  77.3 1.3 %collective-permute-done.11.refs_3_ = bf16[16,2048]{1,0:T(8,128)(2,1)S(1)} collective-permute-done((bf16[16,2048]{1,0:T(8,128)(2,1)S(1)}, bf16[16,2048]{1,0:T(8,128)(2,1)S(1)}, u32[]{:S(2)}, u32[]{:S(2)}) %collective-permute-start.11) | collective-permute-done | bytes 65568 | tf_op jit(solution)/shard_map/ppermute | solution.py:516
  78.6 0.3 scatter_grads.3
  78.9 0.7 collective-permute-start.18
  79.6 2.6 %collective-permute-start.19 = (bf16[16,4608]{1,0:T(8,128)(2,1)S(1)}, bf16[16,4608]{1,0:T(8,128)(2,1)S(1)}, u32[]{:S(2)}, u32[]{:S(2)}) collective-permute-start(bf16[16,4608]{1,0:T(8,128)(2,1)S(1)} %get-tuple-element.59), channel_id=1, source_target_pairs={{0,8},{4,12},{8,0},{12,4},{1,9},{5,13},{9,1},{13,5},{2,10},{6,14},... | collective-permute-start | bytes 442376 | tf_op jit(solution)/shard_map/ppermute | solution.py:516
  82.3 0.6 collective-permute-start.20
  82.8 1.2 %collective-permute-start.14 = (bf16[16,2048]{1,0:T(8,128)(2,1)S(1)}, bf16[16,2048]{1,0:T(8,128)(2,1)S(1)}, u32[]{:S(2)}, u32[]{:S(2)}) collective-permute-start(bf16[16,2048]{1,0:T(8,128)(2,1)S(1)} %sum_grads.2.refs_4_.refs_0_), channel_id=1, source_target_pairs={{0,12},{4,0},{8,4},{12,8},{1,13},{5,1},{9,5},{13,9},{2,14},{6,2},{... | collective-permute-start | bytes 196616 | tf_op jit(solution)/shard_map/ppermute | solution.py:516
  84.0 1.7 %collective-permute-start.13 = (bf16[16,2048]{1,0:T(8,128)(2,1)S(1)}, bf16[16,2048]{1,0:T(8,128)(2,1)S(1)}, u32[]{:S(2)}, u32[]{:S(2)}) collective-permute-start(bf16[16,2048]{1,0:T(8,128)(2,1)S(1)} %sum_grads.2.refs_4_.refs_0_), channel_id=1, source_target_pairs={{0,8},{4,12},{8,0},{12,4},{1,9},{5,13},{9,1},{13,5},{2,10},{6,14},... | collective-permute-start | bytes 196616 | tf_op jit(solution)/shard_map/ppermute | solution.py:516
  85.7 1.9 %collective-permute-done.18.refs_1_ = bf16[16,4608]{1,0:T(8,128)(2,1)S(1)} collective-permute-done((bf16[16,4608]{1,0:T(8,128)(2,1)S(1)}, bf16[16,4608]{1,0:T(8,128)(2,1)S(1)}, u32[]{:S(2)}, u32[]{:S(2)}) %collective-permute-start.18) | collective-permute-done | bytes 147488 | tf_op jit(solution)/shard_map/ppermute | solution.py:516
  87.6 5.4 %collective-permute-done.19.refs_2_ = bf16[16,4608]{1,0:T(8,128)(2,1)S(1)} collective-permute-done((bf16[16,4608]{1,0:T(8,128)(2,1)S(1)}, bf16[16,4608]{1,0:T(8,128)(2,1)S(1)}, u32[]{:S(2)}, u32[]{:S(2)}) %collective-permute-start.19) | collective-permute-done | bytes 147488 | tf_op jit(solution)/shard_map/ppermute | solution.py:516
  93.1 0.7 collective-permute-done.14.refs_3_
  93.8 7.5 %collective-permute-done.13.refs_2_ = bf16[16,2048]{1,0:T(8,128)(2,1)S(1)} collective-permute-done((bf16[16,2048]{1,0:T(8,128)(2,1)S(1)}, bf16[16,2048]{1,0:T(8,128)(2,1)S(1)}, u32[]{:S(2)}, u32[]{:S(2)}) %collective-permute-start.13) | collective-permute-done | bytes 65568 | tf_op jit(solution)/shard_map/ppermute | solution.py:516
  101.4 1.2 collective-permute-start.23
  102.6 0.8 collective-permute-start.22
  103.5 4.4 %collective-permute-done.24.refs_3_ = bf16[16,4608]{1,0:T(8,128)(2,1)S(1)} collective-permute-done((bf16[16,4608]{1,0:T(8,128)(2,1)S(1)}, bf16[16,4608]{1,0:T(8,128)(2,1)S(1)}, u32[]{:S(2)}, u32[]{:S(2)}) %collective-permute-start.24) | collective-permute-done | bytes 147488 | tf_op jit(solution)/shard_map/ppermute | solution.py:516
  107.8 8.5 %collective-permute-done.23.refs_2_ = bf16[16,4608]{1,0:T(8,128)(2,1)S(1)} collective-permute-done((bf16[16,4608]{1,0:T(8,128)(2,1)S(1)}, bf16[16,4608]{1,0:T(8,128)(2,1)S(1)}, u32[]{:S(2)}, u32[]{:S(2)}) %collective-permute-start.23) | collective-permute-done | bytes 147488 | tf_op jit(solution)/shard_map/ppermute | solution.py:516
  116.4 2.0 %collective-permute-done.25.refs_3_ = bf16[64,4608]{1,0:T(8,128)(2,1)S(1)} collective-permute-done((bf16[64,4608]{1,0:T(8,128)(2,1)S(1)}, bf16[64,4608]{1,0:T(8,128)(2,1)S(1)}, u32[]{:S(2)}, u32[]{:S(2)}) %collective-permute-start.25) | collective-permute-done | bytes 589856 | tf_op jit(solution)/shard_map/ppermute | solution.py:511
  118.4 1.9 %finish_grads.1 = (f32[128,4096]{1,0:T(8,128)}, f32[128,2560]{1,0:T(8,128)}) custom-call(bf16[64,2048]{1,0:T(8,128)(2,1)S(1)} %gather_grads.2.refs_0_, bf16[64,2048]{1,0:T(8,128)(2,1)S(1)} %collective-permute-done.21.refs_4_.refs_1_, bf16[64,4608]{1,0:T(8,128)(2,1)S(1)} %gather_grads.3.refs_2_, bf16[64,4608]{1,0:T(8,128)(2,1)S(1)} %collective-permute-done.25.refs_3_), custom_call_target="tpu_custom_call" | custom-call | flops 1703936 | bytes 3407872 | tf_op jit(solution)/shard_map/finish_grads/pallas_call | solution.py:372
  (55 shorter events, 0.8 us)
Async XLA Ops:
  2.5 12.6 %copy-start = (bf16[272,512]{1,0:T(8,128)(2,1)S(1)}, bf16[272,512]{1,0:T(8,128)(2,1)}, u32[]{:S(2)}) copy-start(bf16[272,512]{1,0:T(8,128)(2,1)} %get-tuple-element.34.own.refs_3_.refs_4_.refs_11_) | copy-start | bytes 835588
  2.5 16.4 %copy-start.6 = (bf16[272,512]{1,0:T(8,128)(2,1)S(1)}, bf16[272,512]{1,0:T(8,128)(2,1)}, u32[]{:S(2)}) copy-start(bf16[272,512]{1,0:T(8,128)(2,1)} %get-tuple-element.33.own.refs_3_.refs_4_) | copy-start | bytes 835588
  2.5 12.6 %collective-permute-start.1 = (bf16[272,512]{1,0:T(8,128)(2,1)}, bf16[272,512]{1,0:T(8,128)(2,1)S(1)}, u32[]{:S(2)}, u32[]{:S(2)}) collective-permute-start(bf16[272,512]{1,0:T(8,128)(2,1)} %get-tuple-element.34.own.refs_3_.refs_4_.refs_11_), channel_id=1, source_target_pairs={{0,4},{4,8},{8,12},{1,5},{5,9},{9,13},{2,6},{6,10},{10,14},{3,7},{... | collective-permute-start | bytes 835592 | tf_op jit(solution)/shard_map/ppermute | solution.py:527
  11.0 4.1 %collective-permute-start.2 = (f32[24,256]{1,0:T(8,128)}, f32[24,256]{1,0:T(8,128)S(1)}, u32[]{:S(2)}, u32[]{:S(2)}) collective-permute-start(f32[24,256]{1,0:T(8,128)} %down_project.1.refs_15_.refs_16_.refs_2_), channel_id=1, source_target_pairs={{0,2},{2,0},{1,3},{3,1},{4,6},{6,4},{5,7},{7,5},{8,10},{10,8},{9,1... | collective-permute-start | bytes 73736 | tf_op jit(solution)/shard_map/ppermute | solution.py:511
  15.1 7.3 %copy-start.8 = (f32[24,256]{1,0:T(8,128)}, f32[24,256]{1,0:T(8,128)S(1)}, u32[]{:S(2)}) copy-start(f32[24,256]{1,0:T(8,128)S(1)} %collective-permute-done.2.after.refs_17_) | copy-start | bytes 73732
  15.2 7.2 %copy-start.1 = (bf16[272,512]{1,0:T(8,128)(2,1)}, bf16[272,512]{1,0:T(8,128)(2,1)S(1)}, u32[]{:S(2)}) copy-start(bf16[272,512]{1,0:T(8,128)(2,1)S(1)} %get-tuple-element.35.refs_5_.refs_6_.refs_12_) | copy-start | bytes 835588
  15.2 7.2 %collective-permute-start.4 = (bf16[272,512]{1,0:T(8,128)(2,1)S(1)}, bf16[272,512]{1,0:T(8,128)(2,1)S(1)}, u32[]{:S(2)}, u32[]{:S(2)}) collective-permute-start(bf16[272,512]{1,0:T(8,128)(2,1)S(1)} %get-tuple-element.36), channel_id=1, source_target_pairs={{0,1},{1,4},{4,5},{5,8},{8,9},{9,12},{12,13},{2,3},{3,6},{6,7},{7,... | collective-permute-start | bytes 835592 | tf_op jit(solution)/shard_map/ppermute | solution.py:527
  16.5 5.9 %collective-permute-start.3 = (bf16[272,512]{1,0:T(8,128)(2,1)S(1)}, bf16[272,512]{1,0:T(8,128)(2,1)S(1)}, u32[]{:S(2)}, u32[]{:S(2)}) collective-permute-start(bf16[272,512]{1,0:T(8,128)(2,1)S(1)} %get-tuple-element.35.refs_5_.refs_6_.refs_12_), channel_id=1, source_target_pairs={{0,1},{1,0},{2,3},{3,2},{4,5},{5,4},{6,7},{7,6},{8,9},{9,8},{10,11... | collective-permute-start | bytes 835592 | tf_op jit(solution)/shard_map/ppermute | solution.py:511
  18.9 10.9 %collective-permute-start = (bf16[272,512]{1,0:T(8,128)(2,1)S(1)}, bf16[272,512]{1,0:T(8,128)(2,1)S(1)}, u32[]{:S(2)}, u32[]{:S(2)}) collective-permute-start(bf16[272,512]{1,0:T(8,128)(2,1)S(1)} %copy-done.6), channel_id=1, source_target_pairs={{0,4},{4,8},{8,12},{1,5},{5,9},{9,13},{2,6},{6,10},{10,14},{3,7},{... | collective-permute-start | bytes 835592 | tf_op jit(solution)/shard_map/ppermute | solution.py:527
  22.4 0.7 copy-start.13
  22.4 0.8 copy-start.14
  29.8 0.7 copy-start.11
  30.7 12.6 %copy-start.7 = (bf16[272,512]{1,0:T(8,128)(2,1)}, bf16[272,512]{1,0:T(8,128)(2,1)S(1)}, u32[]{:S(2)}) copy-start(bf16[272,512]{1,0:T(8,128)(2,1)S(1)} %get-tuple-element.38.refs_5_.refs_6_) | copy-start | bytes 835588
  30.7 14.3 %collective-permute-start.6 = (bf16[272,512]{1,0:T(8,128)(2,1)S(1)}, bf16[272,512]{1,0:T(8,128)(2,1)S(1)}, u32[]{:S(2)}, u32[]{:S(2)}) collective-permute-start(bf16[272,512]{1,0:T(8,128)(2,1)S(1)} %get-tuple-element.39), channel_id=1, source_target_pairs={{0,1},{1,4},{4,5},{5,8},{8,9},{9,12},{12,13},{2,3},{3,6},{6,7},{7,... | collective-permute-start | bytes 835592 | tf_op jit(solution)/shard_map/ppermute | solution.py:527
  33.6 11.3 %collective-permute-start.5 = (bf16[272,512]{1,0:T(8,128)(2,1)S(1)}, bf16[272,512]{1,0:T(8,128)(2,1)S(1)}, u32[]{:S(2)}, u32[]{:S(2)}) collective-permute-start(bf16[272,512]{1,0:T(8,128)(2,1)S(1)} %get-tuple-element.38.refs_5_.refs_6_), channel_id=1, source_target_pairs={{0,1},{1,0},{2,3},{3,2},{4,5},{5,4},{6,7},{7,6},{8,9},{9,8},{10,11... | collective-permute-start | bytes 835592 | tf_op jit(solution)/shard_map/ppermute | solution.py:511
  36.2 21.3 %collective-permute-start.7 = (bf16[64,1024]{1,0:T(8,128)(2,1)}, bf16[64,1024]{1,0:T(8,128)(2,1)S(1)}, u32[]{:S(2)}, u32[]{:S(2)}) collective-permute-start(bf16[64,1024]{1,0:T(8,128)(2,1)} %get-tuple-element.45), channel_id=1, source_target_pairs={{0,1},{1,0},{2,3},{3,2},{4,5},{5,4},{6,7},{7,6},{8,9},{9,8},{10,11... | collective-permute-start | bytes 393224 | tf_op jit(solution)/shard_map/ppermute | solution.py:511
  43.3 14.2 %collective-permute-start.8 = (bf16[64,1024]{1,0:T(8,128)(2,1)}, bf16[64,1024]{1,0:T(8,128)(2,1)S(1)}, u32[]{:S(2)}, u32[]{:S(2)}) collective-permute-start(bf16[64,1024]{1,0:T(8,128)(2,1)} %get-tuple-element.47), channel_id=1, source_target_pairs={{0,1},{1,0},{2,3},{3,2},{4,5},{5,4},{6,7},{7,6},{8,9},{9,8},{10,11... | collective-permute-start | bytes 393224 | tf_op jit(solution)/shard_map/ppermute | solution.py:511
  45.0 0.7 copy-start.15
  45.0 0.8 copy-start.16
  45.8 11.8 %copy-start.9 = (bf16[64,1024]{1,0:T(8,128)(2,1)S(1)}, bf16[64,1024]{1,0:T(8,128)(2,1)}, u32[]{:S(2)}) copy-start(bf16[64,1024]{1,0:T(8,128)(2,1)} %get-tuple-element.44.refs_0_) | copy-start | bytes 393220
  45.8 11.8 %copy-start.10 = (bf16[64,1024]{1,0:T(8,128)(2,1)S(1)}, bf16[64,1024]{1,0:T(8,128)(2,1)}, u32[]{:S(2)}) copy-start(bf16[64,1024]{1,0:T(8,128)(2,1)} %get-tuple-element.46.refs_2_) | copy-start | bytes 393220
  45.8 23.5 %copy-start.2 = (bf16[256,2560]{1,0:T(8,128)(2,1)S(1)}, bf16[256,2560]{1,0:T(8,128)(2,1)}, u32[]{:S(2)}) copy-start(bf16[256,2560]{1,0:T(8,128)(2,1)} %refs_3_.1) | copy-start | bytes 3932164
  45.8 23.5 %copy-start.5 = (f32[24,256]{1,0:T(8,128)S(1)}, f32[24,256]{1,0:T(8,128)}, u32[]{:S(2)}) copy-start(f32[24,256]{1,0:T(8,128)} %down_project.1.refs_15_.refs_16_.refs_2_) | copy-start | bytes 73732
  57.5 1.0 copy-start.3
  58.5 12.8 %copy-start.17 = (bf16[64,2048]{1,0:T(8,128)(2,1)S(1)}, bf16[64,2048]{1,0:T(8,128)(2,1)}, u32[]{:S(2)}) copy-start(bf16[64,2048]{1,0:T(8,128)(2,1)} %get-tuple-element.53) | copy-start | bytes 786436
  58.5 20.1 %copy-start.4 = (bf16[64,2048]{1,0:T(8,128)(2,1)S(1)}, bf16[64,2048]{1,0:T(8,128)(2,1)}, u32[]{:S(2)}) copy-start(bf16[64,2048]{1,0:T(8,128)(2,1)} %get-tuple-element.48.refs_4_.refs_0_) | copy-start | bytes 786436
  58.6 10.7 %collective-permute-start.9 = (bf16[16,2048]{1,0:T(8,128)(2,1)S(1)}, bf16[16,2048]{1,0:T(8,128)(2,1)S(1)}, u32[]{:S(2)}, u32[]{:S(2)}) collective-permute-start(bf16[16,2048]{1,0:T(8,128)(2,1)S(1)} %get-tuple-element.50), channel_id=1, source_target_pairs={{0,4},{4,8},{8,12},{12,0},{1,5},{5,9},{9,13},{13,1},{2,6},{6,10},{... | collective-permute-start | bytes 196616 | tf_op jit(solution)/shard_map/ppermute | solution.py:516
  62.1 3.9 %collective-permute-start.16 = (f32[16,256]{1,0:T(8,128)}, f32[16,256]{1,0:T(8,128)S(1)}, u32[]{:S(2)}, u32[]{:S(2)}) collective-permute-start(f32[16,256]{1,0:T(8,128)} %get-tuple-element.54.refs_0_), channel_id=1, source_target_pairs={{0,2},{2,0},{1,3},{3,1},{4,6},{6,4},{5,7},{7,5},{8,10},{10,8},{9,1... | collective-permute-start | bytes 49160 | tf_op jit(solution)/shard_map/ppermute | solution.py:511
  69.3 0.7 copy-start.12
  70.4 8.2 %collective-permute-start.17 = (bf16[64,2560]{1,0:T(8,128)(2,1)S(1)}, bf16[64,2560]{1,0:T(8,128)(2,1)S(1)}, u32[]{:S(2)}, u32[]{:S(2)}) collective-permute-start(bf16[64,2560]{1,0:T(8,128)(2,1)S(1)} %get-tuple-element.56), channel_id=1, source_target_pairs={{0,1},{1,0},{2,3},{3,2},{4,5},{5,4},{6,7},{7,6},{8,9},{9,8},{10,11... | collective-permute-start | bytes 983048 | tf_op jit(solution)/shard_map/ppermute | solution.py:511
  71.3 7.3 %collective-permute-start.15 = (bf16[64,2048]{1,0:T(8,128)(2,1)S(1)}, bf16[64,2048]{1,0:T(8,128)(2,1)S(1)}, u32[]{:S(2)}, u32[]{:S(2)}) collective-permute-start(bf16[64,2048]{1,0:T(8,128)(2,1)S(1)} %copy-done.17), channel_id=1, source_target_pairs={{0,1},{1,0},{2,3},{3,2},{4,5},{5,4},{6,7},{7,6},{8,9},{9,8},{10,11... | collective-permute-start | bytes 786440 | tf_op jit(solution)/shard_map/ppermute | solution.py:511
  71.3 5.9 %collective-permute-start.10 = (bf16[16,2048]{1,0:T(8,128)(2,1)S(1)}, bf16[16,2048]{1,0:T(8,128)(2,1)S(1)}, u32[]{:S(2)}, u32[]{:S(2)}) collective-permute-start(bf16[16,2048]{1,0:T(8,128)(2,1)S(1)} %get-tuple-element.51), channel_id=1, source_target_pairs={{0,8},{4,12},{8,0},{12,4},{1,9},{5,13},{9,1},{13,5},{2,10},{6,14},... | collective-permute-start | bytes 196616 | tf_op jit(solution)/shard_map/ppermute | solution.py:516
  73.3 5.3 %collective-permute-start.11 = (bf16[16,2048]{1,0:T(8,128)(2,1)S(1)}, bf16[16,2048]{1,0:T(8,128)(2,1)S(1)}, u32[]{:S(2)}, u32[]{:S(2)}) collective-permute-start(bf16[16,2048]{1,0:T(8,128)(2,1)S(1)} %get-tuple-element.52), channel_id=1, source_target_pairs={{0,12},{4,0},{8,4},{12,8},{1,13},{5,1},{9,5},{13,9},{2,14},{6,2},{... | collective-permute-start | bytes 196616 | tf_op jit(solution)/shard_map/ppermute | solution.py:516
  78.9 8.7 %collective-permute-start.18 = (bf16[16,4608]{1,0:T(8,128)(2,1)S(1)}, bf16[16,4608]{1,0:T(8,128)(2,1)S(1)}, u32[]{:S(2)}, u32[]{:S(2)}) collective-permute-start(bf16[16,4608]{1,0:T(8,128)(2,1)S(1)} %get-tuple-element.58), channel_id=1, source_target_pairs={{0,4},{4,8},{8,12},{12,0},{1,5},{5,9},{9,13},{13,1},{2,6},{6,10},{... | collective-permute-start | bytes 442376 | tf_op jit(solution)/shard_map/ppermute | solution.py:516
  79.6 13.4 %collective-permute-start.19 = (bf16[16,4608]{1,0:T(8,128)(2,1)S(1)}, bf16[16,4608]{1,0:T(8,128)(2,1)S(1)}, u32[]{:S(2)}, u32[]{:S(2)}) collective-permute-start(bf16[16,4608]{1,0:T(8,128)(2,1)S(1)} %get-tuple-element.59), channel_id=1, source_target_pairs={{0,8},{4,12},{8,0},{12,4},{1,9},{5,13},{9,1},{13,5},{2,10},{6,14},... | collective-permute-start | bytes 442376 | tf_op jit(solution)/shard_map/ppermute | solution.py:516
  82.3 10.8 %collective-permute-start.20 = (bf16[16,4608]{1,0:T(8,128)(2,1)S(1)}, bf16[16,4608]{1,0:T(8,128)(2,1)S(1)}, u32[]{:S(2)}, u32[]{:S(2)}) collective-permute-start(bf16[16,4608]{1,0:T(8,128)(2,1)S(1)} %get-tuple-element.60), channel_id=1, source_target_pairs={{0,12},{4,0},{8,4},{12,8},{1,13},{5,1},{9,5},{13,9},{2,14},{6,2},{... | collective-permute-start | bytes 442376 | tf_op jit(solution)/shard_map/ppermute | solution.py:516
  82.8 11.0 %collective-permute-start.14 = (bf16[16,2048]{1,0:T(8,128)(2,1)S(1)}, bf16[16,2048]{1,0:T(8,128)(2,1)S(1)}, u32[]{:S(2)}, u32[]{:S(2)}) collective-permute-start(bf16[16,2048]{1,0:T(8,128)(2,1)S(1)} %sum_grads.2.refs_4_.refs_0_), channel_id=1, source_target_pairs={{0,12},{4,0},{8,4},{12,8},{1,13},{5,1},{9,5},{13,9},{2,14},{6,2},{... | collective-permute-start | bytes 196616 | tf_op jit(solution)/shard_map/ppermute | solution.py:516
  84.0 17.2 %collective-permute-start.13 = (bf16[16,2048]{1,0:T(8,128)(2,1)S(1)}, bf16[16,2048]{1,0:T(8,128)(2,1)S(1)}, u32[]{:S(2)}, u32[]{:S(2)}) collective-permute-start(bf16[16,2048]{1,0:T(8,128)(2,1)S(1)} %sum_grads.2.refs_4_.refs_0_), channel_id=1, source_target_pairs={{0,8},{4,12},{8,0},{12,4},{1,9},{5,13},{9,1},{13,5},{2,10},{6,14},... | collective-permute-start | bytes 196616 | tf_op jit(solution)/shard_map/ppermute | solution.py:516
  87.6 13.6 %collective-permute-start.12 = (bf16[16,2048]{1,0:T(8,128)(2,1)S(1)}, bf16[16,2048]{1,0:T(8,128)(2,1)S(1)}, u32[]{:S(2)}, u32[]{:S(2)}) collective-permute-start(bf16[16,2048]{1,0:T(8,128)(2,1)S(1)} %sum_grads.2.refs_4_.refs_0_), channel_id=1, source_target_pairs={{0,4},{4,8},{8,12},{12,0},{1,5},{5,9},{9,13},{13,1},{2,6},{6,10},{... | collective-permute-start | bytes 196616 | tf_op jit(solution)/shard_map/ppermute | solution.py:516
  101.3 15.0 %collective-permute-start.21 = (bf16[64,2048]{1,0:T(8,128)(2,1)S(1)}, bf16[64,2048]{1,0:T(8,128)(2,1)S(1)}, u32[]{:S(2)}, u32[]{:S(2)}) collective-permute-start(bf16[64,2048]{1,0:T(8,128)(2,1)S(1)} %gather_grads.2.refs_0_), channel_id=1, source_target_pairs={{0,1},{1,0},{2,3},{3,2},{4,5},{5,4},{6,7},{7,6},{8,9},{9,8},{10,11... | collective-permute-start | bytes 786440 | tf_op jit(solution)/shard_map/ppermute | solution.py:511
  101.4 6.4 %collective-permute-start.24 = (bf16[16,4608]{1,0:T(8,128)(2,1)S(1)}, bf16[16,4608]{1,0:T(8,128)(2,1)S(1)}, u32[]{:S(2)}, u32[]{:S(2)}) collective-permute-start(bf16[16,4608]{1,0:T(8,128)(2,1)S(1)} %sum_grads.3.refs_4_.refs_0_), channel_id=1, source_target_pairs={{0,12},{4,0},{8,4},{12,8},{1,13},{5,1},{9,5},{13,9},{2,14},{6,2},{... | collective-permute-start | bytes 442376 | tf_op jit(solution)/shard_map/ppermute | solution.py:516
  101.4 14.8 %collective-permute-start.23 = (bf16[16,4608]{1,0:T(8,128)(2,1)S(1)}, bf16[16,4608]{1,0:T(8,128)(2,1)S(1)}, u32[]{:S(2)}, u32[]{:S(2)}) collective-permute-start(bf16[16,4608]{1,0:T(8,128)(2,1)S(1)} %sum_grads.3.refs_4_.refs_0_), channel_id=1, source_target_pairs={{0,8},{4,12},{8,0},{12,4},{1,9},{5,13},{9,1},{13,5},{2,10},{6,14},... | collective-permute-start | bytes 442376 | tf_op jit(solution)/shard_map/ppermute | solution.py:516
  102.6 13.7 %collective-permute-start.22 = (bf16[16,4608]{1,0:T(8,128)(2,1)S(1)}, bf16[16,4608]{1,0:T(8,128)(2,1)S(1)}, u32[]{:S(2)}, u32[]{:S(2)}) collective-permute-start(bf16[16,4608]{1,0:T(8,128)(2,1)S(1)} %sum_grads.3.refs_4_.refs_0_), channel_id=1, source_target_pairs={{0,4},{4,8},{8,12},{12,0},{1,5},{5,9},{9,13},{13,1},{2,6},{6,10},{... | collective-permute-start | bytes 442376 | tf_op jit(solution)/shard_map/ppermute | solution.py:516
  116.3 2.1 %collective-permute-start.25 = (bf16[64,4608]{1,0:T(8,128)(2,1)S(1)}, bf16[64,4608]{1,0:T(8,128)(2,1)S(1)}, u32[]{:S(2)}, u32[]{:S(2)}) collective-permute-start(bf16[64,4608]{1,0:T(8,128)(2,1)S(1)} %gather_grads.3.refs_2_), channel_id=1, source_target_pairs={{0,1},{1,0},{2,3},{3,2},{4,5},{5,4},{6,7},{7,6},{8,9},{9,8},{10,11... | collective-permute-start | bytes 1769480 | tf_op jit(solution)/shard_map/ppermute | solution.py:511
where the time goes:
time: 120 us
  waiting for transfers between devices  43.8 us (36%)
  starting transfers between devices  37.9 us (32%)
  Pallas kernels  33.8 us (28%)
  local copies, waits for them, and re-layouts  3.99 us (3%)
    ppermute x12, waiting for transfers between devices, rotate_over(): return lax.ppermute(block, axis, [(i, (i + d) % size) for i in range(size)])  36.8 us
    pallas_call x3, Pallas kernels, attention(): pl.pallas_call(kernel, grid=(count,), out_shape=[jax.ShapeDtypeStruct((ro...  25.4 us
    ppermute x12, starting transfers between devices, rotate_over(): return lax.ppermute(block, axis, [(i, (i + d) % size) for i in range(size)])  14.3 us
    ppermute x4, starting transfers between devices, shift_over(): return lax.ppermute(block, axis, [(i, i + 1) for i in range(size - 1)])  12.8 us
    ppermute x10, starting transfers between devices, swap_over(): return lax.ppermute(block, axis, [(0, 1), (1, 0)])  10.7 us
    ppermute x10, waiting for transfers between devices, swap_over(): return lax.ppermute(block, axis, [(0, 1), (1, 0)])  7.02 us
    unnamed x36, local copies, waits for them, and re-layouts  3.99 us
    pallas_call x1, Pallas kernels, down_project(): pl.pallas_call(functools.partial(down_kernel, tenants, rank), out_shape=j...  3.35 us
  transfers between devices with their start and end apart: 26, of which 12 were waited for; matrix products, arithmetic and copies ran while one was open for 0% of the time, Pallas kernels for 24%

commit v1 on v0

--- a/solution.py
+++ b/solution.py
@@ -190,7 +190,7 @@
     tall = tenants * rank
     half = tall // 2
     span = group * HEAD
-    pair = min(4, group)
+    pair = min(8, group)
     scale = HEAD**-0.5
     wide = lambda r: pl.BlockSpec((r, span), lambda i: (0, i + head))
     narrow = pl.BlockSpec((half, span), lambda i: (0, i))
@@ -324,9 +324,9 @@
                     moved = dq if moved is None else moved + dq
                 gquery[span_i, :] = (moved * (inverses[i] * (LIFT * scale))).astype(jnp.bfloat16)
 
-        for reached in range(REACH + 1):
-
-            @pl.when(r["reach"][0] == reached)
+        for reached in (1, REACH):
+
+            @pl.when((r["reach"][0] > 1) == (reached > 1))
             def _():
                 @pl.loop(0, group // pair)
                 def _(i):
@@ -434,19 +434,23 @@
 
 
 def gather_kernel(size, *refs):
-    pieces, out = refs[:-1], refs[-1]
+    pieces, out, col = refs[:-1], refs[-1], 0
     me = lax.axis_index("seq")
-    rows = pieces[0].shape[0]
-    for d, piece in enumerate(pieces):
-        at = pl.multiple_of(lax.rem(me + size - d, size) * rows, rows)
-        out[pl.ds(at, rows), :] = piece[...]
-
-
-def gather(pieces, after=()):
-    size, (rows, width) = len(pieces), pieces[0].shape
+    for first in range(0, len(pieces), size):
+        rows, width = pieces[first].shape
+        for d in range(size):
+            at = pl.multiple_of(lax.rem(me + size - d, size) * rows, rows)
+            out[pl.ds(at, rows), col : col + width] = pieces[first + d][...]
+        col += width
+
+
+def gather(*sums):
+    size, rows = len(sums[0]), sums[0][0].shape[0]
+    width = sum(pieces[0].shape[1] for pieces in sums)
     return small_call(
         functools.partial(gather_kernel, size), "gather_grads",
-        jax.ShapeDtypeStruct((rows * size, width), jnp.bfloat16), *pieces, after=after,
+        jax.ShapeDtypeStruct((rows * size, width), jnp.bfloat16),
+        *[piece for pieces in sums for piece in pieces],
     )
 
 
@@ -576,13 +580,10 @@
         shards = scatter(
             (keep_late, swap_over(send_late, "sub")), (keep_a, swap_over(send_a, "sub")), after=[early]
         )
-        late = add_up(exchange(shards))
-        half_early = gather(spread(early), after=[late])
-        other_early = swap_over(half_early, "sub")
-        half_late = gather(spread(late), after=[other_early])
-        grad_b, grad_a = finish(
-            [(half_early, other_early), (half_late, swap_over(half_late, "sub"))], up_width
-        )
+        all_early = spread(early)
+        late = add_up(exchange(shards), after=all_early[1:])
+        half = gather(all_early, spread(late))
+        grad_b, grad_a = finish([(half, swap_over(half, "sub"))], up_width)
     else:
         one, other = terms_over(gdown, "mp")
         part_a = small_call(

time: 120 us -> 123 us (1.025)
  waiting for transfers between devices: 43.8 us -> 31.7 us
  starting transfers between devices: 37.9 us -> 48.4 us
  Pallas kernels: 33.8 us -> 37.2 us
    ppermute x12, waiting for transfers between devices: 36.8 us -> 24.2 us  [rotate_over(): return lax.ppermute(block, axis, [(i, (i + d) % size) for i in range(size)])]
    ppermute x12, starting transfers between devices: 14.3 us -> 26 us  [rotate_over(): return lax.ppermute(block, axis, [(i, (i + d) % size) for i in range(size)])]
    pallas_call x3, Pallas kernels: 25.4 us -> 28.8 us  [attention(): pl.pallas_call(kernel, grid=(count,), out_shape=[jax.ShapeDtypeStruct((ro...]
    ppermute x10 -> x9, waiting for transfers between devices: 7.02 us -> 7.4 us  [swap_over(): return lax.ppermute(block, axis, [(0, 1), (1, 0)])]
    pallas_call x8 -> x7, Pallas kernels: 2.94 us -> 2.93 us  [small_call(): pl.pallas_call(lambda *refs: kernel(*refs[:count], *refs[len(given):outs]...]
    ppermute x10 -> x9, starting transfers between devices: 10.7 us -> 10.7 us  [swap_over(): return lax.ppermute(block, axis, [(0, 1), (1, 0)])]
  transfers between devices with their start and end apart: 26 -> 25, of which waited for: 12 -> 9; matrix products, arithmetic and copies ran while one was open for 0% -> 0% of each run, Pallas kernels for 24% -> 26%
where the time goes in v1:
time: 123 us; the launch traced here: 122 us
  starting transfers between devices  48.4 us (39%)
  Pallas kernels  37.2 us (30%)
  waiting for transfers between devices  31.7 us (26%)
  local copies, waits for them, and re-layouts  3.97 us (3%)
    pallas_call x3, Pallas kernels, attention(): pl.pallas_call(kernel, grid=(count,), out_shape=[jax.ShapeDtypeStruct((ro...  28.8 us
    ppermute x12, starting transfers between devices, rotate_over(): return lax.ppermute(block, axis, [(i, (i + d) % size) for i in range(size)])  26 us
    ppermute x12, waiting for transfers between devices, rotate_over(): return lax.ppermute(block, axis, [(i, (i + d) % size) for i in range(size)])  24.2 us
    ppermute x4, starting transfers between devices, shift_over(): return lax.ppermute(block, axis, [(i, i + 1) for i in range(size - 1)])  11.7 us
    ppermute x9, starting transfers between devices, swap_over(): return lax.ppermute(block, axis, [(0, 1), (1, 0)])  10.7 us
    ppermute x9, waiting for transfers between devices, swap_over(): return lax.ppermute(block, axis, [(0, 1), (1, 0)])  7.4 us
    unnamed x36, local copies, waits for them, and re-layouts  3.97 us
    pallas_call x1, Pallas kernels, down_project(): pl.pallas_call(functools.partial(down_kernel, tenants, rank), out_shape=j...  3.36 us
  transfers between devices with their start and end apart: 25, of which 9 were waited for; matrix products, arithmetic and copies ran while one was open for 0% of the time, Pallas kernels for 26%

profile of v1, /device:TPU:0, one launch (start us, length us, event | category | flops | bytes accessed | tf_op | source)
XLA Modules:
  0.0 122.2 jit_solution(14250171627391598477)
XLA Ops:
  0.6 1.9 %pack_keys_values.1 = (bf16[272,512]{1,0:T(8,128)(2,1)}, bf16[272,512]{1,0:T(8,128)(2,1)}) custom-call(bf16[256,512]{1,0:T(8,128)(2,1)} %keys.1, bf16[256,512]{1,0:T(8,128)(2,1)} %values.1, s32[1,256]{1,0:T(1,128)} %bitcast.13), custom_call_target="tpu_custom_call" | custom-call | bytes 1048576 | tf_op jit(solution)/shard_map/pack_keys_values/pallas_call | solution.py:70
  2.5 5.1 %collective-permute-start.1 = (bf16[272,512]{1,0:T(8,128)(2,1)}, bf16[272,512]{1,0:T(8,128)(2,1)S(1)}, u32[]{:S(2)}, u32[]{:S(2)}) collective-permute-start(bf16[272,512]{1,0:T(8,128)(2,1)} %get-tuple-element.34.own.refs_3_.refs_4_.refs_11_), channel_id=1, source_target_pairs={{0,4},{4,8},{8,12},{1,5},{5,9},{9,13},{2,6},{6,10},{10,14},{3,7},{... | collective-permute-start | bytes 835592 | tf_op jit(solution)/shard_map/ppermute | solution.py:531
  7.6 3.4 %down_project.1.refs_15_.refs_16_.refs_2_ = f32[24,256]{1,0:T(8,128)} custom-call(bf16[256,2560]{1,0:T(8,128)(2,1)} %refs_3_.1, bf16[128,2560]{1,0:T(8,128)(2,1)} %bitcast.12, s32[1,256]{1,0:T(1,128)} %bitcast.14, s32[16]{0:T(128)} %tenant_of.1), custom_call_target="tpu_custom_call" | custom-call | flops 167772160 | bytes 1966080 | tf_op jit(solution)/shard_map/down_project/pallas_call | solution.py:156
  11.0 1.6 %collective-permute-start.2 = (f32[24,256]{1,0:T(8,128)}, f32[24,256]{1,0:T(8,128)S(1)}, u32[]{:S(2)}, u32[]{:S(2)}) collective-permute-start(f32[24,256]{1,0:T(8,128)} %down_project.1.refs_15_.refs_16_.refs_2_), channel_id=1, source_target_pairs={{0,2},{2,0},{1,3},{3,1},{4,6},{6,4},{5,7},{7,5},{8,10},{10,8},{9,1... | collective-permute-start | bytes 73736 | tf_op jit(solution)/shard_map/ppermute | solution.py:515
  12.6 2.5 %collective-permute-done.2.after.refs_17_ = f32[24,256]{1,0:T(8,128)S(1)} collective-permute-done((f32[24,256]{1,0:T(8,128)}, f32[24,256]{1,0:T(8,128)S(1)}, u32[]{:S(2)}, u32[]{:S(2)}) %collective-permute-start.2) | collective-permute-done | bytes 24608 | tf_op jit(solution)/shard_map/ppermute | solution.py:515
  15.1 0.1 relay_block.2
  15.2 1.3 %collective-permute-start.4 = (bf16[272,512]{1,0:T(8,128)(2,1)S(1)}, bf16[272,512]{1,0:T(8,128)(2,1)S(1)}, u32[]{:S(2)}, u32[]{:S(2)}) collective-permute-start(bf16[272,512]{1,0:T(8,128)(2,1)S(1)} %get-tuple-element.36), channel_id=1, source_target_pairs={{0,1},{1,4},{4,5},{5,8},{8,9},{9,12},{12,13},{2,3},{3,6},{6,7},{7,... | collective-permute-start | bytes 835592 | tf_op jit(solution)/shard_map/ppermute | solution.py:531
  16.6 2.3 %collective-permute-start.3 = (bf16[272,512]{1,0:T(8,128)(2,1)S(1)}, bf16[272,512]{1,0:T(8,128)(2,1)S(1)}, u32[]{:S(2)}, u32[]{:S(2)}) collective-permute-start(bf16[272,512]{1,0:T(8,128)(2,1)S(1)} %get-tuple-element.35.refs_5_.refs_6_.refs_12_), channel_id=1, source_target_pairs={{0,1},{1,0},{2,3},{3,2},{4,5},{5,4},{6,7},{7,6},{8,9},{9,8},{10,11... | collective-permute-start | bytes 835592 | tf_op jit(solution)/shard_map/ppermute | solution.py:515
  18.9 3.5 %collective-permute-start = (bf16[272,512]{1,0:T(8,128)(2,1)S(1)}, bf16[272,512]{1,0:T(8,128)(2,1)S(1)}, u32[]{:S(2)}, u32[]{:S(2)}) collective-permute-start(bf16[272,512]{1,0:T(8,128)(2,1)S(1)} %copy-done.6), channel_id=1, source_target_pairs={{0,4},{4,8},{8,12},{1,5},{5,9},{9,13},{2,6},{6,10},{10,14},{3,7},{... | collective-permute-start | bytes 835592 | tf_op jit(solution)/shard_map/ppermute | solution.py:531
  22.5 0.6 copy-done.13
  23.1 0.1 copy-done.14
  23.2 7.5 %attention.3 = (bf16[256,4096]{1,0:T(8,128)(2,1)}, bf16[64,1024]{1,0:T(8,128)(2,1)}, bf16[64,1024]{1,0:T(8,128)(2,1)}, f32[16,256]{1,0:T(8,128)}) custom-call(bf16[256,4096]{1,0:T(8,128)(2,1)} %refs_0_.5, bf16[256,4096]{1,0:T(8,128)(2,1)} %refs_1_.5, bf16[128,4096]{1,0:T(8,128)(2,1)} %bitcast.9, ...), custom_call_target="tpu_custom_call" | custom-call | flops 2147483648 | bytes 1572864 | tf_op jit(solution)/shard_map/attention/pallas_call | solution.py:345
  30.7 0.7 copy-done.11
  31.5 0.1 relay_block.3
  31.6 1.8 %collective-permute-start.6 = (bf16[272,512]{1,0:T(8,128)(2,1)S(1)}, bf16[272,512]{1,0:T(8,128)(2,1)S(1)}, u32[]{:S(2)}, u32[]{:S(2)}) collective-permute-start(bf16[272,512]{1,0:T(8,128)(2,1)S(1)} %get-tuple-element.39), channel_id=1, source_target_pairs={{0,1},{1,4},{4,5},{5,8},{8,9},{9,12},{12,13},{2,3},{3,6},{6,7},{7,... | collective-permute-start | bytes 835592 | tf_op jit(solution)/shard_map/ppermute | solution.py:531
  33.4 2.5 %collective-permute-start.5 = (bf16[272,512]{1,0:T(8,128)(2,1)S(1)}, bf16[272,512]{1,0:T(8,128)(2,1)S(1)}, u32[]{:S(2)}, u32[]{:S(2)}) collective-permute-start(bf16[272,512]{1,0:T(8,128)(2,1)S(1)} %get-tuple-element.38.refs_5_.refs_6_), channel_id=1, source_target_pairs={{0,1},{1,0},{2,3},{3,2},{4,5},{5,4},{6,7},{7,6},{8,9},{9,8},{10,11... | collective-permute-start | bytes 835592 | tf_op jit(solution)/shard_map/ppermute | solution.py:515
  36.0 8.0 %attention.4 = (bf16[256,4096]{1,0:T(8,128)(2,1)}, bf16[64,1024]{1,0:T(8,128)(2,1)}, bf16[64,1024]{1,0:T(8,128)(2,1)}, f32[16,256]{1,0:T(8,128)}) custom-call(bf16[256,4096]{1,0:T(8,128)(2,1)} %refs_0_.5, bf16[256,4096]{1,0:T(8,128)(2,1)} %refs_1_.5, bf16[128,4096]{1,0:T(8,128)(2,1)} %bitcast.10, ...), custom_call_target="tpu_custom_call", output_to_operand_aliasing={{0}: (19, {})} | custom-call | flops 2147483648 | bytes 1572864 | tf_op jit(solution)/shard_map/attention/pallas_call | solution.py:345
  44.0 0.5 collective-permute-start.8
  44.5 0.7 copy-done.15
  45.2 0.1 copy-done.16
  45.3 13.4 %attention.5 = (bf16[256,4096]{1,0:T(8,128)(2,1)}, bf16[64,2048]{1,0:T(8,128)(2,1)}, bf16[64,2048]{1,0:T(8,128)(2,1)}, f32[16,256]{1,0:T(8,128)}) custom-call(bf16[256,4096]{1,0:T(8,128)(2,1)} %refs_0_.5, bf16[256,4096]{1,0:T(8,128)(2,1)} %refs_1_.5, bf16[128,4096]{1,0:T(8,128)(2,1)} %bitcast.11, ...), custom_call_target="tpu_custom_call", output_to_operand_aliasing={{0}: (19, {})} | custom-call | flops 4294967296 | bytes 3145728 | tf_op jit(solution)/shard_map/attention/pallas_call | solution.py:345
  58.7 0.9 copy-done.3
  59.7 0.1 scatter_grads.2
  59.8 5.0 %collective-permute-start.9 = (bf16[16,2048]{1,0:T(8,128)(2,1)S(1)}, bf16[16,2048]{1,0:T(8,128)(2,1)S(1)}, u32[]{:S(2)}, u32[]{:S(2)}) collective-permute-start(bf16[16,2048]{1,0:T(8,128)(2,1)S(1)} %get-tuple-element.50), channel_id=1, source_target_pairs={{0,4},{4,8},{8,12},{12,0},{1,5},{5,9},{9,13},{13,1},{2,6},{6,10},{... | collective-permute-start | bytes 196616 | tf_op jit(solution)/shard_map/ppermute | solution.py:520
  64.8 1.5 %collective-permute-start.16 = (f32[16,256]{1,0:T(8,128)}, f32[16,256]{1,0:T(8,128)S(1)}, u32[]{:S(2)}, u32[]{:S(2)}) collective-permute-start(f32[16,256]{1,0:T(8,128)} %get-tuple-element.54.refs_0_), channel_id=1, source_target_pairs={{0,2},{2,0},{1,3},{3,1},{4,6},{6,4},{5,7},{7,5},{8,10},{10,8},{9,1... | collective-permute-start | bytes 49160 | tf_op jit(solution)/shard_map/ppermute | solution.py:515
  66.3 2.5 %collective-permute-done.16.refs_1_ = f32[16,256]{1,0:T(8,128)S(1)} collective-permute-done((f32[16,256]{1,0:T(8,128)}, f32[16,256]{1,0:T(8,128)S(1)}, u32[]{:S(2)}, u32[]{:S(2)}) %collective-permute-start.16) | collective-permute-done | bytes 16416 | tf_op jit(solution)/shard_map/ppermute | solution.py:515
  68.8 0.7 copy-done.12
  69.5 0.4 split_grads.1
  69.9 2.1 %collective-permute-start.17 = (bf16[64,2560]{1,0:T(8,128)(2,1)S(1)}, bf16[64,2560]{1,0:T(8,128)(2,1)S(1)}, u32[]{:S(2)}, u32[]{:S(2)}) collective-permute-start(bf16[64,2560]{1,0:T(8,128)(2,1)S(1)} %get-tuple-element.56), channel_id=1, source_target_pairs={{0,1},{1,0},{2,3},{3,2},{4,5},{5,4},{6,7},{7,6},{8,9},{9,8},{10,11... | collective-permute-start | bytes 983048 | tf_op jit(solution)/shard_map/ppermute | solution.py:515
  72.0 1.6 %collective-permute-start.10 = (bf16[16,2048]{1,0:T(8,128)(2,1)S(1)}, bf16[16,2048]{1,0:T(8,128)(2,1)S(1)}, u32[]{:S(2)}, u32[]{:S(2)}) collective-permute-start(bf16[16,2048]{1,0:T(8,128)(2,1)S(1)} %get-tuple-element.51), channel_id=1, source_target_pairs={{0,8},{4,12},{8,0},{12,4},{1,9},{5,13},{9,1},{13,5},{2,10},{6,14},... | collective-permute-start | bytes 196616 | tf_op jit(solution)/shard_map/ppermute | solution.py:520
  73.7 2.5 %collective-permute-start.11 = (bf16[16,2048]{1,0:T(8,128)(2,1)S(1)}, bf16[16,2048]{1,0:T(8,128)(2,1)S(1)}, u32[]{:S(2)}, u32[]{:S(2)}) collective-permute-start(bf16[16,2048]{1,0:T(8,128)(2,1)S(1)} %get-tuple-element.52), channel_id=1, source_target_pairs={{0,12},{4,0},{8,4},{12,8},{1,13},{5,1},{9,5},{13,9},{2,14},{6,2},{... | collective-permute-start | bytes 196616 | tf_op jit(solution)/shard_map/ppermute | solution.py:520
  76.2 3.1 %collective-permute-done.10.refs_2_ = bf16[16,2048]{1,0:T(8,128)(2,1)S(1)} collective-permute-done((bf16[16,2048]{1,0:T(8,128)(2,1)S(1)}, bf16[16,2048]{1,0:T(8,128)(2,1)S(1)}, u32[]{:S(2)}, u32[]{:S(2)}) %collective-permute-start.10) | collective-permute-done | bytes 65568 | tf_op jit(solution)/shard_map/ppermute | solution.py:520
  79.3 0.3 scatter_grads.3
  79.6 1.6 %collective-permute-start.18 = (bf16[16,4608]{1,0:T(8,128)(2,1)S(1)}, bf16[16,4608]{1,0:T(8,128)(2,1)S(1)}, u32[]{:S(2)}, u32[]{:S(2)}) collective-permute-start(bf16[16,4608]{1,0:T(8,128)(2,1)S(1)} %get-tuple-element.58), channel_id=1, source_target_pairs={{0,4},{4,8},{8,12},{12,0},{1,5},{5,9},{9,13},{13,1},{2,6},{6,10},{... | collective-permute-start | bytes 442376 | tf_op jit(solution)/shard_map/ppermute | solution.py:520
  81.2 2.0 %collective-permute-start.19 = (bf16[16,4608]{1,0:T(8,128)(2,1)S(1)}, bf16[16,4608]{1,0:T(8,128)(2,1)S(1)}, u32[]{:S(2)}, u32[]{:S(2)}) collective-permute-start(bf16[16,4608]{1,0:T(8,128)(2,1)S(1)} %get-tuple-element.59), channel_id=1, source_target_pairs={{0,8},{4,12},{8,0},{12,4},{1,9},{5,13},{9,1},{13,5},{2,10},{6,14},... | collective-permute-start | bytes 442376 | tf_op jit(solution)/shard_map/ppermute | solution.py:520
  83.2 0.4 collective-permute-start.20
  83.6 1.9 %collective-permute-start.14 = (bf16[16,2048]{1,0:T(8,128)(2,1)S(1)}, bf16[16,2048]{1,0:T(8,128)(2,1)S(1)}, u32[]{:S(2)}, u32[]{:S(2)}) collective-permute-start(bf16[16,2048]{1,0:T(8,128)(2,1)S(1)} %sum_grads.2.refs_4_.refs_0_), channel_id=1, source_target_pairs={{0,12},{4,0},{8,4},{12,8},{1,13},{5,1},{9,5},{13,9},{2,14},{6,2},{... | collective-permute-start | bytes 196616 | tf_op jit(solution)/shard_map/ppermute | solution.py:520
  85.6 1.1 collective-permute-start.13
  86.7 7.3 %collective-permute-done.14.refs_6_.refs_3_ = bf16[16,2048]{1,0:T(8,128)(2,1)S(1)} collective-permute-done((bf16[16,2048]{1,0:T(8,128)(2,1)S(1)}, bf16[16,2048]{1,0:T(8,128)(2,1)S(1)}, u32[]{:S(2)}, u32[]{:S(2)}) %collective-permute-start.14) | collective-permute-done | bytes 65568 | tf_op jit(solution)/shard_map/ppermute | solution.py:520
  94.0 5.9 %collective-permute-start.12 = (bf16[16,2048]{1,0:T(8,128)(2,1)S(1)}, bf16[16,2048]{1,0:T(8,128)(2,1)S(1)}, u32[]{:S(2)}, u32[]{:S(2)}) collective-permute-start(bf16[16,2048]{1,0:T(8,128)(2,1)S(1)} %sum_grads.2.refs_4_.refs_0_), channel_id=1, source_target_pairs={{0,4},{4,8},{8,12},{12,0},{1,5},{5,9},{9,13},{13,1},{2,6},{6,10},{... | collective-permute-start | bytes 196616 | tf_op jit(solution)/shard_map/ppermute | solution.py:520
  99.9 1.4 %collective-permute-done.13.refs_5_.refs_2_ = bf16[16,2048]{1,0:T(8,128)(2,1)S(1)} collective-permute-done((bf16[16,2048]{1,0:T(8,128)(2,1)S(1)}, bf16[16,2048]{1,0:T(8,128)(2,1)S(1)}, u32[]{:S(2)}, u32[]{:S(2)}) %collective-permute-start.13) | collective-permute-done | bytes 65568 | tf_op jit(solution)/shard_map/ppermute | solution.py:520
  101.3 0.5 collective-permute-done.12.refs_4_.refs_1_
  101.9 0.8 collective-permute-start.23
  102.7 3.0 %collective-permute-start.22 = (bf16[16,4608]{1,0:T(8,128)(2,1)S(1)}, bf16[16,4608]{1,0:T(8,128)(2,1)S(1)}, u32[]{:S(2)}, u32[]{:S(2)}) collective-permute-start(bf16[16,4608]{1,0:T(8,128)(2,1)S(1)} %sum_grads.3.refs_4_), channel_id=1, source_target_pairs={{0,8},{4,12},{8,0},{12,4},{1,9},{5,13},{9,1},{13,5},{2,10},{6,14},... | collective-permute-start | bytes 442376 | tf_op jit(solution)/shard_map/ppermute | solution.py:520
  105.8 1.7 %collective-permute-done.23.refs_7_ = bf16[16,4608]{1,0:T(8,128)(2,1)S(1)} collective-permute-done((bf16[16,4608]{1,0:T(8,128)(2,1)S(1)}, bf16[16,4608]{1,0:T(8,128)(2,1)S(1)}, u32[]{:S(2)}, u32[]{:S(2)}) %collective-permute-start.23) | collective-permute-done | bytes 147488 | tf_op jit(solution)/shard_map/ppermute | solution.py:520
  107.5 10.3 %collective-permute-done.22.refs_6_ = bf16[16,4608]{1,0:T(8,128)(2,1)S(1)} collective-permute-done((bf16[16,4608]{1,0:T(8,128)(2,1)S(1)}, bf16[16,4608]{1,0:T(8,128)(2,1)S(1)}, u32[]{:S(2)}, u32[]{:S(2)}) %collective-permute-start.22) | collective-permute-done | bytes 147488 | tf_op jit(solution)/shard_map/ppermute | solution.py:520
  117.9 2.4 %collective-permute-done.24.refs_1_ = bf16[64,6656]{1,0:T(8,128)(2,1)S(1)} collective-permute-done((bf16[64,6656]{1,0:T(8,128)(2,1)S(1)}, bf16[64,6656]{1,0:T(8,128)(2,1)S(1)}, u32[]{:S(2)}, u32[]{:S(2)}) %collective-permute-start.24) | collective-permute-done | bytes 852000 | tf_op jit(solution)/shard_map/ppermute | solution.py:515
  120.3 1.9 %finish_grads.1 = (f32[128,4096]{1,0:T(8,128)}, f32[128,2560]{1,0:T(8,128)}) custom-call(bf16[64,6656]{1,0:T(8,128)(2,1)S(1)} %gather_grads.1.refs_0_, bf16[64,6656]{1,0:T(8,128)(2,1)S(1)} %collective-permute-done.24.refs_1_), custom_call_target="tpu_custom_call" | custom-call | flops 1703936 | bytes 3407872 | tf_op jit(solution)/shard_map/finish_grads/pallas_call | solution.py:372
  (52 shorter events, 0.5 us)
Async XLA Ops:
  2.5 12.6 %copy-start = (bf16[272,512]{1,0:T(8,128)(2,1)S(1)}, bf16[272,512]{1,0:T(8,128)(2,1)}, u32[]{:S(2)}) copy-start(bf16[272,512]{1,0:T(8,128)(2,1)} %get-tuple-element.34.own.refs_3_.refs_4_.refs_11_) | copy-start | bytes 835588
  2.5 16.4 %copy-start.6 = (bf16[272,512]{1,0:T(8,128)(2,1)S(1)}, bf16[272,512]{1,0:T(8,128)(2,1)}, u32[]{:S(2)}) copy-start(bf16[272,512]{1,0:T(8,128)(2,1)} %get-tuple-element.33.own.refs_3_.refs_4_) | copy-start | bytes 835588
  2.5 12.6 %collective-permute-start.1 = (bf16[272,512]{1,0:T(8,128)(2,1)}, bf16[272,512]{1,0:T(8,128)(2,1)S(1)}, u32[]{:S(2)}, u32[]{:S(2)}) collective-permute-start(bf16[272,512]{1,0:T(8,128)(2,1)} %get-tuple-element.34.own.refs_3_.refs_4_.refs_11_), channel_id=1, source_target_pairs={{0,4},{4,8},{8,12},{1,5},{5,9},{9,13},{2,6},{6,10},{10,14},{3,7},{... | collective-permute-start | bytes 835592 | tf_op jit(solution)/shard_map/ppermute | solution.py:531
  11.0 4.1 %collective-permute-start.2 = (f32[24,256]{1,0:T(8,128)}, f32[24,256]{1,0:T(8,128)S(1)}, u32[]{:S(2)}, u32[]{:S(2)}) collective-permute-start(f32[24,256]{1,0:T(8,128)} %down_project.1.refs_15_.refs_16_.refs_2_), channel_id=1, source_target_pairs={{0,2},{2,0},{1,3},{3,1},{4,6},{6,4},{5,7},{7,5},{8,10},{10,8},{9,1... | collective-permute-start | bytes 73736 | tf_op jit(solution)/shard_map/ppermute | solution.py:515
  15.1 7.3 %copy-start.8 = (f32[24,256]{1,0:T(8,128)}, f32[24,256]{1,0:T(8,128)S(1)}, u32[]{:S(2)}) copy-start(f32[24,256]{1,0:T(8,128)S(1)} %collective-permute-done.2.after.refs_17_) | copy-start | bytes 73732
  15.2 7.2 %copy-start.1 = (bf16[272,512]{1,0:T(8,128)(2,1)}, bf16[272,512]{1,0:T(8,128)(2,1)S(1)}, u32[]{:S(2)}) copy-start(bf16[272,512]{1,0:T(8,128)(2,1)S(1)} %get-tuple-element.35.refs_5_.refs_6_.refs_12_) | copy-start | bytes 835588
  15.2 7.2 %collective-permute-start.4 = (bf16[272,512]{1,0:T(8,128)(2,1)S(1)}, bf16[272,512]{1,0:T(8,128)(2,1)S(1)}, u32[]{:S(2)}, u32[]{:S(2)}) collective-permute-start(bf16[272,512]{1,0:T(8,128)(2,1)S(1)} %get-tuple-element.36), channel_id=1, source_target_pairs={{0,1},{1,4},{4,5},{5,8},{8,9},{9,12},{12,13},{2,3},{3,6},{6,7},{7,... | collective-permute-start | bytes 835592 | tf_op jit(solution)/shard_map/ppermute | solution.py:531
  16.6 5.9 %collective-permute-start.3 = (bf16[272,512]{1,0:T(8,128)(2,1)S(1)}, bf16[272,512]{1,0:T(8,128)(2,1)S(1)}, u32[]{:S(2)}, u32[]{:S(2)}) collective-permute-start(bf16[272,512]{1,0:T(8,128)(2,1)S(1)} %get-tuple-element.35.refs_5_.refs_6_.refs_12_), channel_id=1, source_target_pairs={{0,1},{1,0},{2,3},{3,2},{4,5},{5,4},{6,7},{7,6},{8,9},{9,8},{10,11... | collective-permute-start | bytes 835592 | tf_op jit(solution)/shard_map/ppermute | solution.py:515
  18.9 11.8 %collective-permute-start = (bf16[272,512]{1,0:T(8,128)(2,1)S(1)}, bf16[272,512]{1,0:T(8,128)(2,1)S(1)}, u32[]{:S(2)}, u32[]{:S(2)}) collective-permute-start(bf16[272,512]{1,0:T(8,128)(2,1)S(1)} %copy-done.6), channel_id=1, source_target_pairs={{0,4},{4,8},{8,12},{1,5},{5,9},{9,13},{2,6},{6,10},{10,14},{3,7},{... | collective-permute-start | bytes 835592 | tf_op jit(solution)/shard_map/ppermute | solution.py:531
  22.4 0.7 copy-start.13
  22.4 0.8 copy-start.14
  30.7 0.7 copy-start.11
  31.6 12.4 %copy-start.7 = (bf16[272,512]{1,0:T(8,128)(2,1)}, bf16[272,512]{1,0:T(8,128)(2,1)S(1)}, u32[]{:S(2)}) copy-start(bf16[272,512]{1,0:T(8,128)(2,1)S(1)} %get-tuple-element.38.refs_5_.refs_6_) | copy-start | bytes 835588
  31.6 12.9 %collective-permute-start.6 = (bf16[272,512]{1,0:T(8,128)(2,1)S(1)}, bf16[272,512]{1,0:T(8,128)(2,1)S(1)}, u32[]{:S(2)}, u32[]{:S(2)}) collective-permute-start(bf16[272,512]{1,0:T(8,128)(2,1)S(1)} %get-tuple-element.39), channel_id=1, source_target_pairs={{0,1},{1,4},{4,5},{5,8},{8,9},{9,12},{12,13},{2,3},{3,6},{6,7},{7,... | collective-permute-start | bytes 835592 | tf_op jit(solution)/shard_map/ppermute | solution.py:531
  33.4 11.1 %collective-permute-start.5 = (bf16[272,512]{1,0:T(8,128)(2,1)S(1)}, bf16[272,512]{1,0:T(8,128)(2,1)S(1)}, u32[]{:S(2)}, u32[]{:S(2)}) collective-permute-start(bf16[272,512]{1,0:T(8,128)(2,1)S(1)} %get-tuple-element.38.refs_5_.refs_6_), channel_id=1, source_target_pairs={{0,1},{1,0},{2,3},{3,2},{4,5},{5,4},{6,7},{7,6},{8,9},{9,8},{10,11... | collective-permute-start | bytes 835592 | tf_op jit(solution)/shard_map/ppermute | solution.py:515
  35.9 22.7 %collective-permute-start.7 = (bf16[64,1024]{1,0:T(8,128)(2,1)}, bf16[64,1024]{1,0:T(8,128)(2,1)S(1)}, u32[]{:S(2)}, u32[]{:S(2)}) collective-permute-start(bf16[64,1024]{1,0:T(8,128)(2,1)} %get-tuple-element.45), channel_id=1, source_target_pairs={{0,1},{1,0},{2,3},{3,2},{4,5},{5,4},{6,7},{7,6},{8,9},{9,8},{10,11... | collective-permute-start | bytes 393224 | tf_op jit(solution)/shard_map/ppermute | solution.py:515
  44.0 14.7 %collective-permute-start.8 = (bf16[64,1024]{1,0:T(8,128)(2,1)}, bf16[64,1024]{1,0:T(8,128)(2,1)S(1)}, u32[]{:S(2)}, u32[]{:S(2)}) collective-permute-start(bf16[64,1024]{1,0:T(8,128)(2,1)} %get-tuple-element.47), channel_id=1, source_target_pairs={{0,1},{1,0},{2,3},{3,2},{4,5},{5,4},{6,7},{7,6},{8,9},{9,8},{10,11... | collective-permute-start | bytes 393224 | tf_op jit(solution)/shard_map/ppermute | solution.py:515
  44.5 0.7 copy-start.15
  44.5 0.8 copy-start.16
  45.3 13.4 %copy-start.9 = (bf16[64,1024]{1,0:T(8,128)(2,1)S(1)}, bf16[64,1024]{1,0:T(8,128)(2,1)}, u32[]{:S(2)}) copy-start(bf16[64,1024]{1,0:T(8,128)(2,1)} %get-tuple-element.44.refs_0_) | copy-start | bytes 393220
  45.3 13.4 %copy-start.10 = (bf16[64,1024]{1,0:T(8,128)(2,1)S(1)}, bf16[64,1024]{1,0:T(8,128)(2,1)}, u32[]{:S(2)}) copy-start(bf16[64,1024]{1,0:T(8,128)(2,1)} %get-tuple-element.46.refs_2_) | copy-start | bytes 393220
  45.3 23.5 %copy-start.2 = (bf16[256,2560]{1,0:T(8,128)(2,1)S(1)}, bf16[256,2560]{1,0:T(8,128)(2,1)}, u32[]{:S(2)}) copy-start(bf16[256,2560]{1,0:T(8,128)(2,1)} %refs_3_.1) | copy-start | bytes 3932164
  45.3 23.5 %copy-start.5 = (f32[24,256]{1,0:T(8,128)S(1)}, f32[24,256]{1,0:T(8,128)}, u32[]{:S(2)}) copy-start(f32[24,256]{1,0:T(8,128)} %down_project.1.refs_15_.refs_16_.refs_2_) | copy-start | bytes 73732
  58.7 1.0 copy-start.3
  59.7 12.3 %copy-start.17 = (bf16[64,2048]{1,0:T(8,128)(2,1)S(1)}, bf16[64,2048]{1,0:T(8,128)(2,1)}, u32[]{:S(2)}) copy-start(bf16[64,2048]{1,0:T(8,128)(2,1)} %get-tuple-element.53) | copy-start | bytes 786436
  59.7 19.6 %copy-start.4 = (bf16[64,2048]{1,0:T(8,128)(2,1)S(1)}, bf16[64,2048]{1,0:T(8,128)(2,1)}, u32[]{:S(2)}) copy-start(bf16[64,2048]{1,0:T(8,128)(2,1)} %get-tuple-element.48.refs_4_.refs_0_) | copy-start | bytes 786436
  59.8 9.0 %collective-permute-start.9 = (bf16[16,2048]{1,0:T(8,128)(2,1)S(1)}, bf16[16,2048]{1,0:T(8,128)(2,1)S(1)}, u32[]{:S(2)}, u32[]{:S(2)}) collective-permute-start(bf16[16,2048]{1,0:T(8,128)(2,1)S(1)} %get-tuple-element.50), channel_id=1, source_target_pairs={{0,4},{4,8},{8,12},{12,0},{1,5},{5,9},{9,13},{13,1},{2,6},{6,10},{... | collective-permute-start | bytes 196616 | tf_op jit(solution)/shard_map/ppermute | solution.py:520
  64.8 3.9 %collective-permute-start.16 = (f32[16,256]{1,0:T(8,128)}, f32[16,256]{1,0:T(8,128)S(1)}, u32[]{:S(2)}, u32[]{:S(2)}) collective-permute-start(f32[16,256]{1,0:T(8,128)} %get-tuple-element.54.refs_0_), channel_id=1, source_target_pairs={{0,2},{2,0},{1,3},{3,1},{4,6},{6,4},{5,7},{7,5},{8,10},{10,8},{9,1... | collective-permute-start | bytes 49160 | tf_op jit(solution)/shard_map/ppermute | solution.py:515
  68.8 0.7 copy-start.12
  69.9 9.4 %collective-permute-start.17 = (bf16[64,2560]{1,0:T(8,128)(2,1)S(1)}, bf16[64,2560]{1,0:T(8,128)(2,1)S(1)}, u32[]{:S(2)}, u32[]{:S(2)}) collective-permute-start(bf16[64,2560]{1,0:T(8,128)(2,1)S(1)} %get-tuple-element.56), channel_id=1, source_target_pairs={{0,1},{1,0},{2,3},{3,2},{4,5},{5,4},{6,7},{7,6},{8,9},{9,8},{10,11... | collective-permute-start | bytes 983048 | tf_op jit(solution)/shard_map/ppermute | solution.py:515
  72.0 7.3 %collective-permute-start.15 = (bf16[64,2048]{1,0:T(8,128)(2,1)S(1)}, bf16[64,2048]{1,0:T(8,128)(2,1)S(1)}, u32[]{:S(2)}, u32[]{:S(2)}) collective-permute-start(bf16[64,2048]{1,0:T(8,128)(2,1)S(1)} %copy-done.17), channel_id=1, source_target_pairs={{0,1},{1,0},{2,3},{3,2},{4,5},{5,4},{6,7},{7,6},{8,9},{9,8},{10,11... | collective-permute-start | bytes 786440 | tf_op jit(solution)/shard_map/ppermute | solution.py:515
  72.0 7.2 %collective-permute-start.10 = (bf16[16,2048]{1,0:T(8,128)(2,1)S(1)}, bf16[16,2048]{1,0:T(8,128)(2,1)S(1)}, u32[]{:S(2)}, u32[]{:S(2)}) collective-permute-start(bf16[16,2048]{1,0:T(8,128)(2,1)S(1)} %get-tuple-element.51), channel_id=1, source_target_pairs={{0,8},{4,12},{8,0},{12,4},{1,9},{5,13},{9,1},{13,5},{2,10},{6,14},... | collective-permute-start | bytes 196616 | tf_op jit(solution)/shard_map/ppermute | solution.py:520
  73.7 5.6 %collective-permute-start.11 = (bf16[16,2048]{1,0:T(8,128)(2,1)S(1)}, bf16[16,2048]{1,0:T(8,128)(2,1)S(1)}, u32[]{:S(2)}, u32[]{:S(2)}) collective-permute-start(bf16[16,2048]{1,0:T(8,128)(2,1)S(1)} %get-tuple-element.52), channel_id=1, source_target_pairs={{0,12},{4,0},{8,4},{12,8},{1,13},{5,1},{9,5},{13,9},{2,14},{6,2},{... | collective-permute-start | bytes 196616 | tf_op jit(solution)/shard_map/ppermute | solution.py:520
  79.6 22.2 %collective-permute-start.18 = (bf16[16,4608]{1,0:T(8,128)(2,1)S(1)}, bf16[16,4608]{1,0:T(8,128)(2,1)S(1)}, u32[]{:S(2)}, u32[]{:S(2)}) collective-permute-start(bf16[16,4608]{1,0:T(8,128)(2,1)S(1)} %get-tuple-element.58), channel_id=1, source_target_pairs={{0,4},{4,8},{8,12},{12,0},{1,5},{5,9},{9,13},{13,1},{2,6},{6,10},{... | collective-permute-start | bytes 442376 | tf_op jit(solution)/shard_map/ppermute | solution.py:520
  81.2 20.6 %collective-permute-start.19 = (bf16[16,4608]{1,0:T(8,128)(2,1)S(1)}, bf16[16,4608]{1,0:T(8,128)(2,1)S(1)}, u32[]{:S(2)}, u32[]{:S(2)}) collective-permute-start(bf16[16,4608]{1,0:T(8,128)(2,1)S(1)} %get-tuple-element.59), channel_id=1, source_target_pairs={{0,8},{4,12},{8,0},{12,4},{1,9},{5,13},{9,1},{13,5},{2,10},{6,14},... | collective-permute-start | bytes 442376 | tf_op jit(solution)/shard_map/ppermute | solution.py:520
  83.2 18.6 %collective-permute-start.20 = (bf16[16,4608]{1,0:T(8,128)(2,1)S(1)}, bf16[16,4608]{1,0:T(8,128)(2,1)S(1)}, u32[]{:S(2)}, u32[]{:S(2)}) collective-permute-start(bf16[16,4608]{1,0:T(8,128)(2,1)S(1)} %get-tuple-element.60), channel_id=1, source_target_pairs={{0,12},{4,0},{8,4},{12,8},{1,13},{5,1},{9,5},{13,9},{2,14},{6,2},{... | collective-permute-start | bytes 442376 | tf_op jit(solution)/shard_map/ppermute | solution.py:520
  83.6 10.3 %collective-permute-start.14 = (bf16[16,2048]{1,0:T(8,128)(2,1)S(1)}, bf16[16,2048]{1,0:T(8,128)(2,1)S(1)}, u32[]{:S(2)}, u32[]{:S(2)}) collective-permute-start(bf16[16,2048]{1,0:T(8,128)(2,1)S(1)} %sum_grads.2.refs_4_.refs_0_), channel_id=1, source_target_pairs={{0,12},{4,0},{8,4},{12,8},{1,13},{5,1},{9,5},{13,9},{2,14},{6,2},{... | collective-permute-start | bytes 196616 | tf_op jit(solution)/shard_map/ppermute | solution.py:520
  85.6 15.8 %collective-permute-start.13 = (bf16[16,2048]{1,0:T(8,128)(2,1)S(1)}, bf16[16,2048]{1,0:T(8,128)(2,1)S(1)}, u32[]{:S(2)}, u32[]{:S(2)}) collective-permute-start(bf16[16,2048]{1,0:T(8,128)(2,1)S(1)} %sum_grads.2.refs_4_.refs_0_), channel_id=1, source_target_pairs={{0,8},{4,12},{8,0},{12,4},{1,9},{5,13},{9,1},{13,5},{2,10},{6,14},... | collective-permute-start | bytes 196616 | tf_op jit(solution)/shard_map/ppermute | solution.py:520
  94.0 7.8 %collective-permute-start.12 = (bf16[16,2048]{1,0:T(8,128)(2,1)S(1)}, bf16[16,2048]{1,0:T(8,128)(2,1)S(1)}, u32[]{:S(2)}, u32[]{:S(2)}) collective-permute-start(bf16[16,2048]{1,0:T(8,128)(2,1)S(1)} %sum_grads.2.refs_4_.refs_0_), channel_id=1, source_target_pairs={{0,4},{4,8},{8,12},{12,0},{1,5},{5,9},{9,13},{13,1},{2,6},{6,10},{... | collective-permute-start | bytes 196616 | tf_op jit(solution)/shard_map/ppermute | solution.py:520
  101.9 5.6 %collective-permute-start.23 = (bf16[16,4608]{1,0:T(8,128)(2,1)S(1)}, bf16[16,4608]{1,0:T(8,128)(2,1)S(1)}, u32[]{:S(2)}, u32[]{:S(2)}) collective-permute-start(bf16[16,4608]{1,0:T(8,128)(2,1)S(1)} %sum_grads.3.refs_4_), channel_id=1, source_target_pairs={{0,12},{4,0},{8,4},{12,8},{1,13},{5,1},{9,5},{13,9},{2,14},{6,2},{... | collective-permute-start | bytes 442376 | tf_op jit(solution)/shard_map/ppermute | solution.py:520
  102.7 15.0 %collective-permute-start.22 = (bf16[16,4608]{1,0:T(8,128)(2,1)S(1)}, bf16[16,4608]{1,0:T(8,128)(2,1)S(1)}, u32[]{:S(2)}, u32[]{:S(2)}) collective-permute-start(bf16[16,4608]{1,0:T(8,128)(2,1)S(1)} %sum_grads.3.refs_4_), channel_id=1, source_target_pairs={{0,8},{4,12},{8,0},{12,4},{1,9},{5,13},{9,1},{13,5},{2,10},{6,14},... | collective-permute-start | bytes 442376 | tf_op jit(solution)/shard_map/ppermute | solution.py:520
  105.8 12.0 %collective-permute-start.21 = (bf16[16,4608]{1,0:T(8,128)(2,1)S(1)}, bf16[16,4608]{1,0:T(8,128)(2,1)S(1)}, u32[]{:S(2)}, u32[]{:S(2)}) collective-permute-start(bf16[16,4608]{1,0:T(8,128)(2,1)S(1)} %sum_grads.3.refs_4_), channel_id=1, source_target_pairs={{0,4},{4,8},{8,12},{12,0},{1,5},{5,9},{9,13},{13,1},{2,6},{6,10},{... | collective-permute-start | bytes 442376 | tf_op jit(solution)/shard_map/ppermute | solution.py:520
  117.8 2.4 %collective-permute-start.24 = (bf16[64,6656]{1,0:T(8,128)(2,1)S(1)}, bf16[64,6656]{1,0:T(8,128)(2,1)S(1)}, u32[]{:S(2)}, u32[]{:S(2)}) collective-permute-start(bf16[64,6656]{1,0:T(8,128)(2,1)S(1)} %gather_grads.1.refs_0_), channel_id=1, source_target_pairs={{0,1},{1,0},{2,3},{3,2},{4,5},{5,4},{6,7},{7,6},{8,9},{9,8},{10,11... | collective-permute-start | bytes 2555912 | tf_op jit(solution)/shard_map/ppermute | solution.py:515

commit v2 on v1

--- a/solution.py
+++ b/solution.py
@@ -83,7 +83,8 @@
     )(keys, values, doc)
 
 
-def relay_kernel(own, got, after, out, got_out, held, sems):
+def relay_kernel(own, got, *rest):
+    out, _, held, sems = rest[-4:]
     sub = lax.axis_index("sub")
 
     def move(source):
@@ -109,14 +110,14 @@
     return pl.pallas_call(
         relay_kernel,
         out_shape=[shape, shape],
-        in_specs=[ANY, ANY, ANY],
+        in_specs=[ANY] * (2 + len(after)),
         out_specs=[ANY, ANY],
         input_output_aliases={1: 1},
         scratch_shapes=[pltpu.VMEM(own.shape, own.dtype), pltpu.SemaphoreType.DMA((2,))],
         compiler_params=params(),
         cost_estimate=pl.CostEstimate(flops=0, bytes_accessed=4 * own.size, transcendentals=0),
         name="relay_block",
-    )(own, got, after)
+    )(own, got, *after)
 
 
 def selector_of(owner, tenants, rank):
@@ -178,14 +179,40 @@
     return info[rank : rank + 1, :].astype(jnp.int32)
 
 
+def turn_kernel(base, grad, up, base_t, grad_t, up_t, token):
+    base_t[...] = base[...].T
+    grad_t[...] = grad[...].T
+    up_t[...] = up[...].T
+    token[...] = jnp.zeros_like(token)
+
+
+def turn_operands(base, grad, up, group):
+    (rows, width), tall, span = base.shape, up.shape[0], group * HEAD
+    flat = lambda r: pl.BlockSpec((r, span), lambda i: (0, i))
+    high = lambda r: pl.BlockSpec((span, r), lambda i: (i, 0))
+    shape = lambda r: jax.ShapeDtypeStruct((width, r), jnp.bfloat16)
+    return pl.pallas_call(
+        turn_kernel,
+        grid=(width // span,),
+        out_shape=[shape(rows), shape(rows), shape(tall), jax.ShapeDtypeStruct((8, HEAD), jnp.float32)],
+        in_specs=[flat(rows), flat(rows), flat(tall)],
+        out_specs=[high(rows), high(rows), high(tall), pl.BlockSpec((8, HEAD), lambda i: (0, 0))],
+        compiler_params=params(VMEM_MOST),
+        cost_estimate=pl.CostEstimate(
+            flops=0, bytes_accessed=4 * width * (2 * rows + tall), transcendentals=0
+        ),
+        name="turn_operands",
+    )(base, grad, up)
+
+
 def turn(x):
     return x.astype(jnp.float32).T.astype(jnp.bfloat16)
 
 
 def attention(
-    head, at, count, group, base, grad, up, blocks, with_ids, info, terms, before, tenants, rank
+    head, at, count, group, turned, up, blocks, with_ids, info, terms, before, tenants, rank
 ):
-    rows, width = base.shape
+    width, rows = turned[0].shape
     window = (REACH + 1) * rows
     tall = tenants * rank
     half = tall // 2
@@ -199,7 +226,8 @@
     values = pl.BlockSpec((rows, HEAD), lambda i: (0, i + at + skip))
     ids = pl.BlockSpec((TAIL, rows), lambda i: (rows // TAIL, 0))
     same = lambda a: pl.BlockSpec(a.shape, lambda i: (0, 0))
-    operands, specs = [base, grad, up], [wide(rows), wide(rows), wide(tall)]
+    high = lambda r: pl.BlockSpec((span, r), lambda i: (i + head, 0))
+    operands, specs = [*turned, up], [high(rows), high(rows), high(tall), wide(tall)]
     for block in blocks:
         operands += [block, block]
         specs += [keys, values]
@@ -213,11 +241,9 @@
         vw=pltpu.VMEM((window, HEAD), jnp.bfloat16),
         kt=pltpu.VMEM((HEAD, window), jnp.bfloat16),
         vt=pltpu.VMEM((HEAD + TAIL, window), jnp.bfloat16),
-        bottle=pltpu.VMEM((rows, tall), jnp.bfloat16),
         bottle_t=pltpu.VMEM((tall, rows), jnp.bfloat16),
         bias=pltpu.VMEM((window, rows), jnp.float32),
         query=pltpu.VMEM((span, rows), jnp.bfloat16),
-        gt=pltpu.VMEM((span, rows), jnp.bfloat16),
         gquery=pltpu.VMEM((span, rows), jnp.bfloat16),
         scores=pltpu.VMEM((pair, window, rows), jnp.float32),
         part=pltpu.VMEM((tall, span), jnp.bfloat16),
@@ -226,14 +252,12 @@
     )
 
     def kernel(*refs):
-        base, grad, up = refs[0:3]
-        kv, tails, info, terms = refs[3:11], refs[11:15], refs[15], refs[16:18]
+        base, gt, up_t, up = refs[0:4]
+        kv, tails, info, terms = refs[4:12], refs[12:16], refs[16], refs[17:19]
         out, keep, send, projected = refs[len(operands) : len(operands) + 4]
         r = dict(zip(held, refs[len(operands) + 4 :]))
         kw, vw, kt, vt = (r[n] for n in ("kw", "vw", "kt", "vt"))
-        bias, query, gt, gquery, scores = (
-            r[n] for n in ("bias", "query", "gt", "gquery", "scores")
-        )
+        bias, query, gquery, scores = (r[n] for n in ("bias", "query", "gquery", "scores"))
         sub = lax.axis_index("sub")
         step = pl.program_id(0)
 
@@ -242,7 +266,6 @@
             owner = owner_of(info, rank)
             lifted = unfold((terms[0][...] + terms[1][...])[0:rank], owner, tenants, rank)
             r["bottle_t"][...] = lifted.astype(jnp.bfloat16)
-            r["bottle"][...] = lifted.T.astype(jnp.bfloat16)
             r["total"][...] = jnp.zeros((tall, rows), jnp.float32)
             vt[HEAD:, :] = jnp.ones((TAIL, window), jnp.bfloat16)
             own, two, swap, passed = (ref[...].astype(jnp.float32) for ref in tails)
@@ -284,9 +307,8 @@
             place(2, *kv[6:8])
             place(0, *kv[4:6])
 
-        lift = LIFT * nn(r["bottle"][...], up[...])
-        query[...] = (base[...].astype(jnp.float32) + lift).T.astype(jnp.bfloat16)
-        gt[...] = turn(grad[...])
+        lift = LIFT * nn(up_t[...], r["bottle_t"][...])
+        query[...] = (base[...].astype(jnp.float32) + lift).astype(jnp.bfloat16)
 
         def run(reached, numbers):
             chunks = [slice(c * rows, (c + 1) * rows) for c in range(REACH - reached, REACH + 1)]
@@ -340,7 +362,7 @@
         @pl.when(step == count - 1)
         def _():
             folded = fold(r["total"][...], owner_of(info, rank), tenants, rank)
-            projected[...] = folded if before is None else folded + refs[18][...]
+            projected[...] = folded if before is None else folded + refs[19][...]
 
     return pl.pallas_call(
         kernel,
@@ -353,7 +375,7 @@
         in_specs=specs,
         out_specs=[wide(rows), narrow, narrow, pl.BlockSpec((rank, rows), lambda i: (0, 0))],
         scratch_shapes=list(held.values()),
-        input_output_aliases={19: 0} if before is not None else {},
+        input_output_aliases={20: 0} if before is not None else {},
         compiler_params=params(VMEM_HEADS),
         cost_estimate=pl.CostEstimate(
             flops=8 * rows * window * span * count,
@@ -550,6 +572,7 @@
     info = down_project(normed_inputs, adapter, doc, document_tenant, tenants, rank)
     terms = terms_over(info, "mp")
     group = base_queries.shape[1] // HEAD // key_heads
+    *turned, token = turn_operands(base_queries, output_gradient, up, group)
     per = key_heads // chunks
     counts = [1, per - 1, per] if chunks == 2 else [1] * per
     state, pairs, held, with_ids, head = None, [], [], None, 0
@@ -557,12 +580,12 @@
         chunk = head // per
         if len(held) < chunks and i < 2:
             two = shift_over(own[i], "seq")
-            passing, two = relay(own[i], two, terms[1] if i == 0 else state[1])
+            passing, two = relay(own[i], two, [terms[1], token] if i == 0 else [pairs[0][0]])
             held.append((own[i], two, swap_over(two, "sub"), shift_over(passing, ("seq", "sub"))))
         with_ids = held[0]
         out, keep, send, gdown = attention(
-            head, head % per, count, group, base_queries, output_gradient, up, held[chunk],
-            with_ids, info, terms, state, tenants, rank,
+            head, head % per, count, group, turned, up, held[chunk], with_ids,
+            info, terms, state, tenants, rank,
         )
         state = (out, gdown)
         pairs.append((keep, send))
@@ -575,10 +598,10 @@
         early = add_up(pieces)
         keep_a, send_a = small_call(
             functools.partial(split_kernel, tenants, rank), "split_grads", halves_of(tall, width),
-            one, other, info, normed_inputs, after=pieces[1:2],
+            one, other, info, normed_inputs, after=pieces[1:],
         )
         shards = scatter(
-            (keep_late, swap_over(send_late, "sub")), (keep_a, swap_over(send_a, "sub")), after=[early]
+            (keep_late, swap_over(send_late, "sub")), (keep_a, swap_over(send_a, "sub"))
         )
         all_early = spread(early)
         late = add_up(exchange(shards), after=all_early[1:])

time: 123 us -> 124 us (level)
  Pallas kernels: 37.2 us -> 42.2 us
  starting transfers between devices: 48.4 us -> 44.1 us
    pallas_call x2 -> x3, Pallas kernels: 0.21 us -> 5.62 us  [the longest x1 5.42 us: turn_operands(): pl.pallas_call(turn_kernel, grid=(width // span,), out_shape=[shape(rows)...]
    ppermute x9, starting transfers between devices: 10.7 us -> 8.2 us  [swap_over(): return lax.ppermute(block, axis, [(0, 1), (1, 0)])]
    ppermute x12, starting transfers between devices: 26 us -> 24.4 us  [rotate_over(): return lax.ppermute(block, axis, [(i, (i + d) % size) for i in range(size)])]
    unnamed x36 -> x38, local copies, waits for them, and re-layouts: 3.97 us -> 4.84 us
  transfers between devices with their start and end apart: 25 -> 25, of which waited for: 9 -> 10; matrix products, arithmetic and copies ran while one was open for 0% -> 0% of each run, Pallas kernels for 26% -> 30%
where the time goes in v2:
time: 124 us; the launch traced here: 123 us
  starting transfers between devices  44.1 us (36%)
  Pallas kernels  42.2 us (34%)
  waiting for transfers between devices  31 us (25%)
  local copies, waits for them, and re-layouts  4.84 us (4%)
    pallas_call x3, Pallas kernels, attention(): pl.pallas_call(kernel, grid=(count,), out_shape=[jax.ShapeDtypeStruct((ro...  28.4 us
    ppermute x12, starting transfers between devices, rotate_over(): return lax.ppermute(block, axis, [(i, (i + d) % size) for i in range(size)])  24.4 us
    ppermute x12, waiting for transfers between devices, rotate_over(): return lax.ppermute(block, axis, [(i, (i + d) % size) for i in range(size)])  23.7 us
    ppermute x4, starting transfers between devices, shift_over(): return lax.ppermute(block, axis, [(i, i + 1) for i in range(size - 1)])  11.6 us
    ppermute x9, starting transfers between devices, swap_over(): return lax.ppermute(block, axis, [(0, 1), (1, 0)])  8.2 us
    ppermute x9, waiting for transfers between devices, swap_over(): return lax.ppermute(block, axis, [(0, 1), (1, 0)])  7.28 us
    pallas_call x1, Pallas kernels, turn_operands(): pl.pallas_call(turn_kernel, grid=(width // span,), out_shape=[shape(rows)...  5.42 us
    unnamed x38, local copies, waits for them, and re-layouts  4.84 us
  transfers between devices with their start and end apart: 25, of which 10 were waited for; matrix products, arithmetic and copies ran while one was open for 0% of the time, Pallas kernels for 30%

profile of v2, /device:TPU:0, one launch (start us, length us, event | category | flops | bytes accessed | tf_op | source)
XLA Modules:
  0.0 123.1 jit_solution(16661866158709749638)
XLA Ops:
  0.6 1.9 %pack_keys_values.1 = (bf16[272,512]{1,0:T(8,128)(2,1)}, bf16[272,512]{1,0:T(8,128)(2,1)}) custom-call(bf16[256,512]{1,0:T(8,128)(2,1)} %keys.1, bf16[256,512]{1,0:T(8,128)(2,1)} %values.1, s32[1,256]{1,0:T(1,128)} %bitcast.14), custom_call_target="tpu_custom_call" | custom-call | bytes 1048576 | tf_op jit(solution)/shard_map/pack_keys_values/pallas_call | solution.py:70
  2.5 4.9 %collective-permute-start.1 = (bf16[272,512]{1,0:T(8,128)(2,1)}, bf16[272,512]{1,0:T(8,128)(2,1)S(1)}, u32[]{:S(2)}, u32[]{:S(2)}) collective-permute-start(bf16[272,512]{1,0:T(8,128)(2,1)} %get-tuple-element.41.own.refs_4_.refs_5_.refs_12_), channel_id=1, source_target_pairs={{0,4},{4,8},{8,12},{1,5},{5,9},{9,13},{2,6},{6,10},{10,14},{3,7},{... | collective-permute-start | bytes 835592 | tf_op jit(solution)/shard_map/ppermute | solution.py:553
  7.5 3.4 %down_project.1.refs_16_.refs_17_.refs_2_ = f32[24,256]{1,0:T(8,128)} custom-call(bf16[256,2560]{1,0:T(8,128)(2,1)} %refs_3_.1, bf16[128,2560]{1,0:T(8,128)(2,1)} %bitcast.13, s32[1,256]{1,0:T(1,128)} %bitcast.15, s32[16]{0:T(128)} %tenant_of.1), custom_call_target="tpu_custom_call" | custom-call | flops 167772160 | bytes 1966080 | tf_op jit(solution)/shard_map/down_project/pallas_call | solution.py:157
  10.8 1.6 %collective-permute-start.2 = (f32[24,256]{1,0:T(8,128)}, f32[24,256]{1,0:T(8,128)S(1)}, u32[]{:S(2)}, u32[]{:S(2)}) collective-permute-start(f32[24,256]{1,0:T(8,128)} %down_project.1.refs_16_.refs_17_.refs_2_), channel_id=1, source_target_pairs={{0,2},{2,0},{1,3},{3,1},{4,6},{6,4},{5,7},{7,5},{8,10},{10,8},{9,1... | collective-permute-start | bytes 73736 | tf_op jit(solution)/shard_map/ppermute | solution.py:537
  12.4 5.4 %turn_operands.1 = (bf16[4096,256]{1,0:T(8,128)(2,1)}, bf16[4096,256]{1,0:T(8,128)(2,1)}, bf16[4096,128]{1,0:T(8,128)(2,1)}, f32[8,128]{1,0:T(8,128)}) custom-call(bf16[256,4096]{1,0:T(8,128)(2,1)} %base.1, bf16[256,4096]{1,0:T(8,128)(2,1)} %grad.1, bf16[128,4096]{1,0:T(8,128)(2,1)} %bitcast.9), custom_call_target="tpu_custom_call" | custom-call | bytes 10485760 | tf_op jit(solution)/shard_map/turn_operands/pallas_call | solution.py:194
  17.9 0.7 copy-done.13
  18.5 0.1 relay_block.2
  18.7 1.3 %collective-permute-start.4 = (bf16[272,512]{1,0:T(8,128)(2,1)S(1)}, bf16[272,512]{1,0:T(8,128)(2,1)S(1)}, u32[]{:S(2)}, u32[]{:S(2)}) collective-permute-start(bf16[272,512]{1,0:T(8,128)(2,1)S(1)} %get-tuple-element.44), channel_id=1, source_target_pairs={{0,1},{1,4},{4,5},{5,8},{8,9},{9,12},{12,13},{2,3},{3,6},{6,7},{7,... | collective-permute-start | bytes 835592 | tf_op jit(solution)/shard_map/ppermute | solution.py:553
  20.0 2.3 %collective-permute-start.3 = (bf16[272,512]{1,0:T(8,128)(2,1)S(1)}, bf16[272,512]{1,0:T(8,128)(2,1)S(1)}, u32[]{:S(2)}, u32[]{:S(2)}) collective-permute-start(bf16[272,512]{1,0:T(8,128)(2,1)S(1)} %get-tuple-element.43.refs_6_.refs_7_.refs_13_), channel_id=1, source_target_pairs={{0,1},{1,0},{2,3},{3,2},{4,5},{5,4},{6,7},{7,6},{8,9},{9,8},{10,11... | collective-permute-start | bytes 835592 | tf_op jit(solution)/shard_map/ppermute | solution.py:537
  22.3 3.5 %collective-permute-start = (bf16[272,512]{1,0:T(8,128)(2,1)S(1)}, bf16[272,512]{1,0:T(8,128)(2,1)S(1)}, u32[]{:S(2)}, u32[]{:S(2)}) collective-permute-start(bf16[272,512]{1,0:T(8,128)(2,1)S(1)} %copy-done.8), channel_id=1, source_target_pairs={{0,4},{4,8},{8,12},{1,5},{5,9},{9,13},{2,6},{6,10},{10,14},{3,7},{... | collective-permute-start | bytes 835592 | tf_op jit(solution)/shard_map/ppermute | solution.py:553
  25.9 0.7 copy-done.14
  26.5 0.1 copy-done.15
  26.6 7.4 %attention.3 = (bf16[256,4096]{1,0:T(8,128)(2,1)}, bf16[64,1024]{1,0:T(8,128)(2,1)}, bf16[64,1024]{1,0:T(8,128)(2,1)}, f32[16,256]{1,0:T(8,128)}) custom-call(bf16[4096,256]{1,0:T(8,128)(2,1)} %get-tuple-element.37.refs_0_, bf16[4096,256]{1,0:T(8,128)(2,1)} %get-tuple-element.38.refs_1_, bf16[4096,128]{1,0:T(8,128)(2,1)} %get-tuple-element.39.refs_2_, ...), custom_call_target="tpu_custom_call" | custom-call | flops 2147483648 | bytes 1572864 | tf_op jit(solution)/shard_map/attention/pallas_call | solution.py:367
  34.0 0.9 copy-done.6
  34.9 0.1 relay_block.3
  35.1 1.8 %collective-permute-start.6 = (bf16[272,512]{1,0:T(8,128)(2,1)S(1)}, bf16[272,512]{1,0:T(8,128)(2,1)S(1)}, u32[]{:S(2)}, u32[]{:S(2)}) collective-permute-start(bf16[272,512]{1,0:T(8,128)(2,1)S(1)} %get-tuple-element.47), channel_id=1, source_target_pairs={{0,1},{1,4},{4,5},{5,8},{8,9},{9,12},{12,13},{2,3},{3,6},{6,7},{7,... | collective-permute-start | bytes 835592 | tf_op jit(solution)/shard_map/ppermute | solution.py:553
  36.9 2.5 %collective-permute-start.5 = (bf16[272,512]{1,0:T(8,128)(2,1)S(1)}, bf16[272,512]{1,0:T(8,128)(2,1)S(1)}, u32[]{:S(2)}, u32[]{:S(2)}) collective-permute-start(bf16[272,512]{1,0:T(8,128)(2,1)S(1)} %get-tuple-element.46.refs_6_.refs_7_), channel_id=1, source_target_pairs={{0,1},{1,0},{2,3},{3,2},{4,5},{5,4},{6,7},{7,6},{8,9},{9,8},{10,11... | collective-permute-start | bytes 835592 | tf_op jit(solution)/shard_map/ppermute | solution.py:537
  39.5 7.8 %attention.4 = (bf16[256,4096]{1,0:T(8,128)(2,1)}, bf16[64,1024]{1,0:T(8,128)(2,1)}, bf16[64,1024]{1,0:T(8,128)(2,1)}, f32[16,256]{1,0:T(8,128)}) custom-call(bf16[4096,256]{1,0:T(8,128)(2,1)} %get-tuple-element.37.refs_0_, bf16[4096,256]{1,0:T(8,128)(2,1)} %get-tuple-element.38.refs_1_, ...), custom_call_target="tpu_custom_call", output_to_operand_aliasing={{0}: (20, {})} | custom-call | flops 2147483648 | bytes 1572864 | tf_op jit(solution)/shard_map/attention/pallas_call | solution.py:367
  47.3 0.5 collective-permute-start.8
  47.9 0.7 copy-done.16
  48.7 13.2 %attention.5 = (bf16[256,4096]{1,0:T(8,128)(2,1)}, bf16[64,2048]{1,0:T(8,128)(2,1)}, bf16[64,2048]{1,0:T(8,128)(2,1)}, f32[16,256]{1,0:T(8,128)}) custom-call(bf16[4096,256]{1,0:T(8,128)(2,1)} %get-tuple-element.37.refs_0_, bf16[4096,256]{1,0:T(8,128)(2,1)} %get-tuple-element.38.refs_1_, ...), custom_call_target="tpu_custom_call", output_to_operand_aliasing={{0}: (20, {})} | custom-call | flops 4294967296 | bytes 3145728 | tf_op jit(solution)/shard_map/attention/pallas_call | solution.py:367
  61.9 0.9 copy-done.3
  62.8 0.1 scatter_grads.2
  63.0 1.9 %collective-permute-start.9 = (bf16[16,2048]{1,0:T(8,128)(2,1)S(1)}, bf16[16,2048]{1,0:T(8,128)(2,1)S(1)}, u32[]{:S(2)}, u32[]{:S(2)}) collective-permute-start(bf16[16,2048]{1,0:T(8,128)(2,1)S(1)} %get-tuple-element.58), channel_id=1, source_target_pairs={{0,4},{4,8},{8,12},{12,0},{1,5},{5,9},{9,13},{13,1},{2,6},{6,10},{... | collective-permute-start | bytes 196616 | tf_op jit(solution)/shard_map/ppermute | solution.py:542
  64.8 5.4 %collective-permute-start.10 = (bf16[16,2048]{1,0:T(8,128)(2,1)S(1)}, bf16[16,2048]{1,0:T(8,128)(2,1)S(1)}, u32[]{:S(2)}, u32[]{:S(2)}) collective-permute-start(bf16[16,2048]{1,0:T(8,128)(2,1)S(1)} %get-tuple-element.59), channel_id=1, source_target_pairs={{0,8},{4,12},{8,0},{12,4},{1,9},{5,13},{9,1},{13,5},{2,10},{6,14},... | collective-permute-start | bytes 196616 | tf_op jit(solution)/shard_map/ppermute | solution.py:542
  70.2 0.5 collective-permute-start.16
  70.8 3.4 %collective-permute-done.16.refs_1_ = f32[16,256]{1,0:T(8,128)S(1)} collective-permute-done((f32[16,256]{1,0:T(8,128)}, f32[16,256]{1,0:T(8,128)S(1)}, u32[]{:S(2)}, u32[]{:S(2)}) %collective-permute-start.16) | collective-permute-done | bytes 16416 | tf_op jit(solution)/shard_map/ppermute | solution.py:537
  74.2 1.1 collective-permute-done.10.refs_2_.refs_5_
  75.3 0.5 collective-permute-done.11.refs_3_.refs_6_
  75.8 0.7 copy-done.12
  76.5 0.4 split_grads.1
  77.0 0.5 collective-permute-start.15
  77.5 1.5 %collective-permute-done.15.refs_1_ = bf16[64,2048]{1,0:T(8,128)(2,1)S(1)} collective-permute-done((bf16[64,2048]{1,0:T(8,128)(2,1)S(1)}, bf16[64,2048]{1,0:T(8,128)(2,1)S(1)}, u32[]{:S(2)}, u32[]{:S(2)}) %collective-permute-start.15) | collective-permute-done | bytes 262176 | tf_op jit(solution)/shard_map/ppermute | solution.py:537
  79.0 0.3 scatter_grads.3
  79.3 1.5 %collective-permute-start.18 = (bf16[16,4608]{1,0:T(8,128)(2,1)S(1)}, bf16[16,4608]{1,0:T(8,128)(2,1)S(1)}, u32[]{:S(2)}, u32[]{:S(2)}) collective-permute-start(bf16[16,4608]{1,0:T(8,128)(2,1)S(1)} %get-tuple-element.66), channel_id=1, source_target_pairs={{0,4},{4,8},{8,12},{12,0},{1,5},{5,9},{9,13},{13,1},{2,6},{6,10},{... | collective-permute-start | bytes 442376 | tf_op jit(solution)/shard_map/ppermute | solution.py:542
  80.8 1.3 %collective-permute-start.19 = (bf16[16,4608]{1,0:T(8,128)(2,1)S(1)}, bf16[16,4608]{1,0:T(8,128)(2,1)S(1)}, u32[]{:S(2)}, u32[]{:S(2)}) collective-permute-start(bf16[16,4608]{1,0:T(8,128)(2,1)S(1)} %get-tuple-element.67), channel_id=1, source_target_pairs={{0,8},{4,12},{8,0},{12,4},{1,9},{5,13},{9,1},{13,5},{2,10},{6,14},... | collective-permute-start | bytes 442376 | tf_op jit(solution)/shard_map/ppermute | solution.py:542
  82.1 1.1 collective-permute-start.20
  83.3 2.0 %collective-permute-start.14 = (bf16[16,2048]{1,0:T(8,128)(2,1)S(1)}, bf16[16,2048]{1,0:T(8,128)(2,1)S(1)}, u32[]{:S(2)}, u32[]{:S(2)}) collective-permute-start(bf16[16,2048]{1,0:T(8,128)(2,1)S(1)} %sum_grads.2.refs_0_), channel_id=1, source_target_pairs={{0,12},{4,0},{8,4},{12,8},{1,13},{5,1},{9,5},{13,9},{2,14},{6,2},{... | collective-permute-start | bytes 196616 | tf_op jit(solution)/shard_map/ppermute | solution.py:542
  85.3 0.4 collective-permute-start.13
  85.7 9.1 %collective-permute-done.14.refs_6_.refs_3_ = bf16[16,2048]{1,0:T(8,128)(2,1)S(1)} collective-permute-done((bf16[16,2048]{1,0:T(8,128)(2,1)S(1)}, bf16[16,2048]{1,0:T(8,128)(2,1)S(1)}, u32[]{:S(2)}, u32[]{:S(2)}) %collective-permute-start.14) | collective-permute-done | bytes 65568 | tf_op jit(solution)/shard_map/ppermute | solution.py:542
  94.7 6.7 %collective-permute-start.12 = (bf16[16,2048]{1,0:T(8,128)(2,1)S(1)}, bf16[16,2048]{1,0:T(8,128)(2,1)S(1)}, u32[]{:S(2)}, u32[]{:S(2)}) collective-permute-start(bf16[16,2048]{1,0:T(8,128)(2,1)S(1)} %sum_grads.2.refs_0_), channel_id=1, source_target_pairs={{0,4},{4,8},{8,12},{12,0},{1,5},{5,9},{9,13},{13,1},{2,6},{6,10},{... | collective-permute-start | bytes 196616 | tf_op jit(solution)/shard_map/ppermute | solution.py:542
  101.4 0.7 collective-permute-done.13.refs_5_.refs_2_
  102.2 1.5 %collective-permute-done.12.refs_4_.refs_1_ = bf16[16,2048]{1,0:T(8,128)(2,1)S(1)} collective-permute-done((bf16[16,2048]{1,0:T(8,128)(2,1)S(1)}, bf16[16,2048]{1,0:T(8,128)(2,1)S(1)}, u32[]{:S(2)}, u32[]{:S(2)}) %collective-permute-start.12) | collective-permute-done | bytes 65568 | tf_op jit(solution)/shard_map/ppermute | solution.py:542
  103.9 3.9 %collective-permute-start.22 = (bf16[16,4608]{1,0:T(8,128)(2,1)S(1)}, bf16[16,4608]{1,0:T(8,128)(2,1)S(1)}, u32[]{:S(2)}, u32[]{:S(2)}) collective-permute-start(bf16[16,4608]{1,0:T(8,128)(2,1)S(1)} %sum_grads.3.refs_4_), channel_id=1, source_target_pairs={{0,8},{4,12},{8,0},{12,4},{1,9},{5,13},{9,1},{13,5},{2,10},{6,14},... | collective-permute-start | bytes 442376 | tf_op jit(solution)/shard_map/ppermute | solution.py:542
  107.8 2.9 %collective-permute-done.23.refs_7_ = bf16[16,4608]{1,0:T(8,128)(2,1)S(1)} collective-permute-done((bf16[16,4608]{1,0:T(8,128)(2,1)S(1)}, bf16[16,4608]{1,0:T(8,128)(2,1)S(1)}, u32[]{:S(2)}, u32[]{:S(2)}) %collective-permute-start.23) | collective-permute-done | bytes 147488 | tf_op jit(solution)/shard_map/ppermute | solution.py:542
  110.7 7.9 %collective-permute-done.22.refs_6_ = bf16[16,4608]{1,0:T(8,128)(2,1)S(1)} collective-permute-done((bf16[16,4608]{1,0:T(8,128)(2,1)S(1)}, bf16[16,4608]{1,0:T(8,128)(2,1)S(1)}, u32[]{:S(2)}, u32[]{:S(2)}) %collective-permute-start.22) | collective-permute-done | bytes 147488 | tf_op jit(solution)/shard_map/ppermute | solution.py:542
  118.8 2.4 %collective-permute-done.24.refs_1_ = bf16[64,6656]{1,0:T(8,128)(2,1)S(1)} collective-permute-done((bf16[64,6656]{1,0:T(8,128)(2,1)S(1)}, bf16[64,6656]{1,0:T(8,128)(2,1)S(1)}, u32[]{:S(2)}, u32[]{:S(2)}) %collective-permute-start.24) | collective-permute-done | bytes 852000 | tf_op jit(solution)/shard_map/ppermute | solution.py:537
  121.1 1.9 %finish_grads.1 = (f32[128,4096]{1,0:T(8,128)}, f32[128,2560]{1,0:T(8,128)}) custom-call(bf16[64,6656]{1,0:T(8,128)(2,1)S(1)} %gather_grads.1.refs_0_, bf16[64,6656]{1,0:T(8,128)(2,1)S(1)} %collective-permute-done.24.refs_1_), custom_call_target="tpu_custom_call" | custom-call | flops 1703936 | bytes 3407872 | tf_op jit(solution)/shard_map/finish_grads/pallas_call | solution.py:394
  (55 shorter events, 0.7 us)
Async XLA Ops:
  2.5 15.3 %collective-permute-start.1 = (bf16[272,512]{1,0:T(8,128)(2,1)}, bf16[272,512]{1,0:T(8,128)(2,1)S(1)}, u32[]{:S(2)}, u32[]{:S(2)}) collective-permute-start(bf16[272,512]{1,0:T(8,128)(2,1)} %get-tuple-element.41.own.refs_4_.refs_5_.refs_12_), channel_id=1, source_target_pairs={{0,4},{4,8},{8,12},{1,5},{5,9},{9,13},{2,6},{6,10},{10,14},{3,7},{... | collective-permute-start | bytes 835592 | tf_op jit(solution)/shard_map/ppermute | solution.py:553
  10.8 7.0 %collective-permute-start.2 = (f32[24,256]{1,0:T(8,128)}, f32[24,256]{1,0:T(8,128)S(1)}, u32[]{:S(2)}, u32[]{:S(2)}) collective-permute-start(f32[24,256]{1,0:T(8,128)} %down_project.1.refs_16_.refs_17_.refs_2_), channel_id=1, source_target_pairs={{0,2},{2,0},{1,3},{3,1},{4,6},{6,4},{5,7},{7,5},{8,10},{10,8},{9,1... | collective-permute-start | bytes 73736 | tf_op jit(solution)/shard_map/ppermute | solution.py:537
  12.4 5.4 %copy-start = (bf16[272,512]{1,0:T(8,128)(2,1)S(1)}, bf16[272,512]{1,0:T(8,128)(2,1)}, u32[]{:S(2)}) copy-start(bf16[272,512]{1,0:T(8,128)(2,1)} %get-tuple-element.41.own.refs_4_.refs_5_.refs_12_) | copy-start | bytes 835588
  12.4 9.9 %copy-start.8 = (bf16[272,512]{1,0:T(8,128)(2,1)S(1)}, bf16[272,512]{1,0:T(8,128)(2,1)}, u32[]{:S(2)}) copy-start(bf16[272,512]{1,0:T(8,128)(2,1)} %get-tuple-element.40.own.refs_4_.refs_5_) | copy-start | bytes 835588
  17.8 8.0 %copy-start.10 = (f32[24,256]{1,0:T(8,128)}, f32[24,256]{1,0:T(8,128)S(1)}, u32[]{:S(2)}) copy-start(f32[24,256]{1,0:T(8,128)S(1)} %collective-permute-done.2.rest_0_.refs_18_) | copy-start | bytes 73732
  17.9 0.7 copy-start.13
  18.6 7.2 %copy-start.1 = (bf16[272,512]{1,0:T(8,128)(2,1)}, bf16[272,512]{1,0:T(8,128)(2,1)S(1)}, u32[]{:S(2)}) copy-start(bf16[272,512]{1,0:T(8,128)(2,1)S(1)} %get-tuple-element.43.refs_6_.refs_7_.refs_13_) | copy-start | bytes 835588
  18.7 7.2 %collective-permute-start.4 = (bf16[272,512]{1,0:T(8,128)(2,1)S(1)}, bf16[272,512]{1,0:T(8,128)(2,1)S(1)}, u32[]{:S(2)}, u32[]{:S(2)}) collective-permute-start(bf16[272,512]{1,0:T(8,128)(2,1)S(1)} %get-tuple-element.44), channel_id=1, source_target_pairs={{0,1},{1,4},{4,5},{5,8},{8,9},{9,12},{12,13},{2,3},{3,6},{6,7},{7,... | collective-permute-start | bytes 835592 | tf_op jit(solution)/shard_map/ppermute | solution.py:553
  20.0 5.9 %collective-permute-start.3 = (bf16[272,512]{1,0:T(8,128)(2,1)S(1)}, bf16[272,512]{1,0:T(8,128)(2,1)S(1)}, u32[]{:S(2)}, u32[]{:S(2)}) collective-permute-start(bf16[272,512]{1,0:T(8,128)(2,1)S(1)} %get-tuple-element.43.refs_6_.refs_7_.refs_13_), channel_id=1, source_target_pairs={{0,1},{1,0},{2,3},{3,2},{4,5},{5,4},{6,7},{7,6},{8,9},{9,8},{10,11... | collective-permute-start | bytes 835592 | tf_op jit(solution)/shard_map/ppermute | solution.py:537
  22.3 11.7 %collective-permute-start = (bf16[272,512]{1,0:T(8,128)(2,1)S(1)}, bf16[272,512]{1,0:T(8,128)(2,1)S(1)}, u32[]{:S(2)}, u32[]{:S(2)}) collective-permute-start(bf16[272,512]{1,0:T(8,128)(2,1)S(1)} %copy-done.8), channel_id=1, source_target_pairs={{0,4},{4,8},{8,12},{1,5},{5,9},{9,13},{2,6},{6,10},{10,14},{3,7},{... | collective-permute-start | bytes 835592 | tf_op jit(solution)/shard_map/ppermute | solution.py:553
  25.8 0.7 copy-start.14
  25.8 0.8 copy-start.15
  34.0 0.9 copy-start.6
  35.0 12.3 %copy-start.9 = (bf16[272,512]{1,0:T(8,128)(2,1)}, bf16[272,512]{1,0:T(8,128)(2,1)S(1)}, u32[]{:S(2)}) copy-start(bf16[272,512]{1,0:T(8,128)(2,1)S(1)} %get-tuple-element.46.refs_6_.refs_7_) | copy-start | bytes 835588
  35.1 12.8 %collective-permute-start.6 = (bf16[272,512]{1,0:T(8,128)(2,1)S(1)}, bf16[272,512]{1,0:T(8,128)(2,1)S(1)}, u32[]{:S(2)}, u32[]{:S(2)}) collective-permute-start(bf16[272,512]{1,0:T(8,128)(2,1)S(1)} %get-tuple-element.47), channel_id=1, source_target_pairs={{0,1},{1,4},{4,5},{5,8},{8,9},{9,12},{12,13},{2,3},{3,6},{6,7},{7,... | collective-permute-start | bytes 835592 | tf_op jit(solution)/shard_map/ppermute | solution.py:553
  36.9 11.0 %collective-permute-start.5 = (bf16[272,512]{1,0:T(8,128)(2,1)S(1)}, bf16[272,512]{1,0:T(8,128)(2,1)S(1)}, u32[]{:S(2)}, u32[]{:S(2)}) collective-permute-start(bf16[272,512]{1,0:T(8,128)(2,1)S(1)} %get-tuple-element.46.refs_6_.refs_7_), channel_id=1, source_target_pairs={{0,1},{1,0},{2,3},{3,2},{4,5},{5,4},{6,7},{7,6},{8,9},{9,8},{10,11... | collective-permute-start | bytes 835592 | tf_op jit(solution)/shard_map/ppermute | solution.py:537
  39.4 22.4 %collective-permute-start.7 = (bf16[64,1024]{1,0:T(8,128)(2,1)}, bf16[64,1024]{1,0:T(8,128)(2,1)S(1)}, u32[]{:S(2)}, u32[]{:S(2)}) collective-permute-start(bf16[64,1024]{1,0:T(8,128)(2,1)} %get-tuple-element.53), channel_id=1, source_target_pairs={{0,1},{1,0},{2,3},{3,2},{4,5},{5,4},{6,7},{7,6},{8,9},{9,8},{10,11... | collective-permute-start | bytes 393224 | tf_op jit(solution)/shard_map/ppermute | solution.py:537
  47.3 14.5 %collective-permute-start.8 = (bf16[64,1024]{1,0:T(8,128)(2,1)}, bf16[64,1024]{1,0:T(8,128)(2,1)S(1)}, u32[]{:S(2)}, u32[]{:S(2)}) collective-permute-start(bf16[64,1024]{1,0:T(8,128)(2,1)} %get-tuple-element.55), channel_id=1, source_target_pairs={{0,1},{1,0},{2,3},{3,2},{4,5},{5,4},{6,7},{7,6},{8,9},{9,8},{10,11... | collective-permute-start | bytes 393224 | tf_op jit(solution)/shard_map/ppermute | solution.py:537
  47.8 0.7 copy-start.16
  47.8 0.8 copy-start.17
  48.7 13.2 %copy-start.7 = (bf16[64,1024]{1,0:T(8,128)(2,1)S(1)}, bf16[64,1024]{1,0:T(8,128)(2,1)}, u32[]{:S(2)}) copy-start(bf16[64,1024]{1,0:T(8,128)(2,1)} %get-tuple-element.45.rest_0_.refs_0_) | copy-start | bytes 393220
  48.7 13.2 %copy-start.11 = (bf16[64,1024]{1,0:T(8,128)(2,1)S(1)}, bf16[64,1024]{1,0:T(8,128)(2,1)}, u32[]{:S(2)}) copy-start(bf16[64,1024]{1,0:T(8,128)(2,1)} %get-tuple-element.54.refs_2_) | copy-start | bytes 393220
  48.7 27.1 %copy-start.2 = (bf16[256,2560]{1,0:T(8,128)(2,1)S(1)}, bf16[256,2560]{1,0:T(8,128)(2,1)}, u32[]{:S(2)}) copy-start(bf16[256,2560]{1,0:T(8,128)(2,1)} %refs_3_.1) | copy-start | bytes 3932164
  48.7 27.1 %copy-start.5 = (f32[24,256]{1,0:T(8,128)S(1)}, f32[24,256]{1,0:T(8,128)}, u32[]{:S(2)}) copy-start(f32[24,256]{1,0:T(8,128)} %down_project.1.refs_16_.refs_17_.refs_2_) | copy-start | bytes 73732
  61.9 1.0 copy-start.3
  62.8 14.1 %copy-start.18 = (bf16[64,2048]{1,0:T(8,128)(2,1)S(1)}, bf16[64,2048]{1,0:T(8,128)(2,1)}, u32[]{:S(2)}) copy-start(bf16[64,2048]{1,0:T(8,128)(2,1)} %get-tuple-element.61) | copy-start | bytes 786436
  62.8 16.1 %copy-start.4 = (bf16[64,2048]{1,0:T(8,128)(2,1)S(1)}, bf16[64,2048]{1,0:T(8,128)(2,1)}, u32[]{:S(2)}) copy-start(bf16[64,2048]{1,0:T(8,128)(2,1)} %get-tuple-element.56.refs_4_.refs_0_) | copy-start | bytes 786436
  63.0 11.2 %collective-permute-start.9 = (bf16[16,2048]{1,0:T(8,128)(2,1)S(1)}, bf16[16,2048]{1,0:T(8,128)(2,1)S(1)}, u32[]{:S(2)}, u32[]{:S(2)}) collective-permute-start(bf16[16,2048]{1,0:T(8,128)(2,1)S(1)} %get-tuple-element.58), channel_id=1, source_target_pairs={{0,4},{4,8},{8,12},{12,0},{1,5},{5,9},{9,13},{13,1},{2,6},{6,10},{... | collective-permute-start | bytes 196616 | tf_op jit(solution)/shard_map/ppermute | solution.py:542
  64.8 10.5 %collective-permute-start.10 = (bf16[16,2048]{1,0:T(8,128)(2,1)S(1)}, bf16[16,2048]{1,0:T(8,128)(2,1)S(1)}, u32[]{:S(2)}, u32[]{:S(2)}) collective-permute-start(bf16[16,2048]{1,0:T(8,128)(2,1)S(1)} %get-tuple-element.59), channel_id=1, source_target_pairs={{0,8},{4,12},{8,0},{12,4},{1,9},{5,13},{9,1},{13,5},{2,10},{6,14},... | collective-permute-start | bytes 196616 | tf_op jit(solution)/shard_map/ppermute | solution.py:542
  70.2 5.5 %collective-permute-start.11 = (bf16[16,2048]{1,0:T(8,128)(2,1)S(1)}, bf16[16,2048]{1,0:T(8,128)(2,1)S(1)}, u32[]{:S(2)}, u32[]{:S(2)}) collective-permute-start(bf16[16,2048]{1,0:T(8,128)(2,1)S(1)} %get-tuple-element.60), channel_id=1, source_target_pairs={{0,12},{4,0},{8,4},{12,8},{1,13},{5,1},{9,5},{13,9},{2,14},{6,2},{... | collective-permute-start | bytes 196616 | tf_op jit(solution)/shard_map/ppermute | solution.py:542
  70.2 3.9 %collective-permute-start.16 = (f32[16,256]{1,0:T(8,128)}, f32[16,256]{1,0:T(8,128)S(1)}, u32[]{:S(2)}, u32[]{:S(2)}) collective-permute-start(f32[16,256]{1,0:T(8,128)} %get-tuple-element.62.refs_0_), channel_id=1, source_target_pairs={{0,2},{2,0},{1,3},{3,1},{4,6},{6,4},{5,7},{7,5},{8,10},{10,8},{9,1... | collective-permute-start | bytes 49160 | tf_op jit(solution)/shard_map/ppermute | solution.py:537
  75.8 0.7 copy-start.12
  76.9 2.1 %collective-permute-start.17 = (bf16[64,2560]{1,0:T(8,128)(2,1)S(1)}, bf16[64,2560]{1,0:T(8,128)(2,1)S(1)}, u32[]{:S(2)}, u32[]{:S(2)}) collective-permute-start(bf16[64,2560]{1,0:T(8,128)(2,1)S(1)} %get-tuple-element.64), channel_id=1, source_target_pairs={{0,1},{1,0},{2,3},{3,2},{4,5},{5,4},{6,7},{7,6},{8,9},{9,8},{10,11... | collective-permute-start | bytes 983048 | tf_op jit(solution)/shard_map/ppermute | solution.py:537
  77.0 2.0 %collective-permute-start.15 = (bf16[64,2048]{1,0:T(8,128)(2,1)S(1)}, bf16[64,2048]{1,0:T(8,128)(2,1)S(1)}, u32[]{:S(2)}, u32[]{:S(2)}) collective-permute-start(bf16[64,2048]{1,0:T(8,128)(2,1)S(1)} %copy-done.18), channel_id=1, source_target_pairs={{0,1},{1,0},{2,3},{3,2},{4,5},{5,4},{6,7},{7,6},{8,9},{9,8},{10,11... | collective-permute-start | bytes 786440 | tf_op jit(solution)/shard_map/ppermute | solution.py:537
  79.3 24.4 %collective-permute-start.18 = (bf16[16,4608]{1,0:T(8,128)(2,1)S(1)}, bf16[16,4608]{1,0:T(8,128)(2,1)S(1)}, u32[]{:S(2)}, u32[]{:S(2)}) collective-permute-start(bf16[16,4608]{1,0:T(8,128)(2,1)S(1)} %get-tuple-element.66), channel_id=1, source_target_pairs={{0,4},{4,8},{8,12},{12,0},{1,5},{5,9},{9,13},{13,1},{2,6},{6,10},{... | collective-permute-start | bytes 442376 | tf_op jit(solution)/shard_map/ppermute | solution.py:542
  80.8 22.9 %collective-permute-start.19 = (bf16[16,4608]{1,0:T(8,128)(2,1)S(1)}, bf16[16,4608]{1,0:T(8,128)(2,1)S(1)}, u32[]{:S(2)}, u32[]{:S(2)}) collective-permute-start(bf16[16,4608]{1,0:T(8,128)(2,1)S(1)} %get-tuple-element.67), channel_id=1, source_target_pairs={{0,8},{4,12},{8,0},{12,4},{1,9},{5,13},{9,1},{13,5},{2,10},{6,14},... | collective-permute-start | bytes 442376 | tf_op jit(solution)/shard_map/ppermute | solution.py:542
  82.1 21.6 %collective-permute-start.20 = (bf16[16,4608]{1,0:T(8,128)(2,1)S(1)}, bf16[16,4608]{1,0:T(8,128)(2,1)S(1)}, u32[]{:S(2)}, u32[]{:S(2)}) collective-permute-start(bf16[16,4608]{1,0:T(8,128)(2,1)S(1)} %get-tuple-element.68), channel_id=1, source_target_pairs={{0,12},{4,0},{8,4},{12,8},{1,13},{5,1},{9,5},{13,9},{2,14},{6,2},{... | collective-permute-start | bytes 442376 | tf_op jit(solution)/shard_map/ppermute | solution.py:542
  83.3 11.5 %collective-permute-start.14 = (bf16[16,2048]{1,0:T(8,128)(2,1)S(1)}, bf16[16,2048]{1,0:T(8,128)(2,1)S(1)}, u32[]{:S(2)}, u32[]{:S(2)}) collective-permute-start(bf16[16,2048]{1,0:T(8,128)(2,1)S(1)} %sum_grads.2.refs_0_), channel_id=1, source_target_pairs={{0,12},{4,0},{8,4},{12,8},{1,13},{5,1},{9,5},{13,9},{2,14},{6,2},{... | collective-permute-start | bytes 196616 | tf_op jit(solution)/shard_map/ppermute | solution.py:542
  85.3 16.9 %collective-permute-start.13 = (bf16[16,2048]{1,0:T(8,128)(2,1)S(1)}, bf16[16,2048]{1,0:T(8,128)(2,1)S(1)}, u32[]{:S(2)}, u32[]{:S(2)}) collective-permute-start(bf16[16,2048]{1,0:T(8,128)(2,1)S(1)} %sum_grads.2.refs_0_), channel_id=1, source_target_pairs={{0,8},{4,12},{8,0},{12,4},{1,9},{5,13},{9,1},{13,5},{2,10},{6,14},... | collective-permute-start | bytes 196616 | tf_op jit(solution)/shard_map/ppermute | solution.py:542
  94.7 9.0 %collective-permute-start.12 = (bf16[16,2048]{1,0:T(8,128)(2,1)S(1)}, bf16[16,2048]{1,0:T(8,128)(2,1)S(1)}, u32[]{:S(2)}, u32[]{:S(2)}) collective-permute-start(bf16[16,2048]{1,0:T(8,128)(2,1)S(1)} %sum_grads.2.refs_0_), channel_id=1, source_target_pairs={{0,4},{4,8},{8,12},{12,0},{1,5},{5,9},{9,13},{13,1},{2,6},{6,10},{... | collective-permute-start | bytes 196616 | tf_op jit(solution)/shard_map/ppermute | solution.py:542
  103.8 6.9 %collective-permute-start.23 = (bf16[16,4608]{1,0:T(8,128)(2,1)S(1)}, bf16[16,4608]{1,0:T(8,128)(2,1)S(1)}, u32[]{:S(2)}, u32[]{:S(2)}) collective-permute-start(bf16[16,4608]{1,0:T(8,128)(2,1)S(1)} %sum_grads.3.refs_4_), channel_id=1, source_target_pairs={{0,12},{4,0},{8,4},{12,8},{1,13},{5,1},{9,5},{13,9},{2,14},{6,2},{... | collective-permute-start | bytes 442376 | tf_op jit(solution)/shard_map/ppermute | solution.py:542
  103.9 14.7 %collective-permute-start.22 = (bf16[16,4608]{1,0:T(8,128)(2,1)S(1)}, bf16[16,4608]{1,0:T(8,128)(2,1)S(1)}, u32[]{:S(2)}, u32[]{:S(2)}) collective-permute-start(bf16[16,4608]{1,0:T(8,128)(2,1)S(1)} %sum_grads.3.refs_4_), channel_id=1, source_target_pairs={{0,8},{4,12},{8,0},{12,4},{1,9},{5,13},{9,1},{13,5},{2,10},{6,14},... | collective-permute-start | bytes 442376 | tf_op jit(solution)/shard_map/ppermute | solution.py:542
  107.8 10.8 %collective-permute-start.21 = (bf16[16,4608]{1,0:T(8,128)(2,1)S(1)}, bf16[16,4608]{1,0:T(8,128)(2,1)S(1)}, u32[]{:S(2)}, u32[]{:S(2)}) collective-permute-start(bf16[16,4608]{1,0:T(8,128)(2,1)S(1)} %sum_grads.3.refs_4_), channel_id=1, source_target_pairs={{0,4},{4,8},{8,12},{12,0},{1,5},{5,9},{9,13},{13,1},{2,6},{6,10},{... | collective-permute-start | bytes 442376 | tf_op jit(solution)/shard_map/ppermute | solution.py:542
  118.7 2.4 %collective-permute-start.24 = (bf16[64,6656]{1,0:T(8,128)(2,1)S(1)}, bf16[64,6656]{1,0:T(8,128)(2,1)S(1)}, u32[]{:S(2)}, u32[]{:S(2)}) collective-permute-start(bf16[64,6656]{1,0:T(8,128)(2,1)S(1)} %gather_grads.1.refs_0_), channel_id=1, source_target_pairs={{0,1},{1,0},{2,3},{3,2},{4,5},{5,4},{6,7},{7,6},{8,9},{9,8},{10,11... | collective-permute-start | bytes 2555912 | tf_op jit(solution)/shard_map/ppermute | solution.py:537

commit v3 on v1

--- a/solution.py
+++ b/solution.py
@@ -16,6 +16,7 @@
 VMEM_BYTES = 48 * 1024 * 1024
 VMEM_MOST = 60 * 1024 * 1024
 VMEM_HEADS = 57 * 1024 * 1024
+VMEM_RELAY = 59 * 1024 * 1024
 
 VM = pl.BlockSpec(memory_space=pltpu.VMEM)
 SM = pl.BlockSpec(memory_space=pltpu.SMEM)
@@ -113,7 +114,7 @@
         out_specs=[ANY, ANY],
         input_output_aliases={1: 1},
         scratch_shapes=[pltpu.VMEM(own.shape, own.dtype), pltpu.SemaphoreType.DMA((2,))],
-        compiler_params=params(),
+        compiler_params=params(VMEM_RELAY),
         cost_estimate=pl.CostEstimate(flops=0, bytes_accessed=4 * own.size, transcendentals=0),
         name="relay_block",
     )(own, got, after)
@@ -183,7 +184,7 @@
 
 
 def attention(
-    head, at, count, group, base, grad, up, blocks, with_ids, info, terms, before, tenants, rank
+    head, at, count, group, base, grad, up, blocks, with_ids, info, terms, before, after, tenants, rank
 ):
     rows, width = base.shape
     window = (REACH + 1) * rows
@@ -208,6 +209,8 @@
     if before is not None:
         operands += [before[1], before[0]]
         specs += [same(before[1]), ANY]
+    operands += after
+    specs += [ANY] * len(after)
     held = dict(
         kw=pltpu.VMEM((window, HEAD), jnp.bfloat16),
         vw=pltpu.VMEM((window, HEAD), jnp.bfloat16),
@@ -552,36 +555,34 @@
     group = base_queries.shape[1] // HEAD // key_heads
     per = key_heads // chunks
     counts = [1, per - 1, per] if chunks == 2 else [1] * per
-    state, pairs, held, with_ids, head = None, [], [], None, 0
+    state, pairs, held, with_ids, head, after = None, [], [], None, 0, []
     for i, count in enumerate(counts):
         chunk = head // per
         if len(held) < chunks and i < 2:
             two = shift_over(own[i], "seq")
-            passing, two = relay(own[i], two, terms[1] if i == 0 else state[1])
+            passing, two = relay(own[i], two, terms[1] if i == 0 else state[0])
             held.append((own[i], two, swap_over(two, "sub"), shift_over(passing, ("seq", "sub"))))
         with_ids = held[0]
+        if by_hand and i == 2:
+            shards = scatter(*[(keep, swap_over(send, "sub")) for keep, send in pairs])
+            pieces, after = exchange(shards), shards[:1]
         out, keep, send, gdown = attention(
             head, head % per, count, group, base_queries, output_gradient, up, held[chunk],
-            with_ids, info, terms, state, tenants, rank,
+            with_ids, info, terms, state, after, tenants, rank,
         )
         state = (out, gdown)
         pairs.append((keep, send))
         head += count
     if by_hand:
-        keep_late, send_late = pairs[-1]
+        early, gdown = add_up(pieces, through=[gdown])
         one, other = terms_over(gdown, "mp")
-        swapped = [(keep, swap_over(send, "sub")) for keep, send in pairs[:-1]]
-        pieces = exchange(scatter(*swapped, after=[keep_late]))
-        early = add_up(pieces)
+        all_early = spread(early)
         keep_a, send_a = small_call(
             functools.partial(split_kernel, tenants, rank), "split_grads", halves_of(tall, width),
-            one, other, info, normed_inputs, after=pieces[1:2],
+            one, other, info, normed_inputs, after=all_early[1:2],
         )
-        shards = scatter(
-            (keep_late, swap_over(send_late, "sub")), (keep_a, swap_over(send_a, "sub")), after=[early]
-        )
-        all_early = spread(early)
-        late = add_up(exchange(shards), after=all_early[1:])
+        shards = scatter((keep, swap_over(send, "sub")), (keep_a, swap_over(send_a, "sub")))
+        late = add_up(exchange(shards), after=all_early[2:])
         half = gather(all_early, spread(late))
         grad_b, grad_a = finish([(half, swap_over(half, "sub"))], up_width)
     else:

time: 123 us -> 125 us (1.016)
  starting transfers between devices: 48.4 us -> 38.1 us
  waiting for transfers between devices: 31.7 us -> 36.5 us
  local copies, waits for them, and re-layouts: 3.97 us -> 8.12 us
  Pallas kernels: 37.2 us -> 40 us
    ppermute x12, starting transfers between devices: 26 us -> 15.9 us  [rotate_over(): return lax.ppermute(block, axis, [(i, (i + d) % size) for i in range(size)])]
    unnamed x36, local copies, waits for them, and re-layouts: 3.97 us -> 8.12 us
    pallas_call x2, Pallas kernels: 0.21 us -> 3.35 us  [relay(): pl.pallas_call(relay_kernel, out_shape=[shape, shape], in_specs=[ANY, ANY...]
    ppermute x12, waiting for transfers between devices: 24.2 us -> 26.7 us  [rotate_over(): return lax.ppermute(block, axis, [(i, (i + d) % size) for i in range(size)])]
    ppermute x9, waiting for transfers between devices: 7.4 us -> 9.78 us  [swap_over(): return lax.ppermute(block, axis, [(0, 1), (1, 0)])]
  transfers between devices with their start and end apart: 25 -> 25, of which waited for: 9 -> 9; matrix products, arithmetic and copies ran while one was open for 0% -> 0% of each run, Pallas kernels for 26% -> 27%
where the time goes in v3:
time: 125 us; the launch traced here: 124 us
  Pallas kernels  40 us (32%)
  starting transfers between devices  38.1 us (30%)
  waiting for transfers between devices  36.5 us (29%)
  local copies, waits for them, and re-layouts  8.12 us (6%)
    pallas_call x3, Pallas kernels, attention(): pl.pallas_call(kernel, grid=(count,), out_shape=[jax.ShapeDtypeStruct((ro...  28.5 us
    ppermute x12, waiting for transfers between devices, rotate_over(): return lax.ppermute(block, axis, [(i, (i + d) % size) for i in range(size)])  26.7 us
    ppermute x12, starting transfers between devices, rotate_over(): return lax.ppermute(block, axis, [(i, (i + d) % size) for i in range(size)])  15.9 us
    ppermute x4, starting transfers between devices, shift_over(): return lax.ppermute(block, axis, [(i, i + 1) for i in range(size - 1)])  12.1 us
    ppermute x9, starting transfers between devices, swap_over(): return lax.ppermute(block, axis, [(0, 1), (1, 0)])  10.1 us
    ppermute x9, waiting for transfers between devices, swap_over(): return lax.ppermute(block, axis, [(0, 1), (1, 0)])  9.78 us
    unnamed x36, local copies, waits for them, and re-layouts  8.12 us
    pallas_call x2, Pallas kernels, relay(): pl.pallas_call(relay_kernel, out_shape=[shape, shape], in_specs=[ANY, ANY...  3.35 us
  transfers between devices with their start and end apart: 25, of which 9 were waited for; matrix products, arithmetic and copies ran while one was open for 0% of the time, Pallas kernels for 27%

profile of v3, /device:TPU:0, one launch (start us, length us, event | category | flops | bytes accessed | tf_op | source)
XLA Modules:
  0.0 123.6 jit_solution(5085745031826198897)
XLA Ops:
  0.6 1.9 %pack_keys_values.1 = (bf16[272,512]{1,0:T(8,128)(2,1)}, bf16[272,512]{1,0:T(8,128)(2,1)}) custom-call(bf16[256,512]{1,0:T(8,128)(2,1)} %keys.1, bf16[256,512]{1,0:T(8,128)(2,1)} %values.1, s32[1,256]{1,0:T(1,128)} %bitcast.13), custom_call_target="tpu_custom_call" | custom-call | bytes 1048576 | tf_op jit(solution)/shard_map/pack_keys_values/pallas_call | solution.py:71
  2.5 5.1 %collective-permute-start.1 = (bf16[272,512]{1,0:T(8,128)(2,1)}, bf16[272,512]{1,0:T(8,128)(2,1)S(1)}, u32[]{:S(2)}, u32[]{:S(2)}) collective-permute-start(bf16[272,512]{1,0:T(8,128)(2,1)} %get-tuple-element.36.own.refs_3_.refs_4_.refs_11_), channel_id=1, source_target_pairs={{0,4},{4,8},{8,12},{1,5},{5,9},{9,13},{2,6},{6,10},{10,14},{3,7},{... | collective-permute-start | bytes 835592 | tf_op jit(solution)/shard_map/ppermute | solution.py:534
  7.6 3.3 %down_project.1.refs_15_.refs_16_.refs_2_ = f32[24,256]{1,0:T(8,128)} custom-call(bf16[256,2560]{1,0:T(8,128)(2,1)} %refs_3_.1, bf16[128,2560]{1,0:T(8,128)(2,1)} %bitcast.12, s32[1,256]{1,0:T(1,128)} %bitcast.14, s32[16]{0:T(128)} %tenant_of.1), custom_call_target="tpu_custom_call" | custom-call | flops 167772160 | bytes 1966080 | tf_op jit(solution)/shard_map/down_project/pallas_call | solution.py:157
  11.0 1.6 %collective-permute-start.2 = (f32[24,256]{1,0:T(8,128)}, f32[24,256]{1,0:T(8,128)S(1)}, u32[]{:S(2)}, u32[]{:S(2)}) collective-permute-start(f32[24,256]{1,0:T(8,128)} %down_project.1.refs_15_.refs_16_.refs_2_), channel_id=1, source_target_pairs={{0,2},{2,0},{1,3},{3,1},{4,6},{6,4},{5,7},{7,5},{8,10},{10,8},{9,1... | collective-permute-start | bytes 73736 | tf_op jit(solution)/shard_map/ppermute | solution.py:518
  12.5 2.5 %collective-permute-done.2.after.refs_17_ = f32[24,256]{1,0:T(8,128)S(1)} collective-permute-done((f32[24,256]{1,0:T(8,128)}, f32[24,256]{1,0:T(8,128)S(1)}, u32[]{:S(2)}, u32[]{:S(2)}) %collective-permute-start.2) | collective-permute-done | bytes 24608 | tf_op jit(solution)/shard_map/ppermute | solution.py:518
  15.1 0.6 copy-done.15
  15.7 0.7 copy-done.10
  16.4 1.7 %relay_block.2 = (bf16[272,512]{1,0:T(8,128)(2,1)}, bf16[272,512]{1,0:T(8,128)(2,1)}) custom-call(bf16[272,512]{1,0:T(8,128)(2,1)} %get-tuple-element.36.own.refs_3_.refs_4_.refs_11_, bf16[272,512]{1,0:T(8,128)(2,1)} %copy-done.10, f32[24,256]{1,0:T(8,128)} %copy-done.15), custom_call_target="tpu_custom_call", output_to_operand_aliasing={{1}: (1, {})} | custom-call | bytes 557056 | tf_op jit(solution)/shard_map/relay_block/pallas_call | solution.py:110
  18.1 1.3 %collective-permute-start.4 = (bf16[272,512]{1,0:T(8,128)(2,1)}, bf16[272,512]{1,0:T(8,128)(2,1)S(1)}, u32[]{:S(2)}, u32[]{:S(2)}) collective-permute-start(bf16[272,512]{1,0:T(8,128)(2,1)} %get-tuple-element.38), channel_id=1, source_target_pairs={{0,1},{1,4},{4,5},{5,8},{8,9},{9,12},{12,13},{2,3},{3,6},{6,7},{7,... | collective-permute-start | bytes 835592 | tf_op jit(solution)/shard_map/ppermute | solution.py:534
  19.4 2.4 %collective-permute-start.3 = (bf16[272,512]{1,0:T(8,128)(2,1)}, bf16[272,512]{1,0:T(8,128)(2,1)S(1)}, u32[]{:S(2)}, u32[]{:S(2)}) collective-permute-start(bf16[272,512]{1,0:T(8,128)(2,1)} %get-tuple-element.37.refs_5_.refs_6_.refs_12_), channel_id=1, source_target_pairs={{0,1},{1,0},{2,3},{3,2},{4,5},{5,4},{6,7},{7,6},{8,9},{9,8},{10,11... | collective-permute-start | bytes 835592 | tf_op jit(solution)/shard_map/ppermute | solution.py:518
  21.7 3.5 %collective-permute-start = (bf16[272,512]{1,0:T(8,128)(2,1)S(1)}, bf16[272,512]{1,0:T(8,128)(2,1)S(1)}, u32[]{:S(2)}, u32[]{:S(2)}) collective-permute-start(bf16[272,512]{1,0:T(8,128)(2,1)S(1)} %copy-done.13), channel_id=1, source_target_pairs={{0,4},{4,8},{8,12},{1,5},{5,9},{9,13},{2,6},{6,10},{10,14},{3,7},{... | collective-permute-start | bytes 835592 | tf_op jit(solution)/shard_map/ppermute | solution.py:534
  25.3 0.7 copy-done.11
  26.0 7.5 %attention.3 = (bf16[256,4096]{1,0:T(8,128)(2,1)}, bf16[64,1024]{1,0:T(8,128)(2,1)}, bf16[64,1024]{1,0:T(8,128)(2,1)}, f32[16,256]{1,0:T(8,128)}) custom-call(bf16[256,4096]{1,0:T(8,128)(2,1)} %refs_0_.5, bf16[256,4096]{1,0:T(8,128)(2,1)} %refs_1_.5, bf16[128,4096]{1,0:T(8,128)(2,1)} %bitcast.9, ...), custom_call_target="tpu_custom_call" | custom-call | flops 2147483648 | bytes 1572864 | tf_op jit(solution)/shard_map/attention/pallas_call | solution.py:348
  33.8 0.7 copy-done.14
  34.5 1.7 %relay_block.3 = (bf16[272,512]{1,0:T(8,128)(2,1)}, bf16[272,512]{1,0:T(8,128)(2,1)}) custom-call(bf16[272,512]{1,0:T(8,128)(2,1)} %get-tuple-element.35.own.refs_3_.refs_4_, bf16[272,512]{1,0:T(8,128)(2,1)} %copy-done.14, bf16[256,4096]{1,0:T(8,128)(2,1)} %get-tuple-element.39.after.refs_19_), custom_call_target="tpu_custom_call", output_to_operand_aliasing={{1}: (1, {})} | custom-call | bytes 557056 | tf_op jit(solution)/shard_map/relay_block/pallas_call | solution.py:110
  36.2 2.2 %collective-permute-start.6 = (bf16[272,512]{1,0:T(8,128)(2,1)}, bf16[272,512]{1,0:T(8,128)(2,1)S(1)}, u32[]{:S(2)}, u32[]{:S(2)}) collective-permute-start(bf16[272,512]{1,0:T(8,128)(2,1)} %get-tuple-element.41), channel_id=1, source_target_pairs={{0,1},{1,4},{4,5},{5,8},{8,9},{9,12},{12,13},{2,3},{3,6},{6,7},{7,... | collective-permute-start | bytes 835592 | tf_op jit(solution)/shard_map/ppermute | solution.py:534
  38.4 3.8 %collective-permute-start.5 = (bf16[272,512]{1,0:T(8,128)(2,1)}, bf16[272,512]{1,0:T(8,128)(2,1)S(1)}, u32[]{:S(2)}, u32[]{:S(2)}) collective-permute-start(bf16[272,512]{1,0:T(8,128)(2,1)} %get-tuple-element.40.refs_5_.refs_6_), channel_id=1, source_target_pairs={{0,1},{1,0},{2,3},{3,2},{4,5},{5,4},{6,7},{7,6},{8,9},{9,8},{10,11... | collective-permute-start | bytes 835592 | tf_op jit(solution)/shard_map/ppermute | solution.py:518
  42.2 7.7 %attention.4 = (bf16[256,4096]{1,0:T(8,128)(2,1)}, bf16[64,1024]{1,0:T(8,128)(2,1)}, bf16[64,1024]{1,0:T(8,128)(2,1)}, f32[16,256]{1,0:T(8,128)}) custom-call(bf16[256,4096]{1,0:T(8,128)(2,1)} %refs_0_.5, bf16[256,4096]{1,0:T(8,128)(2,1)} %refs_1_.5, bf16[128,4096]{1,0:T(8,128)(2,1)} %bitcast.10, ...), custom_call_target="tpu_custom_call", output_to_operand_aliasing={{0}: (19, {})} | custom-call | flops 2147483648 | bytes 1572864 | tf_op jit(solution)/shard_map/attention/pallas_call | solution.py:348
  50.0 1.5 %collective-permute-done.8.refs_3_ = bf16[64,1024]{1,0:T(8,128)(2,1)S(1)} collective-permute-done((bf16[64,1024]{1,0:T(8,128)(2,1)}, bf16[64,1024]{1,0:T(8,128)(2,1)S(1)}, u32[]{:S(2)}, u32[]{:S(2)}) %collective-permute-start.8) | collective-permute-done | bytes 131104 | tf_op jit(solution)/shard_map/ppermute | solution.py:518
  51.5 0.9 copy-done.4
  52.5 0.6 copy-done.8
  53.1 2.2 %collective-permute-start.9 = (bf16[16,2048]{1,0:T(8,128)(2,1)S(1)}, bf16[16,2048]{1,0:T(8,128)(2,1)S(1)}, u32[]{:S(2)}, u32[]{:S(2)}) collective-permute-start(bf16[16,2048]{1,0:T(8,128)(2,1)S(1)} %get-tuple-element.51), channel_id=1, source_target_pairs={{0,4},{4,8},{8,12},{12,0},{1,5},{5,9},{9,13},{13,1},{2,6},{6,10},{... | collective-permute-start | bytes 196616 | tf_op jit(solution)/shard_map/ppermute | solution.py:523
  55.4 2.4 %collective-permute-start.11 = (bf16[16,2048]{1,0:T(8,128)(2,1)S(1)}, bf16[16,2048]{1,0:T(8,128)(2,1)S(1)}, u32[]{:S(2)}, u32[]{:S(2)}) collective-permute-start(bf16[16,2048]{1,0:T(8,128)(2,1)S(1)} %get-tuple-element.53), channel_id=1, source_target_pairs={{0,12},{4,0},{8,4},{12,8},{1,13},{5,1},{9,5},{13,9},{2,14},{6,2},{... | collective-permute-start | bytes 196616 | tf_op jit(solution)/shard_map/ppermute | solution.py:523
  57.8 0.7 copy-done.16
  58.6 13.3 %attention.5 = (bf16[256,4096]{1,0:T(8,128)(2,1)}, bf16[64,2048]{1,0:T(8,128)(2,1)}, bf16[64,2048]{1,0:T(8,128)(2,1)}, f32[16,256]{1,0:T(8,128)}) custom-call(bf16[256,4096]{1,0:T(8,128)(2,1)} %refs_0_.5, bf16[256,4096]{1,0:T(8,128)(2,1)} %refs_1_.5, bf16[128,4096]{1,0:T(8,128)(2,1)} %bitcast.11, ...), custom_call_target="tpu_custom_call", output_to_operand_aliasing={{0}: (19, {})} | custom-call | flops 4294967296 | bytes 3145728 | tf_op jit(solution)/shard_map/attention/pallas_call | solution.py:348
  71.9 0.7 copy-done.5
  72.7 3.3 %collective-permute-start.12 = (bf16[16,2048]{1,0:T(8,128)(2,1)S(1)}, bf16[16,2048]{1,0:T(8,128)(2,1)S(1)}, u32[]{:S(2)}, u32[]{:S(2)}) collective-permute-start(bf16[16,2048]{1,0:T(8,128)(2,1)S(1)} %get-tuple-element.55.refs_0_), channel_id=1, source_target_pairs={{0,4},{4,8},{8,12},{12,0},{1,5},{5,9},{9,13},{13,1},{2,6},{6,10},{... | collective-permute-start | bytes 196616 | tf_op jit(solution)/shard_map/ppermute | solution.py:523
  75.9 1.5 %collective-permute-start.16 = (f32[16,256]{1,0:T(8,128)S(1)}, f32[16,256]{1,0:T(8,128)S(1)}, u32[]{:S(2)}, u32[]{:S(2)}) collective-permute-start(f32[16,256]{1,0:T(8,128)S(1)} %get-tuple-element.58.refs_0_), channel_id=1, source_target_pairs={{0,2},{2,0},{1,3},{3,1},{4,6},{6,4},{5,7},{7,5},{8,10},{10,8},{9,1... | collective-permute-start | bytes 49160 | tf_op jit(solution)/shard_map/ppermute | solution.py:518
  77.4 0.6 copy-done.6
  78.0 1.6 %collective-permute-done.16.refs_1_ = f32[16,256]{1,0:T(8,128)S(1)} collective-permute-done((f32[16,256]{1,0:T(8,128)S(1)}, f32[16,256]{1,0:T(8,128)S(1)}, u32[]{:S(2)}, u32[]{:S(2)}) %collective-permute-start.16) | collective-permute-done | bytes 16416 | tf_op jit(solution)/shard_map/ppermute | solution.py:518
  79.7 0.7 copy-done.7
  80.4 0.4 split_grads.1
  80.9 0.5 collective-permute-start.15
  81.4 1.7 %collective-permute-done.15.refs_1_ = bf16[64,2048]{1,0:T(8,128)(2,1)S(1)} collective-permute-done((bf16[64,2048]{1,0:T(8,128)(2,1)}, bf16[64,2048]{1,0:T(8,128)(2,1)S(1)}, u32[]{:S(2)}, u32[]{:S(2)}) %collective-permute-start.15) | collective-permute-done | bytes 262176 | tf_op jit(solution)/shard_map/ppermute | solution.py:518
  83.1 0.9 copy-done.2
  84.3 0.6 collective-permute-start.18
  84.9 0.7 collective-permute-start.19
  85.6 2.7 %collective-permute-start.20 = (bf16[16,4608]{1,0:T(8,128)(2,1)S(1)}, bf16[16,4608]{1,0:T(8,128)(2,1)S(1)}, u32[]{:S(2)}, u32[]{:S(2)}) collective-permute-start(bf16[16,4608]{1,0:T(8,128)(2,1)S(1)} %get-tuple-element.64), channel_id=1, source_target_pairs={{0,12},{4,0},{8,4},{12,8},{1,13},{5,1},{9,5},{13,9},{2,14},{6,2},{... | collective-permute-start | bytes 442376 | tf_op jit(solution)/shard_map/ppermute | solution.py:523
  88.2 1.1 collective-permute-start.14
  89.3 1.0 collective-permute-start.13
  90.3 8.9 %collective-permute-done.14.refs_5_.refs_3_ = bf16[16,2048]{1,0:T(8,128)(2,1)S(1)} collective-permute-done((bf16[16,2048]{1,0:T(8,128)(2,1)S(1)}, bf16[16,2048]{1,0:T(8,128)(2,1)S(1)}, u32[]{:S(2)}, u32[]{:S(2)}) %collective-permute-start.14) | collective-permute-done | bytes 65568 | tf_op jit(solution)/shard_map/ppermute | solution.py:523
  99.2 6.0 %collective-permute-done.13.refs_4_.refs_2_ = bf16[16,2048]{1,0:T(8,128)(2,1)S(1)} collective-permute-done((bf16[16,2048]{1,0:T(8,128)(2,1)S(1)}, bf16[16,2048]{1,0:T(8,128)(2,1)S(1)}, u32[]{:S(2)}, u32[]{:S(2)}) %collective-permute-start.13) | collective-permute-done | bytes 65568 | tf_op jit(solution)/shard_map/ppermute | solution.py:523
  105.4 1.2 collective-permute-start.22
  106.7 0.7 collective-permute-start.21
  107.3 3.6 %collective-permute-done.23.refs_7_ = bf16[16,4608]{1,0:T(8,128)(2,1)S(1)} collective-permute-done((bf16[16,4608]{1,0:T(8,128)(2,1)S(1)}, bf16[16,4608]{1,0:T(8,128)(2,1)S(1)}, u32[]{:S(2)}, u32[]{:S(2)}) %collective-permute-start.23) | collective-permute-done | bytes 147488 | tf_op jit(solution)/shard_map/ppermute | solution.py:523
  110.9 8.2 %collective-permute-done.22.refs_6_ = bf16[16,4608]{1,0:T(8,128)(2,1)S(1)} collective-permute-done((bf16[16,4608]{1,0:T(8,128)(2,1)S(1)}, bf16[16,4608]{1,0:T(8,128)(2,1)S(1)}, u32[]{:S(2)}, u32[]{:S(2)}) %collective-permute-start.22) | collective-permute-done | bytes 147488 | tf_op jit(solution)/shard_map/ppermute | solution.py:523
  119.3 2.4 %collective-permute-done.24.refs_1_ = bf16[64,6656]{1,0:T(8,128)(2,1)S(1)} collective-permute-done((bf16[64,6656]{1,0:T(8,128)(2,1)S(1)}, bf16[64,6656]{1,0:T(8,128)(2,1)S(1)}, u32[]{:S(2)}, u32[]{:S(2)}) %collective-permute-start.24) | collective-permute-done | bytes 852000 | tf_op jit(solution)/shard_map/ppermute | solution.py:518
  121.6 1.9 %finish_grads.1 = (f32[128,4096]{1,0:T(8,128)}, f32[128,2560]{1,0:T(8,128)}) custom-call(bf16[64,6656]{1,0:T(8,128)(2,1)S(1)} %gather_grads.1.refs_0_, bf16[64,6656]{1,0:T(8,128)(2,1)S(1)} %collective-permute-done.24.refs_1_), custom_call_target="tpu_custom_call" | custom-call | flops 1703936 | bytes 3407872 | tf_op jit(solution)/shard_map/finish_grads/pallas_call | solution.py:375
  (52 shorter events, 1.4 us)
Async XLA Ops:
  2.5 19.2 %copy-start.13 = (bf16[272,512]{1,0:T(8,128)(2,1)S(1)}, bf16[272,512]{1,0:T(8,128)(2,1)}, u32[]{:S(2)}) copy-start(bf16[272,512]{1,0:T(8,128)(2,1)} %get-tuple-element.35.own.refs_3_.refs_4_) | copy-start | bytes 835588
  2.5 12.5 %collective-permute-start.1 = (bf16[272,512]{1,0:T(8,128)(2,1)}, bf16[272,512]{1,0:T(8,128)(2,1)S(1)}, u32[]{:S(2)}, u32[]{:S(2)}) collective-permute-start(bf16[272,512]{1,0:T(8,128)(2,1)} %get-tuple-element.36.own.refs_3_.refs_4_.refs_11_), channel_id=1, source_target_pairs={{0,4},{4,8},{8,12},{1,5},{5,9},{9,13},{2,6},{6,10},{10,14},{3,7},{... | collective-permute-start | bytes 835592 | tf_op jit(solution)/shard_map/ppermute | solution.py:534
  11.0 4.1 %collective-permute-start.2 = (f32[24,256]{1,0:T(8,128)}, f32[24,256]{1,0:T(8,128)S(1)}, u32[]{:S(2)}, u32[]{:S(2)}) collective-permute-start(f32[24,256]{1,0:T(8,128)} %down_project.1.refs_15_.refs_16_.refs_2_), channel_id=1, source_target_pairs={{0,2},{2,0},{1,3},{3,1},{4,6},{6,4},{5,7},{7,5},{8,10},{10,8},{9,1... | collective-permute-start | bytes 73736 | tf_op jit(solution)/shard_map/ppermute | solution.py:518
  15.1 0.6 copy-start.15
  15.7 0.7 copy-start.10
  18.1 7.2 %collective-permute-start.4 = (bf16[272,512]{1,0:T(8,128)(2,1)}, bf16[272,512]{1,0:T(8,128)(2,1)S(1)}, u32[]{:S(2)}, u32[]{:S(2)}) collective-permute-start(bf16[272,512]{1,0:T(8,128)(2,1)} %get-tuple-element.38), channel_id=1, source_target_pairs={{0,1},{1,4},{4,5},{5,8},{8,9},{9,12},{12,13},{2,3},{3,6},{6,7},{7,... | collective-permute-start | bytes 835592 | tf_op jit(solution)/shard_map/ppermute | solution.py:534
  19.4 5.9 %collective-permute-start.3 = (bf16[272,512]{1,0:T(8,128)(2,1)}, bf16[272,512]{1,0:T(8,128)(2,1)S(1)}, u32[]{:S(2)}, u32[]{:S(2)}) collective-permute-start(bf16[272,512]{1,0:T(8,128)(2,1)} %get-tuple-element.37.refs_5_.refs_6_.refs_12_), channel_id=1, source_target_pairs={{0,1},{1,0},{2,3},{3,2},{4,5},{5,4},{6,7},{7,6},{8,9},{9,8},{10,11... | collective-permute-start | bytes 835592 | tf_op jit(solution)/shard_map/ppermute | solution.py:518
  21.7 12.0 %collective-permute-start = (bf16[272,512]{1,0:T(8,128)(2,1)S(1)}, bf16[272,512]{1,0:T(8,128)(2,1)S(1)}, u32[]{:S(2)}, u32[]{:S(2)}) collective-permute-start(bf16[272,512]{1,0:T(8,128)(2,1)S(1)} %copy-done.13), channel_id=1, source_target_pairs={{0,4},{4,8},{8,12},{1,5},{5,9},{9,13},{2,6},{6,10},{10,14},{3,7},{... | collective-permute-start | bytes 835592 | tf_op jit(solution)/shard_map/ppermute | solution.py:534
  25.2 0.7 copy-start.11
  25.2 0.8 copy-start.12
  33.5 16.4 %collective-permute-start.7 = (bf16[64,1024]{1,0:T(8,128)(2,1)}, bf16[64,1024]{1,0:T(8,128)(2,1)S(1)}, u32[]{:S(2)}, u32[]{:S(2)}) collective-permute-start(bf16[64,1024]{1,0:T(8,128)(2,1)} %get-tuple-element.46), channel_id=1, source_target_pairs={{0,1},{1,0},{2,3},{3,2},{4,5},{5,4},{6,7},{7,6},{8,9},{9,8},{10,11... | collective-permute-start | bytes 393224 | tf_op jit(solution)/shard_map/ppermute | solution.py:518
  33.8 0.7 copy-start.14
  36.2 21.6 %collective-permute-start.6 = (bf16[272,512]{1,0:T(8,128)(2,1)}, bf16[272,512]{1,0:T(8,128)(2,1)S(1)}, u32[]{:S(2)}, u32[]{:S(2)}) collective-permute-start(bf16[272,512]{1,0:T(8,128)(2,1)} %get-tuple-element.41), channel_id=1, source_target_pairs={{0,1},{1,4},{4,5},{5,8},{8,9},{9,12},{12,13},{2,3},{3,6},{6,7},{7,... | collective-permute-start | bytes 835592 | tf_op jit(solution)/shard_map/ppermute | solution.py:534
  38.4 19.4 %collective-permute-start.5 = (bf16[272,512]{1,0:T(8,128)(2,1)}, bf16[272,512]{1,0:T(8,128)(2,1)S(1)}, u32[]{:S(2)}, u32[]{:S(2)}) collective-permute-start(bf16[272,512]{1,0:T(8,128)(2,1)} %get-tuple-element.40.refs_5_.refs_6_), channel_id=1, source_target_pairs={{0,1},{1,0},{2,3},{3,2},{4,5},{5,4},{6,7},{7,6},{8,9},{9,8},{10,11... | collective-permute-start | bytes 835592 | tf_op jit(solution)/shard_map/ppermute | solution.py:518
  42.2 9.3 %copy-start.3 = (bf16[64,1024]{1,0:T(8,128)(2,1)S(1)}, bf16[64,1024]{1,0:T(8,128)(2,1)}, u32[]{:S(2)}) copy-start(bf16[64,1024]{1,0:T(8,128)(2,1)} %get-tuple-element.45.refs_0_) | copy-start | bytes 393220
  49.9 1.6 %collective-permute-start.8 = (bf16[64,1024]{1,0:T(8,128)(2,1)}, bf16[64,1024]{1,0:T(8,128)(2,1)S(1)}, u32[]{:S(2)}, u32[]{:S(2)}) collective-permute-start(bf16[64,1024]{1,0:T(8,128)(2,1)} %get-tuple-element.48), channel_id=1, source_target_pairs={{0,1},{1,0},{2,3},{3,2},{4,5},{5,4},{6,7},{7,6},{8,9},{9,8},{10,11... | collective-permute-start | bytes 393224 | tf_op jit(solution)/shard_map/ppermute | solution.py:518
  51.5 0.9 copy-start.4
  52.5 0.6 copy-start.8
  53.1 18.7 %collective-permute-start.9 = (bf16[16,2048]{1,0:T(8,128)(2,1)S(1)}, bf16[16,2048]{1,0:T(8,128)(2,1)S(1)}, u32[]{:S(2)}, u32[]{:S(2)}) collective-permute-start(bf16[16,2048]{1,0:T(8,128)(2,1)S(1)} %get-tuple-element.51), channel_id=1, source_target_pairs={{0,4},{4,8},{8,12},{12,0},{1,5},{5,9},{9,13},{13,1},{2,6},{6,10},{... | collective-permute-start | bytes 196616 | tf_op jit(solution)/shard_map/ppermute | solution.py:523
  55.4 16.5 %collective-permute-start.10 = (bf16[16,2048]{1,0:T(8,128)(2,1)S(1)}, bf16[16,2048]{1,0:T(8,128)(2,1)S(1)}, u32[]{:S(2)}, u32[]{:S(2)}) collective-permute-start(bf16[16,2048]{1,0:T(8,128)(2,1)S(1)} %get-tuple-element.52), channel_id=1, source_target_pairs={{0,8},{4,12},{8,0},{12,4},{1,9},{5,13},{9,1},{13,5},{2,10},{6,14},... | collective-permute-start | bytes 196616 | tf_op jit(solution)/shard_map/ppermute | solution.py:523
  55.4 16.5 %collective-permute-start.11 = (bf16[16,2048]{1,0:T(8,128)(2,1)S(1)}, bf16[16,2048]{1,0:T(8,128)(2,1)S(1)}, u32[]{:S(2)}, u32[]{:S(2)}) collective-permute-start(bf16[16,2048]{1,0:T(8,128)(2,1)S(1)} %get-tuple-element.53), channel_id=1, source_target_pairs={{0,12},{4,0},{8,4},{12,8},{1,13},{5,1},{9,5},{13,9},{2,14},{6,2},{... | collective-permute-start | bytes 196616 | tf_op jit(solution)/shard_map/ppermute | solution.py:523
  57.7 0.7 copy-start.16
  57.7 0.8 copy-start.17
  58.6 13.3 %copy-start.9 = (bf16[16,2048]{1,0:T(8,128)(2,1)S(1)}, bf16[16,2048]{1,0:T(8,128)(2,1)}, u32[]{:S(2)}) copy-start(bf16[16,2048]{1,0:T(8,128)(2,1)} %copy-done.8) | copy-start | bytes 196612
  58.6 21.1 %copy-start = (bf16[256,2560]{1,0:T(8,128)(2,1)S(1)}, bf16[256,2560]{1,0:T(8,128)(2,1)}, u32[]{:S(2)}) copy-start(bf16[256,2560]{1,0:T(8,128)(2,1)} %refs_3_.1) | copy-start | bytes 3932164
  58.6 21.1 %copy-start.1 = (f32[24,256]{1,0:T(8,128)S(1)}, f32[24,256]{1,0:T(8,128)}, u32[]{:S(2)}) copy-start(f32[24,256]{1,0:T(8,128)} %down_project.1.refs_15_.refs_16_.refs_2_) | copy-start | bytes 73732
  71.9 0.7 copy-start.5
  72.7 7.0 %collective-permute-start.12 = (bf16[16,2048]{1,0:T(8,128)(2,1)S(1)}, bf16[16,2048]{1,0:T(8,128)(2,1)S(1)}, u32[]{:S(2)}, u32[]{:S(2)}) collective-permute-start(bf16[16,2048]{1,0:T(8,128)(2,1)S(1)} %get-tuple-element.55.refs_0_), channel_id=1, source_target_pairs={{0,4},{4,8},{8,12},{12,0},{1,5},{5,9},{9,13},{13,1},{2,6},{6,10},{... | collective-permute-start | bytes 196616 | tf_op jit(solution)/shard_map/ppermute | solution.py:523
  75.9 3.7 %collective-permute-start.16 = (f32[16,256]{1,0:T(8,128)S(1)}, f32[16,256]{1,0:T(8,128)S(1)}, u32[]{:S(2)}, u32[]{:S(2)}) collective-permute-start(f32[16,256]{1,0:T(8,128)S(1)} %get-tuple-element.58.refs_0_), channel_id=1, source_target_pairs={{0,2},{2,0},{1,3},{3,1},{4,6},{6,4},{5,7},{7,5},{8,10},{10,8},{9,1... | collective-permute-start | bytes 49160 | tf_op jit(solution)/shard_map/ppermute | solution.py:518
  77.4 0.6 copy-start.6
  79.7 0.7 copy-start.7
  80.8 2.3 %collective-permute-start.17 = (bf16[64,2560]{1,0:T(8,128)(2,1)S(1)}, bf16[64,2560]{1,0:T(8,128)(2,1)S(1)}, u32[]{:S(2)}, u32[]{:S(2)}) collective-permute-start(bf16[64,2560]{1,0:T(8,128)(2,1)S(1)} %get-tuple-element.60), channel_id=1, source_target_pairs={{0,1},{1,0},{2,3},{3,2},{4,5},{5,4},{6,7},{7,6},{8,9},{9,8},{10,11... | collective-permute-start | bytes 983048 | tf_op jit(solution)/shard_map/ppermute | solution.py:518
  80.9 2.2 %collective-permute-start.15 = (bf16[64,2048]{1,0:T(8,128)(2,1)}, bf16[64,2048]{1,0:T(8,128)(2,1)S(1)}, u32[]{:S(2)}, u32[]{:S(2)}) collective-permute-start(bf16[64,2048]{1,0:T(8,128)(2,1)} %get-tuple-element.57), channel_id=1, source_target_pairs={{0,1},{1,0},{2,3},{3,2},{4,5},{5,4},{6,7},{7,6},{8,9},{9,8},{10,11... | collective-permute-start | bytes 786440 | tf_op jit(solution)/shard_map/ppermute | solution.py:518
  83.1 1.0 copy-start.2
  84.3 20.8 %collective-permute-start.18 = (bf16[16,4608]{1,0:T(8,128)(2,1)S(1)}, bf16[16,4608]{1,0:T(8,128)(2,1)S(1)}, u32[]{:S(2)}, u32[]{:S(2)}) collective-permute-start(bf16[16,4608]{1,0:T(8,128)(2,1)S(1)} %get-tuple-element.62), channel_id=1, source_target_pairs={{0,4},{4,8},{8,12},{12,0},{1,5},{5,9},{9,13},{13,1},{2,6},{6,10},{... | collective-permute-start | bytes 442376 | tf_op jit(solution)/shard_map/ppermute | solution.py:523
  84.9 20.3 %collective-permute-start.19 = (bf16[16,4608]{1,0:T(8,128)(2,1)S(1)}, bf16[16,4608]{1,0:T(8,128)(2,1)S(1)}, u32[]{:S(2)}, u32[]{:S(2)}) collective-permute-start(bf16[16,4608]{1,0:T(8,128)(2,1)S(1)} %get-tuple-element.63), channel_id=1, source_target_pairs={{0,8},{4,12},{8,0},{12,4},{1,9},{5,13},{9,1},{13,5},{2,10},{6,14},... | collective-permute-start | bytes 442376 | tf_op jit(solution)/shard_map/ppermute | solution.py:523
  85.6 19.6 %collective-permute-start.20 = (bf16[16,4608]{1,0:T(8,128)(2,1)S(1)}, bf16[16,4608]{1,0:T(8,128)(2,1)S(1)}, u32[]{:S(2)}, u32[]{:S(2)}) collective-permute-start(bf16[16,4608]{1,0:T(8,128)(2,1)S(1)} %get-tuple-element.64), channel_id=1, source_target_pairs={{0,12},{4,0},{8,4},{12,8},{1,13},{5,1},{9,5},{13,9},{2,14},{6,2},{... | collective-permute-start | bytes 442376 | tf_op jit(solution)/shard_map/ppermute | solution.py:523
  88.2 10.9 %collective-permute-start.14 = (bf16[16,2048]{1,0:T(8,128)(2,1)S(1)}, bf16[16,2048]{1,0:T(8,128)(2,1)S(1)}, u32[]{:S(2)}, u32[]{:S(2)}) collective-permute-start(bf16[16,2048]{1,0:T(8,128)(2,1)S(1)} %get-tuple-element.55.refs_0_), channel_id=1, source_target_pairs={{0,12},{4,0},{8,4},{12,8},{1,13},{5,1},{9,5},{13,9},{2,14},{6,2},{... | collective-permute-start | bytes 196616 | tf_op jit(solution)/shard_map/ppermute | solution.py:523
  89.3 15.9 %collective-permute-start.13 = (bf16[16,2048]{1,0:T(8,128)(2,1)S(1)}, bf16[16,2048]{1,0:T(8,128)(2,1)S(1)}, u32[]{:S(2)}, u32[]{:S(2)}) collective-permute-start(bf16[16,2048]{1,0:T(8,128)(2,1)S(1)} %get-tuple-element.55.refs_0_), channel_id=1, source_target_pairs={{0,8},{4,12},{8,0},{12,4},{1,9},{5,13},{9,1},{13,5},{2,10},{6,14},... | collective-permute-start | bytes 196616 | tf_op jit(solution)/shard_map/ppermute | solution.py:523
  105.3 5.7 %collective-permute-start.23 = (bf16[16,4608]{1,0:T(8,128)(2,1)S(1)}, bf16[16,4608]{1,0:T(8,128)(2,1)S(1)}, u32[]{:S(2)}, u32[]{:S(2)}) collective-permute-start(bf16[16,4608]{1,0:T(8,128)(2,1)S(1)} %sum_grads.3.refs_4_), channel_id=1, source_target_pairs={{0,12},{4,0},{8,4},{12,8},{1,13},{5,1},{9,5},{13,9},{2,14},{6,2},{... | collective-permute-start | bytes 442376 | tf_op jit(solution)/shard_map/ppermute | solution.py:523
  105.4 13.7 %collective-permute-start.22 = (bf16[16,4608]{1,0:T(8,128)(2,1)S(1)}, bf16[16,4608]{1,0:T(8,128)(2,1)S(1)}, u32[]{:S(2)}, u32[]{:S(2)}) collective-permute-start(bf16[16,4608]{1,0:T(8,128)(2,1)S(1)} %sum_grads.3.refs_4_), channel_id=1, source_target_pairs={{0,8},{4,12},{8,0},{12,4},{1,9},{5,13},{9,1},{13,5},{2,10},{6,14},... | collective-permute-start | bytes 442376 | tf_op jit(solution)/shard_map/ppermute | solution.py:523
  106.7 12.5 %collective-permute-start.21 = (bf16[16,4608]{1,0:T(8,128)(2,1)S(1)}, bf16[16,4608]{1,0:T(8,128)(2,1)S(1)}, u32[]{:S(2)}, u32[]{:S(2)}) collective-permute-start(bf16[16,4608]{1,0:T(8,128)(2,1)S(1)} %sum_grads.3.refs_4_), channel_id=1, source_target_pairs={{0,4},{4,8},{8,12},{12,0},{1,5},{5,9},{9,13},{13,1},{2,6},{6,10},{... | collective-permute-start | bytes 442376 | tf_op jit(solution)/shard_map/ppermute | solution.py:523
  119.2 2.4 %collective-permute-start.24 = (bf16[64,6656]{1,0:T(8,128)(2,1)S(1)}, bf16[64,6656]{1,0:T(8,128)(2,1)S(1)}, u32[]{:S(2)}, u32[]{:S(2)}) collective-permute-start(bf16[64,6656]{1,0:T(8,128)(2,1)S(1)} %gather_grads.1.refs_0_), channel_id=1, source_target_pairs={{0,1},{1,0},{2,3},{3,2},{4,5},{5,4},{6,7},{7,6},{8,9},{9,8},{10,11... | collective-permute-start | bytes 2555912 | tf_op jit(solution)/shard_map/ppermute | solution.py:518

commit v4 on v1

--- a/solution.py
+++ b/solution.py
@@ -15,7 +15,7 @@
 TAIL = 16
 VMEM_BYTES = 48 * 1024 * 1024
 VMEM_MOST = 60 * 1024 * 1024
-VMEM_HEADS = 57 * 1024 * 1024
+VMEM_HEADS = 48 * 1024 * 1024
 
 VM = pl.BlockSpec(memory_space=pltpu.VMEM)
 SM = pl.BlockSpec(memory_space=pltpu.SMEM)
@@ -568,21 +568,14 @@
         pairs.append((keep, send))
         head += count
     if by_hand:
-        keep_late, send_late = pairs[-1]
         one, other = terms_over(gdown, "mp")
-        swapped = [(keep, swap_over(send, "sub")) for keep, send in pairs[:-1]]
-        pieces = exchange(scatter(*swapped, after=[keep_late]))
-        early = add_up(pieces)
-        keep_a, send_a = small_call(
+        swapped = [(keep, swap_over(send, "sub")) for keep, send in pairs]
+        keep, send = small_call(
             functools.partial(split_kernel, tenants, rank), "split_grads", halves_of(tall, width),
-            one, other, info, normed_inputs, after=pieces[1:2],
+            one, other, info, normed_inputs, after=[got for _, got in swapped],
         )
-        shards = scatter(
-            (keep_late, swap_over(send_late, "sub")), (keep_a, swap_over(send_a, "sub")), after=[early]
-        )
-        all_early = spread(early)
-        late = add_up(exchange(shards), after=all_early[1:])
-        half = gather(all_early, spread(late))
+        shards = scatter(*swapped, (keep, swap_over(send, "sub")))
+        half = gather(spread(add_up(exchange(shards))))
         grad_b, grad_a = finish([(half, swap_over(half, "sub"))], up_width)
     else:
         one, other = terms_over(gdown, "mp")

time: 123 us -> 116 us (0.943)
  starting transfers between devices: 48.4 us -> 36.5 us
  waiting for transfers between devices: 31.7 us -> 41.9 us
  Pallas kernels: 37.2 us -> 35.2 us
  local copies, waits for them, and re-layouts: 3.97 us -> 1.99 us
    ppermute x12 -> x6, starting transfers between devices: 26 us -> 16.2 us  [rotate_over(): return lax.ppermute(block, axis, [(i, (i + d) % size) for i in range(size)])]
    ppermute x12 -> x6, waiting for transfers between devices: 24.2 us -> 33.1 us  [rotate_over(): return lax.ppermute(block, axis, [(i, (i + d) % size) for i in range(size)])]
    pallas_call x3, Pallas kernels: 28.8 us -> 26.7 us  [attention(): pl.pallas_call(kernel, grid=(count,), out_shape=[jax.ShapeDtypeStruct((ro...]
    ppermute x9, starting transfers between devices: 10.7 us -> 8.63 us  [swap_over(): return lax.ppermute(block, axis, [(0, 1), (1, 0)])]
    unnamed x36 -> x16, local copies, waits for them, and re-layouts: 3.97 us -> 1.99 us
    ppermute x9, waiting for transfers between devices: 7.4 us -> 8.78 us  [swap_over(): return lax.ppermute(block, axis, [(0, 1), (1, 0)])]
    pallas_call x7 -> x5, Pallas kernels: 2.93 us -> 2.91 us  [small_call(): pl.pallas_call(lambda *refs: kernel(*refs[:count], *refs[len(given):outs]...]
  transfers between devices with their start and end apart: 25 -> 19, of which waited for: 9 -> 8; matrix products, arithmetic and copies ran while one was open for 0% -> 0% of each run, Pallas kernels for 26% -> 15%
where the time goes in v4:
time: 116 us
  waiting for transfers between devices  41.9 us (36%)
  starting transfers between devices  36.5 us (31%)
  Pallas kernels  35.2 us (30%)
  local copies, waits for them, and re-layouts  1.99 us (2%)
    ppermute x6, waiting for transfers between devices, rotate_over(): return lax.ppermute(block, axis, [(i, (i + d) % size) for i in range(size)])  33.1 us
    pallas_call x3, Pallas kernels, attention(): pl.pallas_call(kernel, grid=(count,), out_shape=[jax.ShapeDtypeStruct((ro...  26.7 us
    ppermute x6, starting transfers between devices, rotate_over(): return lax.ppermute(block, axis, [(i, (i + d) % size) for i in range(size)])  16.2 us
    ppermute x4, starting transfers between devices, shift_over(): return lax.ppermute(block, axis, [(i, i + 1) for i in range(size - 1)])  11.7 us
    ppermute x9, waiting for transfers between devices, swap_over(): return lax.ppermute(block, axis, [(0, 1), (1, 0)])  8.78 us
    ppermute x9, starting transfers between devices, swap_over(): return lax.ppermute(block, axis, [(0, 1), (1, 0)])  8.63 us
    pallas_call x1, Pallas kernels, down_project(): pl.pallas_call(functools.partial(down_kernel, tenants, rank), out_shape=j...  3.35 us
    pallas_call x5, Pallas kernels, small_call(): pl.pallas_call(lambda *refs: kernel(*refs[:count], *refs[len(given):outs]...  2.91 us
  transfers between devices with their start and end apart: 19, of which 8 were waited for; matrix products, arithmetic and copies ran while one was open for 0% of the time, Pallas kernels for 15%

profile of v4, /device:TPU:0, one launch (start us, length us, event | category | flops | bytes accessed | tf_op | source)
XLA Modules:
  0.0 116.4 jit_solution(5809993381446423473)
XLA Ops:
  0.6 2.0 %pack_keys_values.1 = (bf16[272,512]{1,0:T(8,128)(2,1)}, bf16[272,512]{1,0:T(8,128)(2,1)}) custom-call(bf16[256,512]{1,0:T(8,128)(2,1)} %keys.1, bf16[256,512]{1,0:T(8,128)(2,1)} %values.1, s32[1,256]{1,0:T(1,128)} %bitcast.13), custom_call_target="tpu_custom_call" | custom-call | bytes 1048576 | tf_op jit(solution)/shard_map/pack_keys_values/pallas_call | solution.py:70
  2.7 0.0 copy-start
  2.7 0.0 copy-start.7
  2.7 5.1 %collective-permute-start.1 = (bf16[272,512]{1,0:T(8,128)(2,1)}, bf16[272,512]{1,0:T(8,128)(2,1)S(1)}, u32[]{:S(2)}, u32[]{:S(2)}) collective-permute-start(bf16[272,512]{1,0:T(8,128)(2,1)} %get-tuple-element.30.own.refs_3_.refs_4_.refs_11_), channel_id=1, source_target_pairs={{0,4},{4,8},{8,12},{1,5},{5,9},{9,13},{2,6},{6,10},{10,14},{3,7},{... | collective-permute-start | bytes 835592 | tf_op jit(solution)/shard_map/ppermute | solution.py:531
  7.8 3.3 %down_project.1.refs_15_.refs_16_.refs_2_ = f32[24,256]{1,0:T(8,128)} custom-call(bf16[256,2560]{1,0:T(8,128)(2,1)} %refs_3_.1, bf16[128,2560]{1,0:T(8,128)(2,1)} %bitcast.12, s32[1,256]{1,0:T(1,128)} %bitcast.14, s32[16]{0:T(128)} %tenant_of.1), custom_call_target="tpu_custom_call" | custom-call | flops 167772160 | bytes 1966080 | tf_op jit(solution)/shard_map/down_project/pallas_call | solution.py:156
  11.1 1.6 %collective-permute-start.2 = (f32[24,256]{1,0:T(8,128)}, f32[24,256]{1,0:T(8,128)S(1)}, u32[]{:S(2)}, u32[]{:S(2)}) collective-permute-start(f32[24,256]{1,0:T(8,128)} %down_project.1.refs_15_.refs_16_.refs_2_), channel_id=1, source_target_pairs={{0,2},{2,0},{1,3},{3,1},{4,6},{6,4},{5,7},{7,5},{8,10},{10,8},{9,1... | collective-permute-start | bytes 73736 | tf_op jit(solution)/shard_map/ppermute | solution.py:515
  12.7 2.5 %collective-permute-done.2.after.refs_17_ = f32[24,256]{1,0:T(8,128)S(1)} collective-permute-done((f32[24,256]{1,0:T(8,128)}, f32[24,256]{1,0:T(8,128)S(1)}, u32[]{:S(2)}, u32[]{:S(2)}) %collective-permute-start.2) | collective-permute-done | bytes 24608 | tf_op jit(solution)/shard_map/ppermute | solution.py:515
  15.2 0.1 relay_block.2
  15.4 1.3 %collective-permute-start.4 = (bf16[272,512]{1,0:T(8,128)(2,1)S(1)}, bf16[272,512]{1,0:T(8,128)(2,1)S(1)}, u32[]{:S(2)}, u32[]{:S(2)}) collective-permute-start(bf16[272,512]{1,0:T(8,128)(2,1)S(1)} %get-tuple-element.32), channel_id=1, source_target_pairs={{0,1},{1,4},{4,5},{5,8},{8,9},{9,12},{12,13},{2,3},{3,6},{6,7},{7,... | collective-permute-start | bytes 835592 | tf_op jit(solution)/shard_map/ppermute | solution.py:531
  16.7 2.3 %collective-permute-start.3 = (bf16[272,512]{1,0:T(8,128)(2,1)S(1)}, bf16[272,512]{1,0:T(8,128)(2,1)S(1)}, u32[]{:S(2)}, u32[]{:S(2)}) collective-permute-start(bf16[272,512]{1,0:T(8,128)(2,1)S(1)} %get-tuple-element.31.refs_5_.refs_6_.refs_12_), channel_id=1, source_target_pairs={{0,1},{1,0},{2,3},{3,2},{4,5},{5,4},{6,7},{7,6},{8,9},{9,8},{10,11... | collective-permute-start | bytes 835592 | tf_op jit(solution)/shard_map/ppermute | solution.py:515
  19.0 3.5 %collective-permute-start = (bf16[272,512]{1,0:T(8,128)(2,1)S(1)}, bf16[272,512]{1,0:T(8,128)(2,1)S(1)}, u32[]{:S(2)}, u32[]{:S(2)}) collective-permute-start(bf16[272,512]{1,0:T(8,128)(2,1)S(1)} %copy-done.7), channel_id=1, source_target_pairs={{0,4},{4,8},{8,12},{1,5},{5,9},{9,13},{2,6},{6,10},{10,14},{3,7},{... | collective-permute-start | bytes 835592 | tf_op jit(solution)/shard_map/ppermute | solution.py:531
  22.5 0.0 collective-permute-done.4.refs_9_.refs_10_.refs_14_
  22.5 0.0 collective-permute-done.3.refs_7_.refs_8_.refs_13_
  22.5 0.0 copy-start.3
  22.6 1.2 %copy-done.3 = bf16[8,16,4096]{2,1,0:T(8,128)(2,1)S(1)} copy-done((bf16[8,16,4096]{2,1,0:T(8,128)(2,1)S(1)}, bf16[8,16,4096]{2,1,0:T(8,128)(2,1)}, u32[]{:S(2)}) %copy-start.3) | copy-done | bytes 1048600
  23.8 0.7 copy-done.5
  24.5 6.9 %attention.3 = (bf16[256,4096]{1,0:T(8,128)(2,1)}, bf16[64,1024]{1,0:T(8,128)(2,1)S(1)}, bf16[64,1024]{1,0:T(8,128)(2,1)S(1)}, f32[16,256]{1,0:T(8,128)S(1)}) custom-call(bf16[256,4096]{1,0:T(8,128)(2,1)S(1)} %copy-done.1, bf16[256,4096]{1,0:T(8,128)(2,1)} %refs_1_.5, bf16[128,4096]{1,0:T(8,128)(2,1)S(1)} %bitcast.9, bf16[272,512]{1,0:T(8,128)(2,1)S(1)} %copy-done, ...), custom_call_target="tpu_custom_call" | custom-call | flops 2147483648 | bytes 1572864 | tf_op jit(solution)/shard_map/attention/pallas_call | solution.py:345
  31.4 0.0 collective-permute-done.got
  31.4 0.1 relay_block.3
  31.6 1.8 %collective-permute-start.6 = (bf16[272,512]{1,0:T(8,128)(2,1)S(1)}, bf16[272,512]{1,0:T(8,128)(2,1)S(1)}, u32[]{:S(2)}, u32[]{:S(2)}) collective-permute-start(bf16[272,512]{1,0:T(8,128)(2,1)S(1)} %get-tuple-element.35), channel_id=1, source_target_pairs={{0,1},{1,4},{4,5},{5,8},{8,9},{9,12},{12,13},{2,3},{3,6},{6,7},{7,... | collective-permute-start | bytes 835592 | tf_op jit(solution)/shard_map/ppermute | solution.py:531
  33.3 2.5 %collective-permute-start.5 = (bf16[272,512]{1,0:T(8,128)(2,1)S(1)}, bf16[272,512]{1,0:T(8,128)(2,1)S(1)}, u32[]{:S(2)}, u32[]{:S(2)}) collective-permute-start(bf16[272,512]{1,0:T(8,128)(2,1)S(1)} %get-tuple-element.34.refs_5_.refs_6_), channel_id=1, source_target_pairs={{0,1},{1,0},{2,3},{3,2},{4,5},{5,4},{6,7},{7,6},{8,9},{9,8},{10,11... | collective-permute-start | bytes 835592 | tf_op jit(solution)/shard_map/ppermute | solution.py:515
  35.9 7.2 %attention.4 = (bf16[256,4096]{1,0:T(8,128)(2,1)}, bf16[64,1024]{1,0:T(8,128)(2,1)S(1)}, bf16[64,1024]{1,0:T(8,128)(2,1)S(1)}, f32[16,256]{1,0:T(8,128)S(1)}) custom-call(bf16[256,4096]{1,0:T(8,128)(2,1)S(1)} %copy-done.1, bf16[256,4096]{1,0:T(8,128)(2,1)} %refs_1_.5, bf16[128,4096]{1,0:T(8,128)(2,1)S(1)} %bitcast.10, ...), custom_call_target="tpu_custom_call", output_to_operand_aliasing={{0}: (19, {})} | custom-call | flops 2147483648 | bytes 1572864 | tf_op jit(solution)/shard_map/attention/pallas_call | solution.py:345
  43.1 0.0 collective-permute-done.6.refs_9_.refs_10_
  43.1 0.0 collective-permute-done.5.refs_7_.refs_8_
  43.1 0.0 copy-start.2
  43.1 12.5 %attention.5 = (bf16[256,4096]{1,0:T(8,128)(2,1)}, bf16[64,2048]{1,0:T(8,128)(2,1)S(1)}, bf16[64,2048]{1,0:T(8,128)(2,1)S(1)}, f32[16,256]{1,0:T(8,128)S(1)}) custom-call(bf16[256,4096]{1,0:T(8,128)(2,1)S(1)} %copy-done.1, bf16[256,4096]{1,0:T(8,128)(2,1)} %refs_1_.5, bf16[128,4096]{1,0:T(8,128)(2,1)S(1)} %bitcast.11, ...), custom_call_target="tpu_custom_call", output_to_operand_aliasing={{0}: (19, {})} | custom-call | flops 4294967296 | bytes 3145728 | tf_op jit(solution)/shard_map/attention/pallas_call | solution.py:345
  55.7 0.0 collective-permute-start.9
  55.7 0.5 collective-permute-start.7
  56.2 0.0 collective-permute-start.8
  56.2 1.5 %collective-permute-start.10 = (f32[16,256]{1,0:T(8,128)S(1)}, f32[16,256]{1,0:T(8,128)S(1)}, u32[]{:S(2)}, u32[]{:S(2)}) collective-permute-start(f32[16,256]{1,0:T(8,128)S(1)} %get-tuple-element.46.refs_0_), channel_id=1, source_target_pairs={{0,2},{2,0},{1,3},{3,1},{4,6},{6,4},{5,7},{7,5},{8,10},{10,8},{9,1... | collective-permute-start | bytes 49160 | tf_op jit(solution)/shard_map/ppermute | solution.py:515
  57.7 2.2 %collective-permute-done.10.refs_1_ = f32[16,256]{1,0:T(8,128)S(1)} collective-permute-done((f32[16,256]{1,0:T(8,128)S(1)}, f32[16,256]{1,0:T(8,128)S(1)}, u32[]{:S(2)}, u32[]{:S(2)}) %collective-permute-start.10) | collective-permute-done | bytes 16416 | tf_op jit(solution)/shard_map/ppermute | solution.py:515
  60.0 0.4 split_grads.1
  60.4 0.1 collective-permute-start.11
  60.5 1.6 %collective-permute-done.11.refs_7_ = bf16[64,2560]{1,0:T(8,128)(2,1)S(1)} collective-permute-done((bf16[64,2560]{1,0:T(8,128)(2,1)S(1)}, bf16[64,2560]{1,0:T(8,128)(2,1)S(1)}, u32[]{:S(2)}, u32[]{:S(2)}) %collective-permute-start.11) | collective-permute-done | bytes 327712 | tf_op jit(solution)/shard_map/ppermute | solution.py:515
  62.1 0.4 scatter_grads.1
  62.5 1.6 %collective-permute-start.12 = (bf16[16,6656]{1,0:T(8,128)(2,1)S(1)}, bf16[16,6656]{1,0:T(8,128)(2,1)S(1)}, u32[]{:S(2)}, u32[]{:S(2)}) collective-permute-start(bf16[16,6656]{1,0:T(8,128)(2,1)S(1)} %get-tuple-element.50), channel_id=1, source_target_pairs={{0,4},{4,8},{8,12},{12,0},{1,5},{5,9},{9,13},{13,1},{2,6},{6,10},{... | collective-permute-start | bytes 638984 | tf_op jit(solution)/shard_map/ppermute | solution.py:520
  64.1 8.0 %collective-permute-start.13 = (bf16[16,6656]{1,0:T(8,128)(2,1)S(1)}, bf16[16,6656]{1,0:T(8,128)(2,1)S(1)}, u32[]{:S(2)}, u32[]{:S(2)}) collective-permute-start(bf16[16,6656]{1,0:T(8,128)(2,1)S(1)} %get-tuple-element.51), channel_id=1, source_target_pairs={{0,8},{4,12},{8,0},{12,4},{1,9},{5,13},{9,1},{13,5},{2,10},{6,14},... | collective-permute-start | bytes 638984 | tf_op jit(solution)/shard_map/ppermute | solution.py:520
  72.1 5.6 %collective-permute-done.12.refs_1_ = bf16[16,6656]{1,0:T(8,128)(2,1)S(1)} collective-permute-done((bf16[16,6656]{1,0:T(8,128)(2,1)S(1)}, bf16[16,6656]{1,0:T(8,128)(2,1)S(1)}, u32[]{:S(2)}, u32[]{:S(2)}) %collective-permute-start.12) | collective-permute-done | bytes 213024 | tf_op jit(solution)/shard_map/ppermute | solution.py:520
  77.7 8.6 %collective-permute-done.13.refs_2_ = bf16[16,6656]{1,0:T(8,128)(2,1)S(1)} collective-permute-done((bf16[16,6656]{1,0:T(8,128)(2,1)S(1)}, bf16[16,6656]{1,0:T(8,128)(2,1)S(1)}, u32[]{:S(2)}, u32[]{:S(2)}) %collective-permute-start.13) | collective-permute-done | bytes 213024 | tf_op jit(solution)/shard_map/ppermute | solution.py:520
  86.4 0.1 sum_grads.1.refs_0_
  86.5 2.7 %collective-permute-start.17 = (bf16[16,6656]{1,0:T(8,128)(2,1)S(1)}, bf16[16,6656]{1,0:T(8,128)(2,1)S(1)}, u32[]{:S(2)}, u32[]{:S(2)}) collective-permute-start(bf16[16,6656]{1,0:T(8,128)(2,1)S(1)} %sum_grads.1.refs_0_), channel_id=1, source_target_pairs={{0,12},{4,0},{8,4},{12,8},{1,13},{5,1},{9,5},{13,9},{2,14},{6,2},{... | collective-permute-start | bytes 638984 | tf_op jit(solution)/shard_map/ppermute | solution.py:520
  89.2 3.9 %collective-permute-start.16 = (bf16[16,6656]{1,0:T(8,128)(2,1)S(1)}, bf16[16,6656]{1,0:T(8,128)(2,1)S(1)}, u32[]{:S(2)}, u32[]{:S(2)}) collective-permute-start(bf16[16,6656]{1,0:T(8,128)(2,1)S(1)} %sum_grads.1.refs_0_), channel_id=1, source_target_pairs={{0,8},{4,12},{8,0},{12,4},{1,9},{5,13},{9,1},{13,5},{2,10},{6,14},... | collective-permute-start | bytes 638984 | tf_op jit(solution)/shard_map/ppermute | solution.py:520
  93.1 4.0 %collective-permute-done.17.refs_3_ = bf16[16,6656]{1,0:T(8,128)(2,1)S(1)} collective-permute-done((bf16[16,6656]{1,0:T(8,128)(2,1)S(1)}, bf16[16,6656]{1,0:T(8,128)(2,1)S(1)}, u32[]{:S(2)}, u32[]{:S(2)}) %collective-permute-start.17) | collective-permute-done | bytes 213024 | tf_op jit(solution)/shard_map/ppermute | solution.py:520
  97.0 14.9 %collective-permute-done.16.refs_2_ = bf16[16,6656]{1,0:T(8,128)(2,1)S(1)} collective-permute-done((bf16[16,6656]{1,0:T(8,128)(2,1)S(1)}, bf16[16,6656]{1,0:T(8,128)(2,1)S(1)}, u32[]{:S(2)}, u32[]{:S(2)}) %collective-permute-start.16) | collective-permute-done | bytes 213024 | tf_op jit(solution)/shard_map/ppermute | solution.py:520
  111.9 0.1 gather_grads.1.refs_0_
  112.0 0.1 collective-permute-start.18
  112.1 2.4 %collective-permute-done.18.refs_1_ = bf16[64,6656]{1,0:T(8,128)(2,1)S(1)} collective-permute-done((bf16[64,6656]{1,0:T(8,128)(2,1)S(1)}, bf16[64,6656]{1,0:T(8,128)(2,1)S(1)}, u32[]{:S(2)}, u32[]{:S(2)}) %collective-permute-start.18) | collective-permute-done | bytes 852000 | tf_op jit(solution)/shard_map/ppermute | solution.py:515
  114.4 1.9 %finish_grads.1 = (f32[128,4096]{1,0:T(8,128)}, f32[128,2560]{1,0:T(8,128)}) custom-call(bf16[64,6656]{1,0:T(8,128)(2,1)S(1)} %gather_grads.1.refs_0_, bf16[64,6656]{1,0:T(8,128)(2,1)S(1)} %collective-permute-done.18.refs_1_), custom_call_target="tpu_custom_call" | custom-call | flops 1703936 | bytes 3407872 | tf_op jit(solution)/shard_map/finish_grads/pallas_call | solution.py:372
  (18 shorter events, 0.0 us)
Async XLA Ops:
  0.6 21.9 %copy-start.1 = (bf16[256,4096]{1,0:T(8,128)(2,1)S(1)}, bf16[256,4096]{1,0:T(8,128)(2,1)}, u32[]{:S(2)}) copy-start(bf16[256,4096]{1,0:T(8,128)(2,1)} %refs_0_.5) | copy-start | bytes 6291460
  2.7 12.6 %copy-start = (bf16[272,512]{1,0:T(8,128)(2,1)S(1)}, bf16[272,512]{1,0:T(8,128)(2,1)}, u32[]{:S(2)}) copy-start(bf16[272,512]{1,0:T(8,128)(2,1)} %get-tuple-element.30.own.refs_3_.refs_4_.refs_11_) | copy-start | bytes 835588
  2.7 16.3 %copy-start.7 = (bf16[272,512]{1,0:T(8,128)(2,1)S(1)}, bf16[272,512]{1,0:T(8,128)(2,1)}, u32[]{:S(2)}) copy-start(bf16[272,512]{1,0:T(8,128)(2,1)} %get-tuple-element.29.own.refs_3_.refs_4_) | copy-start | bytes 835588
  2.7 12.5 %collective-permute-start.1 = (bf16[272,512]{1,0:T(8,128)(2,1)}, bf16[272,512]{1,0:T(8,128)(2,1)S(1)}, u32[]{:S(2)}, u32[]{:S(2)}) collective-permute-start(bf16[272,512]{1,0:T(8,128)(2,1)} %get-tuple-element.30.own.refs_3_.refs_4_.refs_11_), channel_id=1, source_target_pairs={{0,4},{4,8},{8,12},{1,5},{5,9},{9,13},{2,6},{6,10},{10,14},{3,7},{... | collective-permute-start | bytes 835592 | tf_op jit(solution)/shard_map/ppermute | solution.py:531
  11.1 4.1 %collective-permute-start.2 = (f32[24,256]{1,0:T(8,128)}, f32[24,256]{1,0:T(8,128)S(1)}, u32[]{:S(2)}, u32[]{:S(2)}) collective-permute-start(f32[24,256]{1,0:T(8,128)} %down_project.1.refs_15_.refs_16_.refs_2_), channel_id=1, source_target_pairs={{0,2},{2,0},{1,3},{3,1},{4,6},{6,4},{5,7},{7,5},{8,10},{10,8},{9,1... | collective-permute-start | bytes 73736 | tf_op jit(solution)/shard_map/ppermute | solution.py:515
  15.4 7.2 %collective-permute-start.4 = (bf16[272,512]{1,0:T(8,128)(2,1)S(1)}, bf16[272,512]{1,0:T(8,128)(2,1)S(1)}, u32[]{:S(2)}, u32[]{:S(2)}) collective-permute-start(bf16[272,512]{1,0:T(8,128)(2,1)S(1)} %get-tuple-element.32), channel_id=1, source_target_pairs={{0,1},{1,4},{4,5},{5,8},{8,9},{9,12},{12,13},{2,3},{3,6},{6,7},{7,... | collective-permute-start | bytes 835592 | tf_op jit(solution)/shard_map/ppermute | solution.py:531
  16.7 5.9 %collective-permute-start.3 = (bf16[272,512]{1,0:T(8,128)(2,1)S(1)}, bf16[272,512]{1,0:T(8,128)(2,1)S(1)}, u32[]{:S(2)}, u32[]{:S(2)}) collective-permute-start(bf16[272,512]{1,0:T(8,128)(2,1)S(1)} %get-tuple-element.31.refs_5_.refs_6_.refs_12_), channel_id=1, source_target_pairs={{0,1},{1,0},{2,3},{3,2},{4,5},{5,4},{6,7},{7,6},{8,9},{9,8},{10,11... | collective-permute-start | bytes 835592 | tf_op jit(solution)/shard_map/ppermute | solution.py:515
  19.0 12.4 %collective-permute-start = (bf16[272,512]{1,0:T(8,128)(2,1)S(1)}, bf16[272,512]{1,0:T(8,128)(2,1)S(1)}, u32[]{:S(2)}, u32[]{:S(2)}) collective-permute-start(bf16[272,512]{1,0:T(8,128)(2,1)S(1)} %copy-done.7), channel_id=1, source_target_pairs={{0,4},{4,8},{8,12},{1,5},{5,9},{9,13},{2,6},{6,10},{10,14},{3,7},{... | collective-permute-start | bytes 835592 | tf_op jit(solution)/shard_map/ppermute | solution.py:531
  22.5 1.2 %copy-start.3 = (bf16[8,16,4096]{2,1,0:T(8,128)(2,1)S(1)}, bf16[8,16,4096]{2,1,0:T(8,128)(2,1)}, u32[]{:S(2)}) copy-start(bf16[8,16,4096]{2,1,0:T(8,128)(2,1)} %param.14) | copy-start | bytes 3145732
  23.8 0.7 copy-start.5
  24.5 11.4 %copy-start.4 = (bf16[8,16,4096]{2,1,0:T(8,128)(2,1)S(1)}, bf16[8,16,4096]{2,1,0:T(8,128)(2,1)}, u32[]{:S(2)}) copy-start(bf16[8,16,4096]{2,1,0:T(8,128)(2,1)} %param.14) | copy-start | bytes 3145732
  31.6 11.6 %collective-permute-start.6 = (bf16[272,512]{1,0:T(8,128)(2,1)S(1)}, bf16[272,512]{1,0:T(8,128)(2,1)S(1)}, u32[]{:S(2)}, u32[]{:S(2)}) collective-permute-start(bf16[272,512]{1,0:T(8,128)(2,1)S(1)} %get-tuple-element.35), channel_id=1, source_target_pairs={{0,1},{1,4},{4,5},{5,8},{8,9},{9,12},{12,13},{2,3},{3,6},{6,7},{7,... | collective-permute-start | bytes 835592 | tf_op jit(solution)/shard_map/ppermute | solution.py:531
  33.3 9.8 %collective-permute-start.5 = (bf16[272,512]{1,0:T(8,128)(2,1)S(1)}, bf16[272,512]{1,0:T(8,128)(2,1)S(1)}, u32[]{:S(2)}, u32[]{:S(2)}) collective-permute-start(bf16[272,512]{1,0:T(8,128)(2,1)S(1)} %get-tuple-element.34.refs_5_.refs_6_), channel_id=1, source_target_pairs={{0,1},{1,0},{2,3},{3,2},{4,5},{5,4},{6,7},{7,6},{8,9},{9,8},{10,11... | collective-permute-start | bytes 835592 | tf_op jit(solution)/shard_map/ppermute | solution.py:515
  35.9 7.2 %copy-start.6 = (f32[24,256]{1,0:T(8,128)S(1)}, f32[24,256]{1,0:T(8,128)}, u32[]{:S(2)}) copy-start(f32[24,256]{1,0:T(8,128)} %down_project.1.refs_15_.refs_16_.refs_2_) | copy-start | bytes 73732
  43.1 16.8 %copy-start.2 = (bf16[256,2560]{1,0:T(8,128)(2,1)S(1)}, bf16[256,2560]{1,0:T(8,128)(2,1)}, u32[]{:S(2)}) copy-start(bf16[256,2560]{1,0:T(8,128)(2,1)} %refs_3_.1) | copy-start | bytes 3932164
  55.7 4.3 %collective-permute-start.9 = (bf16[64,2048]{1,0:T(8,128)(2,1)S(1)}, bf16[64,2048]{1,0:T(8,128)(2,1)S(1)}, u32[]{:S(2)}, u32[]{:S(2)}) collective-permute-start(bf16[64,2048]{1,0:T(8,128)(2,1)S(1)} %get-tuple-element.45), channel_id=1, source_target_pairs={{0,1},{1,0},{2,3},{3,2},{4,5},{5,4},{6,7},{7,6},{8,9},{9,8},{10,11... | collective-permute-start | bytes 786440 | tf_op jit(solution)/shard_map/ppermute | solution.py:515
  55.7 2.0 %collective-permute-start.7 = (bf16[64,1024]{1,0:T(8,128)(2,1)S(1)}, bf16[64,1024]{1,0:T(8,128)(2,1)S(1)}, u32[]{:S(2)}, u32[]{:S(2)}) collective-permute-start(bf16[64,1024]{1,0:T(8,128)(2,1)S(1)} %get-tuple-element.41), channel_id=1, source_target_pairs={{0,1},{1,0},{2,3},{3,2},{4,5},{5,4},{6,7},{7,6},{8,9},{9,8},{10,11... | collective-permute-start | bytes 393224 | tf_op jit(solution)/shard_map/ppermute | solution.py:515
  56.2 1.5 %collective-permute-start.8 = (bf16[64,1024]{1,0:T(8,128)(2,1)S(1)}, bf16[64,1024]{1,0:T(8,128)(2,1)S(1)}, u32[]{:S(2)}, u32[]{:S(2)}) collective-permute-start(bf16[64,1024]{1,0:T(8,128)(2,1)S(1)} %get-tuple-element.43), channel_id=1, source_target_pairs={{0,1},{1,0},{2,3},{3,2},{4,5},{5,4},{6,7},{7,6},{8,9},{9,8},{10,11... | collective-permute-start | bytes 393224 | tf_op jit(solution)/shard_map/ppermute | solution.py:515
  56.2 3.7 %collective-permute-start.10 = (f32[16,256]{1,0:T(8,128)S(1)}, f32[16,256]{1,0:T(8,128)S(1)}, u32[]{:S(2)}, u32[]{:S(2)}) collective-permute-start(f32[16,256]{1,0:T(8,128)S(1)} %get-tuple-element.46.refs_0_), channel_id=1, source_target_pairs={{0,2},{2,0},{1,3},{3,1},{4,6},{6,4},{5,7},{7,5},{8,10},{10,8},{9,1... | collective-permute-start | bytes 49160 | tf_op jit(solution)/shard_map/ppermute | solution.py:515
  60.4 1.7 %collective-permute-start.11 = (bf16[64,2560]{1,0:T(8,128)(2,1)S(1)}, bf16[64,2560]{1,0:T(8,128)(2,1)S(1)}, u32[]{:S(2)}, u32[]{:S(2)}) collective-permute-start(bf16[64,2560]{1,0:T(8,128)(2,1)S(1)} %get-tuple-element.48), channel_id=1, source_target_pairs={{0,1},{1,0},{2,3},{3,2},{4,5},{5,4},{6,7},{7,6},{8,9},{9,8},{10,11... | collective-permute-start | bytes 983048 | tf_op jit(solution)/shard_map/ppermute | solution.py:515
  62.5 15.3 %collective-permute-start.12 = (bf16[16,6656]{1,0:T(8,128)(2,1)S(1)}, bf16[16,6656]{1,0:T(8,128)(2,1)S(1)}, u32[]{:S(2)}, u32[]{:S(2)}) collective-permute-start(bf16[16,6656]{1,0:T(8,128)(2,1)S(1)} %get-tuple-element.50), channel_id=1, source_target_pairs={{0,4},{4,8},{8,12},{12,0},{1,5},{5,9},{9,13},{13,1},{2,6},{6,10},{... | collective-permute-start | bytes 638984 | tf_op jit(solution)/shard_map/ppermute | solution.py:520
  64.1 22.3 %collective-permute-start.13 = (bf16[16,6656]{1,0:T(8,128)(2,1)S(1)}, bf16[16,6656]{1,0:T(8,128)(2,1)S(1)}, u32[]{:S(2)}, u32[]{:S(2)}) collective-permute-start(bf16[16,6656]{1,0:T(8,128)(2,1)S(1)} %get-tuple-element.51), channel_id=1, source_target_pairs={{0,8},{4,12},{8,0},{12,4},{1,9},{5,13},{9,1},{13,5},{2,10},{6,14},... | collective-permute-start | bytes 638984 | tf_op jit(solution)/shard_map/ppermute | solution.py:520
  72.1 14.2 %collective-permute-start.14 = (bf16[16,6656]{1,0:T(8,128)(2,1)S(1)}, bf16[16,6656]{1,0:T(8,128)(2,1)S(1)}, u32[]{:S(2)}, u32[]{:S(2)}) collective-permute-start(bf16[16,6656]{1,0:T(8,128)(2,1)S(1)} %get-tuple-element.52), channel_id=1, source_target_pairs={{0,12},{4,0},{8,4},{12,8},{1,13},{5,1},{9,5},{13,9},{2,14},{6,2},{... | collective-permute-start | bytes 638984 | tf_op jit(solution)/shard_map/ppermute | solution.py:520
  86.5 10.6 %collective-permute-start.17 = (bf16[16,6656]{1,0:T(8,128)(2,1)S(1)}, bf16[16,6656]{1,0:T(8,128)(2,1)S(1)}, u32[]{:S(2)}, u32[]{:S(2)}) collective-permute-start(bf16[16,6656]{1,0:T(8,128)(2,1)S(1)} %sum_grads.1.refs_0_), channel_id=1, source_target_pairs={{0,12},{4,0},{8,4},{12,8},{1,13},{5,1},{9,5},{13,9},{2,14},{6,2},{... | collective-permute-start | bytes 638984 | tf_op jit(solution)/shard_map/ppermute | solution.py:520
  89.2 22.7 %collective-permute-start.16 = (bf16[16,6656]{1,0:T(8,128)(2,1)S(1)}, bf16[16,6656]{1,0:T(8,128)(2,1)S(1)}, u32[]{:S(2)}, u32[]{:S(2)}) collective-permute-start(bf16[16,6656]{1,0:T(8,128)(2,1)S(1)} %sum_grads.1.refs_0_), channel_id=1, source_target_pairs={{0,8},{4,12},{8,0},{12,4},{1,9},{5,13},{9,1},{13,5},{2,10},{6,14},... | collective-permute-start | bytes 638984 | tf_op jit(solution)/shard_map/ppermute | solution.py:520
  93.0 18.9 %collective-permute-start.15 = (bf16[16,6656]{1,0:T(8,128)(2,1)S(1)}, bf16[16,6656]{1,0:T(8,128)(2,1)S(1)}, u32[]{:S(2)}, u32[]{:S(2)}) collective-permute-start(bf16[16,6656]{1,0:T(8,128)(2,1)S(1)} %sum_grads.1.refs_0_), channel_id=1, source_target_pairs={{0,4},{4,8},{8,12},{12,0},{1,5},{5,9},{9,13},{13,1},{2,6},{6,10},{... | collective-permute-start | bytes 638984 | tf_op jit(solution)/shard_map/ppermute | solution.py:520
  112.0 2.4 %collective-permute-start.18 = (bf16[64,6656]{1,0:T(8,128)(2,1)S(1)}, bf16[64,6656]{1,0:T(8,128)(2,1)S(1)}, u32[]{:S(2)}, u32[]{:S(2)}) collective-permute-start(bf16[64,6656]{1,0:T(8,128)(2,1)S(1)} %gather_grads.1.refs_0_), channel_id=1, source_target_pairs={{0,1},{1,0},{2,3},{3,2},{4,5},{5,4},{6,7},{7,6},{8,9},{9,8},{10,11... | collective-permute-start | bytes 2555912 | tf_op jit(solution)/shard_map/ppermute | solution.py:515

commit v5 on v4

--- a/solution.py
+++ b/solution.py
@@ -183,7 +183,7 @@
 
 
 def attention(
-    head, at, count, group, base, grad, up, blocks, with_ids, info, terms, before, tenants, rank
+    head, at, count, group, base, grad, up, blocks, with_ids, info, before, tenants, rank
 ):
     rows, width = base.shape
     window = (REACH + 1) * rows
@@ -203,8 +203,8 @@
     for block in blocks:
         operands += [block, block]
         specs += [keys, values]
-    operands += [*with_ids, info, *terms]
-    specs += [ids] * 4 + [same(info)] * 3
+    operands += [*with_ids, info]
+    specs += [ids] * 4 + [same(info)]
     if before is not None:
         operands += [before[1], before[0]]
         specs += [same(before[1]), ANY]
@@ -227,7 +227,7 @@
 
     def kernel(*refs):
         base, grad, up = refs[0:3]
-        kv, tails, info, terms = refs[3:11], refs[11:15], refs[15], refs[16:18]
+        kv, tails, info = refs[3:11], refs[11:15], refs[15]
         out, keep, send, projected = refs[len(operands) : len(operands) + 4]
         r = dict(zip(held, refs[len(operands) + 4 :]))
         kw, vw, kt, vt = (r[n] for n in ("kw", "vw", "kt", "vt"))
@@ -240,7 +240,7 @@
         @pl.when(step == 0)
         def _():
             owner = owner_of(info, rank)
-            lifted = unfold((terms[0][...] + terms[1][...])[0:rank], owner, tenants, rank)
+            lifted = unfold(info[0:rank, :], owner, tenants, rank)
             r["bottle_t"][...] = lifted.astype(jnp.bfloat16)
             r["bottle"][...] = lifted.T.astype(jnp.bfloat16)
             r["total"][...] = jnp.zeros((tall, rows), jnp.float32)
@@ -340,7 +340,7 @@
         @pl.when(step == count - 1)
         def _():
             folded = fold(r["total"][...], owner_of(info, rank), tenants, rank)
-            projected[...] = folded if before is None else folded + refs[18][...]
+            projected[...] = folded if before is None else folded + refs[16][...]
 
     return pl.pallas_call(
         kernel,
@@ -353,7 +353,7 @@
         in_specs=specs,
         out_specs=[wide(rows), narrow, narrow, pl.BlockSpec((rank, rows), lambda i: (0, 0))],
         scratch_shapes=list(held.values()),
-        input_output_aliases={19: 0} if before is not None else {},
+        input_output_aliases={17: 0} if before is not None else {},
         compiler_params=params(VMEM_HEADS),
         cost_estimate=pl.CostEstimate(
             flops=8 * rows * window * span * count,
@@ -387,6 +387,11 @@
     return calls if isinstance(shapes, list) or through else calls[0]
 
 
+def join_kernel(rank, info, one, other, out):
+    out[0:rank, :] = one[0:rank, :] + other[0:rank, :]
+    out[rank:, :] = info[rank:, :]
+
+
 def grad_a_of(tenants, rank, one, other, info, x):
     g = unfold((one[...] + other[...]), owner_of(info[...], rank), tenants, rank)
     return nn(g.astype(jnp.bfloat16), x[...]).astype(jnp.bfloat16)
@@ -438,9 +443,9 @@
     me = lax.axis_index("seq")
     for first in range(0, len(pieces), size):
         rows, width = pieces[first].shape
-        for d in range(size):
+        for i, d in enumerate(gather_order(size)):
             at = pl.multiple_of(lax.rem(me + size - d, size) * rows, rows)
-            out[pl.ds(at, rows), col : col + width] = pieces[first + d][...]
+            out[pl.ds(at, rows), col : col + width] = pieces[first + i][...]
         col += width
 
 
@@ -454,33 +459,40 @@
     )
 
 
-def finish_kernel(count, *refs):
-    grad_b, grad_a = refs[2 * count :]
+def finish_kernel(other, block, *refs):
+    grad_b, grad_a, held_b, held_a, sems = refs[-5:]
+    half, wide = held_b.shape
     sub = lax.axis_index("sub")
-    half, wide = refs[0].shape[0], grad_b.shape[1]
-    here = pl.ds(pl.multiple_of(sub * half, half), half)
-    there = pl.ds(pl.multiple_of((1 - sub) * half, half), half)
-    for at, group in ((here, refs[0 : 2 * count : 2]), (there, refs[1 : 2 * count : 2])):
-        col = 0
-        for ref in group:
-            width = ref.shape[1]
-            first = min(width, wide - col)
-            grad_b[at, col : col + first] = ref[:, 0:first].astype(jnp.float32)
-            if first < width:
-                grad_a[at, :] = ref[:, first:].astype(jnp.float32)
-            col += width
-
-
-def finish(pairs, wide):
-    rows, width = pairs[0][0].shape[0] * 2, sum(half.shape[1] for half, _ in pairs)
-    return small_call(
-        functools.partial(finish_kernel, len(pairs)), "finish_grads",
-        [
-            jax.ShapeDtypeStruct((rows, wide), jnp.float32),
-            jax.ShapeDtypeStruct((rows, width - wide), jnp.float32),
+    place = (1 - sub if other else sub) * half
+    at = pl.ds(pl.multiple_of(place, half), half)
+    held_b[...] = block[:, 0:wide].astype(jnp.float32)
+    first = fetch([(held_b, grad_b.at[at, :])], sems.at[pl.ds(0, 1)])
+    held_a[...] = block[:, wide:].astype(jnp.float32)
+    for copy in first + fetch([(held_a, grad_a.at[at, :])], sems.at[pl.ds(1, 1)]):
+        copy.wait()
+
+
+def finish(block, wide, before=None):
+    half, width = block.shape
+    operands = (block,) if before is None else (block, *before)
+    shapes = [(2 * half, wide), (2 * half, width - wide)]
+    return pl.pallas_call(
+        functools.partial(finish_kernel, before is not None),
+        out_shape=[jax.ShapeDtypeStruct(shape, jnp.float32) for shape in shapes],
+        in_specs=[VM] + [ANY] * (len(operands) - 1),
+        out_specs=[ANY] * 2,
+        scratch_shapes=[
+            pltpu.VMEM((half, wide), jnp.float32),
+            pltpu.VMEM((half, width - wide), jnp.float32),
+            pltpu.SemaphoreType.DMA((2,)),
         ],
-        *[block for pair in pairs for block in pair],
-    )
+        input_output_aliases={} if before is None else {1: 0, 2: 1},
+        compiler_params=params(),
+        cost_estimate=pl.CostEstimate(
+            flops=block.size, bytes_accessed=6 * block.size, transcendentals=0
+        ),
+        name="finish_grads",
+    )(*operands)
 
 
 def halves_of(rows, width):
@@ -498,8 +510,16 @@
     )
 
 
+def longest_first(size):
+    return sorted(range(1, size), key=lambda d: -min(d, size - d))
+
+
+def gather_order(size):
+    return [0] + longest_first(size)[::-1]
+
+
 def exchange(shards):
-    return [shards[0]] + [rotate_over(block, "seq", d + 1) for d, block in enumerate(shards[1:])]
+    return [shards[0]] + [rotate_over(shards[d], "seq", d) for d in longest_first(len(shards))]
 
 
 def add_up(pieces, after=(), through=()):
@@ -508,7 +528,8 @@
 
 
 def spread(shard):
-    return [shard] + [rotate_over(shard, "seq", d) for d in range(1, lax.axis_size("seq"))]
+    order = gather_order(lax.axis_size("seq"))
+    return [rotate_over(shard, "seq", d) if d else shard for d in order]
 
 
 def swap_over(block, axis):
@@ -548,7 +569,10 @@
 
     own = pack(base_keys, base_values, doc, chunks)
     info = down_project(normed_inputs, adapter, doc, document_tenant, tenants, rank)
-    terms = terms_over(info, "mp")
+    info = small_call(
+        functools.partial(join_kernel, rank), "join_terms",
+        jax.ShapeDtypeStruct(info.shape, info.dtype), info, *terms_over(info, "mp"),
+    )
     group = base_queries.shape[1] // HEAD // key_heads
     per = key_heads // chunks
     counts = [1, per - 1, per] if chunks == 2 else [1] * per
@@ -557,12 +581,12 @@
         chunk = head // per
         if len(held) < chunks and i < 2:
             two = shift_over(own[i], "seq")
-            passing, two = relay(own[i], two, terms[1] if i == 0 else state[1])
+            passing, two = relay(own[i], two, info if i == 0 else state[1])
             held.append((own[i], two, swap_over(two, "sub"), shift_over(passing, ("seq", "sub"))))
         with_ids = held[0]
         out, keep, send, gdown = attention(
             head, head % per, count, group, base_queries, output_gradient, up, held[chunk],
-            with_ids, info, terms, state, tenants, rank,
+            with_ids, info, state, tenants, rank,
         )
         state = (out, gdown)
         pairs.append((keep, send))
@@ -576,7 +600,8 @@
         )
         shards = scatter(*swapped, (keep, swap_over(send, "sub")))
         half = gather(spread(add_up(exchange(shards))))
-        grad_b, grad_a = finish([(half, swap_over(half, "sub"))], up_width)
+        other = swap_over(half, "sub")
+        grad_b, grad_a = finish(other, up_width, finish(half, up_width))
     else:
         one, other = terms_over(gdown, "mp")
         part_a = small_call(

time: 116 us -> 110 us (0.948)
  the two profiles are of different devices: /device:TPU:0 before, /device:TPU:9 now
where the time goes in v5:
time: 110 us; the launch traced here: 108 us
  waiting for transfers between devices  39.7 us (36%)
  Pallas kernels  35.8 us (33%)
  starting transfers between devices  29.3 us (27%)
  local copies, waits for them, and re-layouts  1.99 us (2%)
    ppermute x6, waiting for transfers between devices, rotate_over(): return lax.ppermute(block, axis, [(i, (i + d) % size) for i in range(size)])  33 us
    pallas_call x3, Pallas kernels, attention(): pl.pallas_call(kernel, grid=(count,), out_shape=[jax.ShapeDtypeStruct((ro...  26.7 us
    ppermute x4, starting transfers between devices, shift_over(): return lax.ppermute(block, axis, [(i, i + 1) for i in range(size - 1)])  14.6 us
    ppermute x9, starting transfers between devices, swap_over(): return lax.ppermute(block, axis, [(0, 1), (1, 0)])  10.7 us
    ppermute x9, waiting for transfers between devices, swap_over(): return lax.ppermute(block, axis, [(0, 1), (1, 0)])  5.34 us
    ppermute x6, starting transfers between devices, rotate_over(): return lax.ppermute(block, axis, [(i, (i + d) % size) for i in range(size)])  3.98 us
    pallas_call x1, Pallas kernels, down_project(): pl.pallas_call(functools.partial(down_kernel, tenants, rank), out_shape=j...  3.36 us
    pallas_call x2, Pallas kernels, finish(): pl.pallas_call(functools.partial(finish_kernel, before is not None), out_...  2.53 us
  transfers between devices with their start and end apart: 19, of which 10 were waited for; matrix products, arithmetic and copies ran while one was open for 0% of the time, Pallas kernels for 17%

profile of v5, /device:TPU:9, one launch (start us, length us, event | category | flops | bytes accessed | tf_op | source)
XLA Modules:
  0.0 107.8 jit_solution(15029530223104986046)
XLA Ops:
  0.6 2.0 %pack_keys_values.1 = (bf16[272,512]{1,0:T(8,128)(2,1)}, bf16[272,512]{1,0:T(8,128)(2,1)}) custom-call(bf16[256,512]{1,0:T(8,128)(2,1)} %keys.1, bf16[256,512]{1,0:T(8,128)(2,1)} %values.1, s32[1,256]{1,0:T(1,128)} %bitcast.15), custom_call_target="tpu_custom_call" | custom-call | bytes 1048576 | tf_op jit(solution)/shard_map/pack_keys_values/pallas_call | solution.py:70
  2.7 0.0 copy-start
  2.7 0.0 copy-start.5
  2.7 3.3 %collective-permute-start.1 = (bf16[272,512]{1,0:T(8,128)(2,1)}, bf16[272,512]{1,0:T(8,128)(2,1)S(1)}, u32[]{:S(2)}, u32[]{:S(2)}) collective-permute-start(bf16[272,512]{1,0:T(8,128)(2,1)} %get-tuple-element.32.own.refs_3_.refs_4_.refs_11_), channel_id=1, source_target_pairs={{0,4},{4,8},{8,12},{1,5},{5,9},{9,13},{2,6},{6,10},{10,14},{3,7},{... | collective-permute-start | bytes 835592 | tf_op jit(solution)/shard_map/ppermute | solution.py:552
  6.0 3.4 %down_project.1.refs_0_.refs_1_ = f32[24,256]{1,0:T(8,128)} custom-call(bf16[256,2560]{1,0:T(8,128)(2,1)} %refs_3_.1, bf16[128,2560]{1,0:T(8,128)(2,1)} %bitcast.14, s32[1,256]{1,0:T(1,128)} %bitcast.16, s32[16]{0:T(128)} %tenant_of.1), custom_call_target="tpu_custom_call" | custom-call | flops 167772160 | bytes 1966080 | tf_op jit(solution)/shard_map/down_project/pallas_call | solution.py:156
  9.4 1.3 %collective-permute-start.2 = (f32[24,256]{1,0:T(8,128)}, f32[24,256]{1,0:T(8,128)S(1)}, u32[]{:S(2)}, u32[]{:S(2)}) collective-permute-start(f32[24,256]{1,0:T(8,128)} %down_project.1.refs_0_.refs_1_), channel_id=1, source_target_pairs={{0,2},{2,0},{1,3},{3,1},{4,6},{6,4},{5,7},{7,5},{8,10},{10,8},{9,1... | collective-permute-start | bytes 73736 | tf_op jit(solution)/shard_map/ppermute | solution.py:536
  10.7 2.0 %collective-permute-done.2.refs_2_ = f32[24,256]{1,0:T(8,128)S(1)} collective-permute-done((f32[24,256]{1,0:T(8,128)}, f32[24,256]{1,0:T(8,128)S(1)}, u32[]{:S(2)}, u32[]{:S(2)}) %collective-permute-start.2) | collective-permute-done | bytes 24608 | tf_op jit(solution)/shard_map/ppermute | solution.py:536
  12.7 0.7 copy-done.6
  13.4 0.1 relay_block.2
  13.5 4.9 %collective-permute-start.4 = (bf16[272,512]{1,0:T(8,128)(2,1)S(1)}, bf16[272,512]{1,0:T(8,128)(2,1)S(1)}, u32[]{:S(2)}, u32[]{:S(2)}) collective-permute-start(bf16[272,512]{1,0:T(8,128)(2,1)S(1)} %get-tuple-element.34), channel_id=1, source_target_pairs={{0,1},{1,4},{4,5},{5,8},{8,9},{9,12},{12,13},{2,3},{3,6},{6,7},{7,... | collective-permute-start | bytes 835592 | tf_op jit(solution)/shard_map/ppermute | solution.py:552
  18.4 0.1 collective-permute-start.3
  18.5 2.0 %collective-permute-start = (bf16[272,512]{1,0:T(8,128)(2,1)S(1)}, bf16[272,512]{1,0:T(8,128)(2,1)S(1)}, u32[]{:S(2)}, u32[]{:S(2)}) collective-permute-start(bf16[272,512]{1,0:T(8,128)(2,1)S(1)} %copy-done.5), channel_id=1, source_target_pairs={{0,4},{4,8},{8,12},{1,5},{5,9},{9,13},{2,6},{6,10},{10,14},{3,7},{... | collective-permute-start | bytes 835592 | tf_op jit(solution)/shard_map/ppermute | solution.py:552
  20.5 1.4 %collective-permute-done.4.refs_9_.refs_10_.refs_14_ = bf16[272,512]{1,0:T(8,128)(2,1)S(1)} collective-permute-done((bf16[272,512]{1,0:T(8,128)(2,1)S(1)}, bf16[272,512]{1,0:T(8,128)(2,1)S(1)}, u32[]{:S(2)}, u32[]{:S(2)}) %collective-permute-start.4) | collective-permute-done | bytes 278560 | tf_op jit(solution)/shard_map/ppermute | solution.py:552
  21.9 0.0 collective-permute-done.3.refs_7_.refs_8_.refs_13_
  21.9 1.2 %copy-done.3 = bf16[8,16,4096]{2,1,0:T(8,128)(2,1)S(1)} copy-done((bf16[8,16,4096]{2,1,0:T(8,128)(2,1)S(1)}, bf16[8,16,4096]{2,1,0:T(8,128)(2,1)}, u32[]{:S(2)}) %copy-start.3) | copy-done | bytes 1048600
  23.2 6.9 %attention.3 = (bf16[256,4096]{1,0:T(8,128)(2,1)}, bf16[64,1024]{1,0:T(8,128)(2,1)S(1)}, bf16[64,1024]{1,0:T(8,128)(2,1)S(1)}, f32[16,256]{1,0:T(8,128)S(1)}) custom-call(bf16[256,4096]{1,0:T(8,128)(2,1)S(1)} %copy-done.1, bf16[256,4096]{1,0:T(8,128)(2,1)} %refs_1_.5, bf16[128,4096]{1,0:T(8,128)(2,1)S(1)} %bitcast.9, bf16[272,512]{1,0:T(8,128)(2,1)S(1)} %copy-done, ...), custom_call_target="tpu_custom_call" | custom-call | flops 2147483648 | bytes 1572864 | tf_op jit(solution)/shard_map/attention/pallas_call | solution.py:345
  30.1 0.1 relay_block.3
  30.2 4.4 %collective-permute-start.6 = (bf16[272,512]{1,0:T(8,128)(2,1)S(1)}, bf16[272,512]{1,0:T(8,128)(2,1)S(1)}, u32[]{:S(2)}, u32[]{:S(2)}) collective-permute-start(bf16[272,512]{1,0:T(8,128)(2,1)S(1)} %get-tuple-element.37), channel_id=1, source_target_pairs={{0,1},{1,4},{4,5},{5,8},{8,9},{9,12},{12,13},{2,3},{3,6},{6,7},{7,... | collective-permute-start | bytes 835592 | tf_op jit(solution)/shard_map/ppermute | solution.py:552
  34.6 0.6 collective-permute-start.5
  35.2 7.3 %attention.4 = (bf16[256,4096]{1,0:T(8,128)(2,1)}, bf16[64,1024]{1,0:T(8,128)(2,1)S(1)}, bf16[64,1024]{1,0:T(8,128)(2,1)S(1)}, f32[16,256]{1,0:T(8,128)S(1)}) custom-call(bf16[256,4096]{1,0:T(8,128)(2,1)S(1)} %copy-done.1, bf16[256,4096]{1,0:T(8,128)(2,1)} %refs_1_.5, bf16[128,4096]{1,0:T(8,128)(2,1)S(1)} %bitcast.10, ...), custom_call_target="tpu_custom_call", output_to_operand_aliasing={{0}: (17, {})} | custom-call | flops 2147483648 | bytes 1572864 | tf_op jit(solution)/shard_map/attention/pallas_call | solution.py:345
  42.4 0.0 collective-permute-done.6.refs_9_.refs_10_
  42.4 0.0 collective-permute-done.5.refs_7_.refs_8_
  42.5 12.5 %attention.5 = (bf16[256,4096]{1,0:T(8,128)(2,1)}, bf16[64,2048]{1,0:T(8,128)(2,1)S(1)}, bf16[64,2048]{1,0:T(8,128)(2,1)S(1)}, f32[16,256]{1,0:T(8,128)S(1)}) custom-call(bf16[256,4096]{1,0:T(8,128)(2,1)S(1)} %copy-done.1, bf16[256,4096]{1,0:T(8,128)(2,1)} %refs_1_.5, bf16[128,4096]{1,0:T(8,128)(2,1)S(1)} %bitcast.11, ...), custom_call_target="tpu_custom_call", output_to_operand_aliasing={{0}: (17, {})} | custom-call | flops 4294967296 | bytes 3145728 | tf_op jit(solution)/shard_map/attention/pallas_call | solution.py:345
  55.0 5.1 %collective-permute-start.9 = (bf16[64,2048]{1,0:T(8,128)(2,1)S(1)}, bf16[64,2048]{1,0:T(8,128)(2,1)S(1)}, u32[]{:S(2)}, u32[]{:S(2)}) collective-permute-start(bf16[64,2048]{1,0:T(8,128)(2,1)S(1)} %get-tuple-element.47), channel_id=1, source_target_pairs={{0,1},{1,0},{2,3},{3,2},{4,5},{5,4},{6,7},{7,6},{8,9},{9,8},{10,11... | collective-permute-start | bytes 786440 | tf_op jit(solution)/shard_map/ppermute | solution.py:536
  60.1 0.0 collective-permute-start.7
  60.1 0.5 collective-permute-start.8
  60.6 1.2 %collective-permute-start.10 = (f32[16,256]{1,0:T(8,128)S(1)}, f32[16,256]{1,0:T(8,128)S(1)}, u32[]{:S(2)}, u32[]{:S(2)}) collective-permute-start(f32[16,256]{1,0:T(8,128)S(1)} %get-tuple-element.48.refs_0_), channel_id=1, source_target_pairs={{0,2},{2,0},{1,3},{3,1},{4,6},{6,4},{5,7},{7,5},{8,10},{10,8},{9,1... | collective-permute-start | bytes 49160 | tf_op jit(solution)/shard_map/ppermute | solution.py:536
  61.8 1.4 %collective-permute-done.10.refs_1_ = f32[16,256]{1,0:T(8,128)S(1)} collective-permute-done((f32[16,256]{1,0:T(8,128)S(1)}, f32[16,256]{1,0:T(8,128)S(1)}, u32[]{:S(2)}, u32[]{:S(2)}) %collective-permute-start.10) | collective-permute-done | bytes 16416 | tf_op jit(solution)/shard_map/ppermute | solution.py:536
  63.2 0.4 split_grads.1
  63.6 1.2 %collective-permute-start.11 = (bf16[64,2560]{1,0:T(8,128)(2,1)S(1)}, bf16[64,2560]{1,0:T(8,128)(2,1)S(1)}, u32[]{:S(2)}, u32[]{:S(2)}) collective-permute-start(bf16[64,2560]{1,0:T(8,128)(2,1)S(1)} %get-tuple-element.50), channel_id=1, source_target_pairs={{0,1},{1,0},{2,3},{3,2},{4,5},{5,4},{6,7},{7,6},{8,9},{9,8},{10,11... | collective-permute-start | bytes 983048 | tf_op jit(solution)/shard_map/ppermute | solution.py:536
  64.9 1.3 %collective-permute-done.11.refs_7_ = bf16[64,2560]{1,0:T(8,128)(2,1)S(1)} collective-permute-done((bf16[64,2560]{1,0:T(8,128)(2,1)S(1)}, bf16[64,2560]{1,0:T(8,128)(2,1)S(1)}, u32[]{:S(2)}, u32[]{:S(2)}) %collective-permute-start.11) | collective-permute-done | bytes 327712 | tf_op jit(solution)/shard_map/ppermute | solution.py:536
  66.1 0.4 scatter_grads.1
  66.5 0.1 collective-permute-start.12
  66.6 0.1 collective-permute-start.13
  66.7 1.5 %collective-permute-start.14 = (bf16[16,6656]{1,0:T(8,128)(2,1)S(1)}, bf16[16,6656]{1,0:T(8,128)(2,1)S(1)}, u32[]{:S(2)}, u32[]{:S(2)}) collective-permute-start(bf16[16,6656]{1,0:T(8,128)(2,1)S(1)} %get-tuple-element.54), channel_id=1, source_target_pairs={{0,12},{4,0},{8,4},{12,8},{1,13},{5,1},{9,5},{13,9},{2,14},{6,2},{... | collective-permute-start | bytes 638984 | tf_op jit(solution)/shard_map/ppermute | solution.py:541
  68.1 5.9 %collective-permute-done.12.refs_1_ = bf16[16,6656]{1,0:T(8,128)(2,1)S(1)} collective-permute-done((bf16[16,6656]{1,0:T(8,128)(2,1)S(1)}, bf16[16,6656]{1,0:T(8,128)(2,1)S(1)}, u32[]{:S(2)}, u32[]{:S(2)}) %collective-permute-start.12) | collective-permute-done | bytes 213024 | tf_op jit(solution)/shard_map/ppermute | solution.py:541
  74.0 7.8 %collective-permute-done.13.refs_2_ = bf16[16,6656]{1,0:T(8,128)(2,1)S(1)} collective-permute-done((bf16[16,6656]{1,0:T(8,128)(2,1)S(1)}, bf16[16,6656]{1,0:T(8,128)(2,1)S(1)}, u32[]{:S(2)}, u32[]{:S(2)}) %collective-permute-start.13) | collective-permute-done | bytes 213024 | tf_op jit(solution)/shard_map/ppermute | solution.py:541
  81.8 2.1 %collective-permute-done.14.refs_3_ = bf16[16,6656]{1,0:T(8,128)(2,1)S(1)} collective-permute-done((bf16[16,6656]{1,0:T(8,128)(2,1)S(1)}, bf16[16,6656]{1,0:T(8,128)(2,1)S(1)}, u32[]{:S(2)}, u32[]{:S(2)}) %collective-permute-start.14) | collective-permute-done | bytes 213024 | tf_op jit(solution)/shard_map/ppermute | solution.py:541
  83.9 0.1 sum_grads.1.refs_0_
  84.1 0.9 collective-permute-start.17
  85.0 1.5 %collective-permute-start.15 = (bf16[16,6656]{1,0:T(8,128)(2,1)S(1)}, bf16[16,6656]{1,0:T(8,128)(2,1)S(1)}, u32[]{:S(2)}, u32[]{:S(2)}) collective-permute-start(bf16[16,6656]{1,0:T(8,128)(2,1)S(1)} %sum_grads.1.refs_0_), channel_id=1, source_target_pairs={{0,12},{4,0},{8,4},{12,8},{1,13},{5,1},{9,5},{13,9},{2,14},{6,2},{... | collective-permute-start | bytes 638984 | tf_op jit(solution)/shard_map/ppermute | solution.py:541
  86.5 8.3 %collective-permute-done.17.refs_3_ = bf16[16,6656]{1,0:T(8,128)(2,1)S(1)} collective-permute-done((bf16[16,6656]{1,0:T(8,128)(2,1)S(1)}, bf16[16,6656]{1,0:T(8,128)(2,1)S(1)}, u32[]{:S(2)}, u32[]{:S(2)}) %collective-permute-start.17) | collective-permute-done | bytes 213024 | tf_op jit(solution)/shard_map/ppermute | solution.py:541
  94.8 8.9 %collective-permute-done.16.refs_2_ = bf16[16,6656]{1,0:T(8,128)(2,1)S(1)} collective-permute-done((bf16[16,6656]{1,0:T(8,128)(2,1)S(1)}, bf16[16,6656]{1,0:T(8,128)(2,1)S(1)}, u32[]{:S(2)}, u32[]{:S(2)}) %collective-permute-start.16) | collective-permute-done | bytes 213024 | tf_op jit(solution)/shard_map/ppermute | solution.py:541
  103.6 0.1 gather_grads.1.block
  103.7 0.6 collective-permute-start.18
  104.3 1.3 %finish_grads.2 = (f32[128,4096]{1,0:T(8,128)}, f32[128,2560]{1,0:T(8,128)}) custom-call(bf16[64,6656]{1,0:T(8,128)(2,1)S(1)} %gather_grads.1.block), custom_call_target="tpu_custom_call" | custom-call | flops 425984 | bytes 2555904 | tf_op jit(solution)/shard_map/finish_grads/pallas_call | solution.py:479
  105.6 0.7 collective-permute-done.18.block
  106.3 1.3 %finish_grads.3 = (f32[128,4096]{1,0:T(8,128)}, f32[128,2560]{1,0:T(8,128)}) custom-call(bf16[64,6656]{1,0:T(8,128)(2,1)S(1)} %collective-permute-done.18.block, f32[128,4096]{1,0:T(8,128)} %get-tuple-element.55.refs_0_, f32[128,2560]{1,0:T(8,128)} %get-tuple-element.56.refs_1_), custom_call_target="tpu_custom_call", output_to_operand_aliasing={{0}: (1, {}), {1}: (2, {})} | custom-call | flops 425984 | bytes 2555904 | tf_op jit(solution)/shard_map/finish_grads/pallas_call | solution.py:479
  (18 shorter events, 0.0 us)
Async XLA Ops:
  0.6 21.3 %copy-start.1 = (bf16[256,4096]{1,0:T(8,128)(2,1)S(1)}, bf16[256,4096]{1,0:T(8,128)(2,1)}, u32[]{:S(2)}) copy-start(bf16[256,4096]{1,0:T(8,128)(2,1)} %refs_0_.5) | copy-start | bytes 6291460
  2.7 10.7 %copy-start = (bf16[272,512]{1,0:T(8,128)(2,1)S(1)}, bf16[272,512]{1,0:T(8,128)(2,1)}, u32[]{:S(2)}) copy-start(bf16[272,512]{1,0:T(8,128)(2,1)} %get-tuple-element.32.own.refs_3_.refs_4_.refs_11_) | copy-start | bytes 835588
  2.7 15.8 %copy-start.5 = (bf16[272,512]{1,0:T(8,128)(2,1)S(1)}, bf16[272,512]{1,0:T(8,128)(2,1)}, u32[]{:S(2)}) copy-start(bf16[272,512]{1,0:T(8,128)(2,1)} %get-tuple-element.31.own.refs_3_.refs_4_) | copy-start | bytes 835588
  2.7 10.7 %collective-permute-start.1 = (bf16[272,512]{1,0:T(8,128)(2,1)}, bf16[272,512]{1,0:T(8,128)(2,1)S(1)}, u32[]{:S(2)}, u32[]{:S(2)}) collective-permute-start(bf16[272,512]{1,0:T(8,128)(2,1)} %get-tuple-element.32.own.refs_3_.refs_4_.refs_11_), channel_id=1, source_target_pairs={{0,4},{4,8},{8,12},{1,5},{5,9},{9,13},{2,6},{6,10},{10,14},{3,7},{... | collective-permute-start | bytes 835592 | tf_op jit(solution)/shard_map/ppermute | solution.py:552
  9.4 3.2 %collective-permute-start.2 = (f32[24,256]{1,0:T(8,128)}, f32[24,256]{1,0:T(8,128)S(1)}, u32[]{:S(2)}, u32[]{:S(2)}) collective-permute-start(f32[24,256]{1,0:T(8,128)} %down_project.1.refs_0_.refs_1_), channel_id=1, source_target_pairs={{0,2},{2,0},{1,3},{3,1},{4,6},{6,4},{5,7},{7,5},{8,10},{10,8},{9,1... | collective-permute-start | bytes 73736 | tf_op jit(solution)/shard_map/ppermute | solution.py:536
  12.7 0.7 copy-start.6
  13.5 8.4 %collective-permute-start.4 = (bf16[272,512]{1,0:T(8,128)(2,1)S(1)}, bf16[272,512]{1,0:T(8,128)(2,1)S(1)}, u32[]{:S(2)}, u32[]{:S(2)}) collective-permute-start(bf16[272,512]{1,0:T(8,128)(2,1)S(1)} %get-tuple-element.34), channel_id=1, source_target_pairs={{0,1},{1,4},{4,5},{5,8},{8,9},{9,12},{12,13},{2,3},{3,6},{6,7},{7,... | collective-permute-start | bytes 835592 | tf_op jit(solution)/shard_map/ppermute | solution.py:552
  18.4 3.5 %collective-permute-start.3 = (bf16[272,512]{1,0:T(8,128)(2,1)S(1)}, bf16[272,512]{1,0:T(8,128)(2,1)S(1)}, u32[]{:S(2)}, u32[]{:S(2)}) collective-permute-start(bf16[272,512]{1,0:T(8,128)(2,1)S(1)} %get-tuple-element.33.refs_5_.refs_6_.refs_12_), channel_id=1, source_target_pairs={{0,1},{1,0},{2,3},{3,2},{4,5},{5,4},{6,7},{7,6},{8,9},{9,8},{10,11... | collective-permute-start | bytes 835592 | tf_op jit(solution)/shard_map/ppermute | solution.py:536
  18.5 11.5 %collective-permute-start = (bf16[272,512]{1,0:T(8,128)(2,1)S(1)}, bf16[272,512]{1,0:T(8,128)(2,1)S(1)}, u32[]{:S(2)}, u32[]{:S(2)}) collective-permute-start(bf16[272,512]{1,0:T(8,128)(2,1)S(1)} %copy-done.5), channel_id=1, source_target_pairs={{0,4},{4,8},{8,12},{1,5},{5,9},{9,13},{2,6},{6,10},{10,14},{3,7},{... | collective-permute-start | bytes 835592 | tf_op jit(solution)/shard_map/ppermute | solution.py:552
  21.9 1.2 %copy-start.3 = (bf16[8,16,4096]{2,1,0:T(8,128)(2,1)S(1)}, bf16[8,16,4096]{2,1,0:T(8,128)(2,1)}, u32[]{:S(2)}) copy-start(bf16[8,16,4096]{2,1,0:T(8,128)(2,1)} %param.14) | copy-start | bytes 3145732
  23.1 12.0 %copy-start.4 = (bf16[8,16,4096]{2,1,0:T(8,128)(2,1)S(1)}, bf16[8,16,4096]{2,1,0:T(8,128)(2,1)}, u32[]{:S(2)}) copy-start(bf16[8,16,4096]{2,1,0:T(8,128)(2,1)} %param.14) | copy-start | bytes 3145732
  30.2 12.3 %collective-permute-start.6 = (bf16[272,512]{1,0:T(8,128)(2,1)S(1)}, bf16[272,512]{1,0:T(8,128)(2,1)S(1)}, u32[]{:S(2)}, u32[]{:S(2)}) collective-permute-start(bf16[272,512]{1,0:T(8,128)(2,1)S(1)} %get-tuple-element.37), channel_id=1, source_target_pairs={{0,1},{1,4},{4,5},{5,8},{8,9},{9,12},{12,13},{2,3},{3,6},{6,7},{7,... | collective-permute-start | bytes 835592 | tf_op jit(solution)/shard_map/ppermute | solution.py:552
  34.6 7.9 %collective-permute-start.5 = (bf16[272,512]{1,0:T(8,128)(2,1)S(1)}, bf16[272,512]{1,0:T(8,128)(2,1)S(1)}, u32[]{:S(2)}, u32[]{:S(2)}) collective-permute-start(bf16[272,512]{1,0:T(8,128)(2,1)S(1)} %get-tuple-element.36.refs_5_.refs_6_), channel_id=1, source_target_pairs={{0,1},{1,0},{2,3},{3,2},{4,5},{5,4},{6,7},{7,6},{8,9},{9,8},{10,11... | collective-permute-start | bytes 835592 | tf_op jit(solution)/shard_map/ppermute | solution.py:536
  42.4 20.8 %copy-start.2 = (bf16[256,2560]{1,0:T(8,128)(2,1)S(1)}, bf16[256,2560]{1,0:T(8,128)(2,1)}, u32[]{:S(2)}) copy-start(bf16[256,2560]{1,0:T(8,128)(2,1)} %refs_3_.1) | copy-start | bytes 3932164
  55.0 8.2 %collective-permute-start.9 = (bf16[64,2048]{1,0:T(8,128)(2,1)S(1)}, bf16[64,2048]{1,0:T(8,128)(2,1)S(1)}, u32[]{:S(2)}, u32[]{:S(2)}) collective-permute-start(bf16[64,2048]{1,0:T(8,128)(2,1)S(1)} %get-tuple-element.47), channel_id=1, source_target_pairs={{0,1},{1,0},{2,3},{3,2},{4,5},{5,4},{6,7},{7,6},{8,9},{9,8},{10,11... | collective-permute-start | bytes 786440 | tf_op jit(solution)/shard_map/ppermute | solution.py:536
  60.1 1.7 %collective-permute-start.7 = (bf16[64,1024]{1,0:T(8,128)(2,1)S(1)}, bf16[64,1024]{1,0:T(8,128)(2,1)S(1)}, u32[]{:S(2)}, u32[]{:S(2)}) collective-permute-start(bf16[64,1024]{1,0:T(8,128)(2,1)S(1)} %get-tuple-element.43), channel_id=1, source_target_pairs={{0,1},{1,0},{2,3},{3,2},{4,5},{5,4},{6,7},{7,6},{8,9},{9,8},{10,11... | collective-permute-start | bytes 393224 | tf_op jit(solution)/shard_map/ppermute | solution.py:536
  60.1 1.7 %collective-permute-start.8 = (bf16[64,1024]{1,0:T(8,128)(2,1)S(1)}, bf16[64,1024]{1,0:T(8,128)(2,1)S(1)}, u32[]{:S(2)}, u32[]{:S(2)}) collective-permute-start(bf16[64,1024]{1,0:T(8,128)(2,1)S(1)} %get-tuple-element.45), channel_id=1, source_target_pairs={{0,1},{1,0},{2,3},{3,2},{4,5},{5,4},{6,7},{7,6},{8,9},{9,8},{10,11... | collective-permute-start | bytes 393224 | tf_op jit(solution)/shard_map/ppermute | solution.py:536
  60.6 2.6 %collective-permute-start.10 = (f32[16,256]{1,0:T(8,128)S(1)}, f32[16,256]{1,0:T(8,128)S(1)}, u32[]{:S(2)}, u32[]{:S(2)}) collective-permute-start(f32[16,256]{1,0:T(8,128)S(1)} %get-tuple-element.48.refs_0_), channel_id=1, source_target_pairs={{0,2},{2,0},{1,3},{3,1},{4,6},{6,4},{5,7},{7,5},{8,10},{10,8},{9,1... | collective-permute-start | bytes 49160 | tf_op jit(solution)/shard_map/ppermute | solution.py:536
  63.6 2.5 %collective-permute-start.11 = (bf16[64,2560]{1,0:T(8,128)(2,1)S(1)}, bf16[64,2560]{1,0:T(8,128)(2,1)S(1)}, u32[]{:S(2)}, u32[]{:S(2)}) collective-permute-start(bf16[64,2560]{1,0:T(8,128)(2,1)S(1)} %get-tuple-element.50), channel_id=1, source_target_pairs={{0,1},{1,0},{2,3},{3,2},{4,5},{5,4},{6,7},{7,6},{8,9},{9,8},{10,11... | collective-permute-start | bytes 983048 | tf_op jit(solution)/shard_map/ppermute | solution.py:536
  66.5 7.5 %collective-permute-start.12 = (bf16[16,6656]{1,0:T(8,128)(2,1)S(1)}, bf16[16,6656]{1,0:T(8,128)(2,1)S(1)}, u32[]{:S(2)}, u32[]{:S(2)}) collective-permute-start(bf16[16,6656]{1,0:T(8,128)(2,1)S(1)} %get-tuple-element.52), channel_id=1, source_target_pairs={{0,8},{4,12},{8,0},{12,4},{1,9},{5,13},{9,1},{13,5},{2,10},{6,14},... | collective-permute-start | bytes 638984 | tf_op jit(solution)/shard_map/ppermute | solution.py:541
  66.6 15.2 %collective-permute-start.13 = (bf16[16,6656]{1,0:T(8,128)(2,1)S(1)}, bf16[16,6656]{1,0:T(8,128)(2,1)S(1)}, u32[]{:S(2)}, u32[]{:S(2)}) collective-permute-start(bf16[16,6656]{1,0:T(8,128)(2,1)S(1)} %get-tuple-element.53), channel_id=1, source_target_pairs={{0,4},{4,8},{8,12},{12,0},{1,5},{5,9},{9,13},{13,1},{2,6},{6,10},{... | collective-permute-start | bytes 638984 | tf_op jit(solution)/shard_map/ppermute | solution.py:541
  66.7 17.3 %collective-permute-start.14 = (bf16[16,6656]{1,0:T(8,128)(2,1)S(1)}, bf16[16,6656]{1,0:T(8,128)(2,1)S(1)}, u32[]{:S(2)}, u32[]{:S(2)}) collective-permute-start(bf16[16,6656]{1,0:T(8,128)(2,1)S(1)} %get-tuple-element.54), channel_id=1, source_target_pairs={{0,12},{4,0},{8,4},{12,8},{1,13},{5,1},{9,5},{13,9},{2,14},{6,2},{... | collective-permute-start | bytes 638984 | tf_op jit(solution)/shard_map/ppermute | solution.py:541
  84.1 10.7 %collective-permute-start.17 = (bf16[16,6656]{1,0:T(8,128)(2,1)S(1)}, bf16[16,6656]{1,0:T(8,128)(2,1)S(1)}, u32[]{:S(2)}, u32[]{:S(2)}) collective-permute-start(bf16[16,6656]{1,0:T(8,128)(2,1)S(1)} %sum_grads.1.refs_0_), channel_id=1, source_target_pairs={{0,8},{4,12},{8,0},{12,4},{1,9},{5,13},{9,1},{13,5},{2,10},{6,14},... | collective-permute-start | bytes 638984 | tf_op jit(solution)/shard_map/ppermute | solution.py:541
  85.0 18.6 %collective-permute-start.16 = (bf16[16,6656]{1,0:T(8,128)(2,1)S(1)}, bf16[16,6656]{1,0:T(8,128)(2,1)S(1)}, u32[]{:S(2)}, u32[]{:S(2)}) collective-permute-start(bf16[16,6656]{1,0:T(8,128)(2,1)S(1)} %sum_grads.1.refs_0_), channel_id=1, source_target_pairs={{0,4},{4,8},{8,12},{12,0},{1,5},{5,9},{9,13},{13,1},{2,6},{6,10},{... | collective-permute-start | bytes 638984 | tf_op jit(solution)/shard_map/ppermute | solution.py:541
  85.0 18.6 %collective-permute-start.15 = (bf16[16,6656]{1,0:T(8,128)(2,1)S(1)}, bf16[16,6656]{1,0:T(8,128)(2,1)S(1)}, u32[]{:S(2)}, u32[]{:S(2)}) collective-permute-start(bf16[16,6656]{1,0:T(8,128)(2,1)S(1)} %sum_grads.1.refs_0_), channel_id=1, source_target_pairs={{0,12},{4,0},{8,4},{12,8},{1,13},{5,1},{9,5},{13,9},{2,14},{6,2},{... | collective-permute-start | bytes 638984 | tf_op jit(solution)/shard_map/ppermute | solution.py:541
  103.7 2.7 %collective-permute-start.18 = (bf16[64,6656]{1,0:T(8,128)(2,1)S(1)}, bf16[64,6656]{1,0:T(8,128)(2,1)S(1)}, u32[]{:S(2)}, u32[]{:S(2)}) collective-permute-start(bf16[64,6656]{1,0:T(8,128)(2,1)S(1)} %gather_grads.1.block), channel_id=1, source_target_pairs={{0,1},{1,0},{2,3},{3,2},{4,5},{5,4},{6,7},{7,6},{8,9},{9,8},{10,11... | collective-permute-start | bytes 2555912 | tf_op jit(solution)/shard_map/ppermute | solution.py:536

commit v6 on v5

--- a/solution.py
+++ b/solution.py
@@ -15,7 +15,7 @@
 TAIL = 16
 VMEM_BYTES = 48 * 1024 * 1024
 VMEM_MOST = 60 * 1024 * 1024
-VMEM_HEADS = 48 * 1024 * 1024
+VMEM_HEADS = 52 * 1024 * 1024
 
 VM = pl.BlockSpec(memory_space=pltpu.VMEM)
 SM = pl.BlockSpec(memory_space=pltpu.SMEM)
@@ -596,7 +596,7 @@
         swapped = [(keep, swap_over(send, "sub")) for keep, send in pairs]
         keep, send = small_call(
             functools.partial(split_kernel, tenants, rank), "split_grads", halves_of(tall, width),
-            one, other, info, normed_inputs, after=[got for _, got in swapped],
+            one, other, info, normed_inputs, after=[swapped[-1][1]],
         )
         shards = scatter(*swapped, (keep, swap_over(send, "sub")))
         half = gather(spread(add_up(exchange(shards))))

time: 110 us -> 112 us (1.018)
  the two profiles are of different devices: /device:TPU:9 before, /device:TPU:15 now
where the time goes in v6:
time: 112 us; the launch traced here: 111 us
  waiting for transfers between devices  43 us (38%)
  Pallas kernels  36.4 us (32%)
  starting transfers between devices  29.9 us (27%)
    ppermute x6, waiting for transfers between devices, rotate_over(): return lax.ppermute(block, axis, [(i, (i + d) % size) for i in range(size)])  34.5 us
    pallas_call x3, Pallas kernels, attention(): pl.pallas_call(kernel, grid=(count,), out_shape=[jax.ShapeDtypeStruct((ro...  27.4 us
    ppermute x4, starting transfers between devices, shift_over(): return lax.ppermute(block, axis, [(i, i + 1) for i in range(size - 1)])  14.6 us
    ppermute x6, starting transfers between devices, rotate_over(): return lax.ppermute(block, axis, [(i, (i + d) % size) for i in range(size)])  10.3 us
    ppermute x9, waiting for transfers between devices, swap_over(): return lax.ppermute(block, axis, [(0, 1), (1, 0)])  7.07 us
    ppermute x9, starting transfers between devices, swap_over(): return lax.ppermute(block, axis, [(0, 1), (1, 0)])  4.89 us
    pallas_call x1, Pallas kernels, down_project(): pl.pallas_call(functools.partial(down_kernel, tenants, rank), out_shape=j...  3.36 us
    pallas_call x2, Pallas kernels, finish(): pl.pallas_call(functools.partial(finish_kernel, before is not None), out_...  2.53 us
  transfers between devices with their start and end apart: 19, of which 12 were waited for; matrix products, arithmetic and copies ran while one was open for 0% of the time, Pallas kernels for 17%

profile of v6, /device:TPU:15, one launch (start us, length us, event | category | flops | bytes accessed | tf_op | source)
XLA Modules:
  0.0 111.0 jit_solution(4563466045722576935)
XLA Ops:
  0.6 1.9 %pack_keys_values.1 = (bf16[272,512]{1,0:T(8,128)(2,1)}, bf16[272,512]{1,0:T(8,128)(2,1)}) custom-call(bf16[256,512]{1,0:T(8,128)(2,1)} %keys.1, bf16[256,512]{1,0:T(8,128)(2,1)} %values.1, s32[1,256]{1,0:T(1,128)} %bitcast.15), custom_call_target="tpu_custom_call" | custom-call | bytes 1048576 | tf_op jit(solution)/shard_map/pack_keys_values/pallas_call | solution.py:70
  2.5 0.0 copy-start
  2.5 0.0 copy-start.5
  2.5 3.3 %collective-permute-start.1 = (bf16[272,512]{1,0:T(8,128)(2,1)}, bf16[272,512]{1,0:T(8,128)(2,1)S(1)}, u32[]{:S(2)}, u32[]{:S(2)}) collective-permute-start(bf16[272,512]{1,0:T(8,128)(2,1)} %get-tuple-element.32.own.refs_3_.refs_4_.refs_11_), channel_id=1, source_target_pairs={{0,4},{4,8},{8,12},{1,5},{5,9},{9,13},{2,6},{6,10},{10,14},{3,7},{... | collective-permute-start | bytes 835592 | tf_op jit(solution)/shard_map/ppermute | solution.py:552
  5.9 3.4 %down_project.1.refs_0_.refs_1_ = f32[24,256]{1,0:T(8,128)} custom-call(bf16[256,2560]{1,0:T(8,128)(2,1)} %refs_3_.1, bf16[128,2560]{1,0:T(8,128)(2,1)} %bitcast.14, s32[1,256]{1,0:T(1,128)} %bitcast.16, s32[16]{0:T(128)} %tenant_of.1), custom_call_target="tpu_custom_call" | custom-call | flops 167772160 | bytes 1966080 | tf_op jit(solution)/shard_map/down_project/pallas_call | solution.py:156
  9.3 0.3 collective-permute-start.2
  9.6 2.9 %collective-permute-done.2.refs_2_ = f32[24,256]{1,0:T(8,128)S(1)} collective-permute-done((f32[24,256]{1,0:T(8,128)}, f32[24,256]{1,0:T(8,128)S(1)}, u32[]{:S(2)}, u32[]{:S(2)}) %collective-permute-start.2) | collective-permute-done | bytes 24608 | tf_op jit(solution)/shard_map/ppermute | solution.py:536
  12.5 0.7 copy-done.6
  13.3 0.1 relay_block.2
  13.4 0.0 copy-start.1
  13.4 4.9 %collective-permute-start.4 = (bf16[272,512]{1,0:T(8,128)(2,1)S(1)}, bf16[272,512]{1,0:T(8,128)(2,1)S(1)}, u32[]{:S(2)}, u32[]{:S(2)}) collective-permute-start(bf16[272,512]{1,0:T(8,128)(2,1)S(1)} %get-tuple-element.34), channel_id=1, source_target_pairs={{0,1},{1,4},{4,5},{5,8},{8,9},{9,12},{12,13},{2,3},{3,6},{6,7},{7,... | collective-permute-start | bytes 835592 | tf_op jit(solution)/shard_map/ppermute | solution.py:552
  18.3 0.1 collective-permute-start.3
  18.4 2.0 %collective-permute-start = (bf16[272,512]{1,0:T(8,128)(2,1)S(1)}, bf16[272,512]{1,0:T(8,128)(2,1)S(1)}, u32[]{:S(2)}, u32[]{:S(2)}) collective-permute-start(bf16[272,512]{1,0:T(8,128)(2,1)S(1)} %copy-done.5), channel_id=1, source_target_pairs={{0,4},{4,8},{8,12},{1,5},{5,9},{9,13},{2,6},{6,10},{10,14},{3,7},{... | collective-permute-start | bytes 835592 | tf_op jit(solution)/shard_map/ppermute | solution.py:552
  20.4 1.4 %collective-permute-done.4.refs_9_.refs_10_.refs_14_ = bf16[272,512]{1,0:T(8,128)(2,1)S(1)} collective-permute-done((bf16[272,512]{1,0:T(8,128)(2,1)S(1)}, bf16[272,512]{1,0:T(8,128)(2,1)S(1)}, u32[]{:S(2)}, u32[]{:S(2)}) %collective-permute-start.4) | collective-permute-done | bytes 278560 | tf_op jit(solution)/shard_map/ppermute | solution.py:552
  21.8 7.2 %attention.3 = (bf16[256,4096]{1,0:T(8,128)(2,1)}, bf16[64,1024]{1,0:T(8,128)(2,1)S(1)}, bf16[64,1024]{1,0:T(8,128)(2,1)S(1)}, f32[16,256]{1,0:T(8,128)S(1)}) custom-call(bf16[256,4096]{1,0:T(8,128)(2,1)} %refs_0_.5, bf16[256,4096]{1,0:T(8,128)(2,1)} %refs_1_.5, bf16[128,4096]{1,0:T(8,128)(2,1)} %bitcast.9, bf16[272,512]{1,0:T(8,128)(2,1)S(1)} %copy-done, ...), custom_call_target="tpu_custom_call" | custom-call | flops 2147483648 | bytes 1572864 | tf_op jit(solution)/shard_map/attention/pallas_call | solution.py:345
  29.0 0.1 relay_block.3
  29.1 4.4 %collective-permute-start.6 = (bf16[272,512]{1,0:T(8,128)(2,1)S(1)}, bf16[272,512]{1,0:T(8,128)(2,1)S(1)}, u32[]{:S(2)}, u32[]{:S(2)}) collective-permute-start(bf16[272,512]{1,0:T(8,128)(2,1)S(1)} %get-tuple-element.37), channel_id=1, source_target_pairs={{0,1},{1,4},{4,5},{5,8},{8,9},{9,12},{12,13},{2,3},{3,6},{6,7},{7,... | collective-permute-start | bytes 835592 | tf_op jit(solution)/shard_map/ppermute | solution.py:552
  33.5 0.1 collective-permute-start.5
  33.6 7.4 %attention.4 = (bf16[256,4096]{1,0:T(8,128)(2,1)}, bf16[64,1024]{1,0:T(8,128)(2,1)S(1)}, bf16[64,1024]{1,0:T(8,128)(2,1)S(1)}, f32[16,256]{1,0:T(8,128)S(1)}) custom-call(bf16[256,4096]{1,0:T(8,128)(2,1)} %refs_0_.5, bf16[256,4096]{1,0:T(8,128)(2,1)} %refs_1_.5, bf16[128,4096]{1,0:T(8,128)(2,1)} %bitcast.10, ...), custom_call_target="tpu_custom_call", output_to_operand_aliasing={{0}: (17, {})} | custom-call | flops 2147483648 | bytes 1572864 | tf_op jit(solution)/shard_map/attention/pallas_call | solution.py:345
  41.1 12.8 %attention.5 = (bf16[256,4096]{1,0:T(8,128)(2,1)}, bf16[64,2048]{1,0:T(8,128)(2,1)S(1)}, bf16[64,2048]{1,0:T(8,128)(2,1)S(1)}, f32[16,256]{1,0:T(8,128)S(1)}) custom-call(bf16[256,4096]{1,0:T(8,128)(2,1)} %refs_0_.5, bf16[256,4096]{1,0:T(8,128)(2,1)} %refs_1_.5, bf16[128,4096]{1,0:T(8,128)(2,1)} %bitcast.11, ...), custom_call_target="tpu_custom_call", output_to_operand_aliasing={{0}: (17, {})} | custom-call | flops 4294967296 | bytes 3145728 | tf_op jit(solution)/shard_map/attention/pallas_call | solution.py:345
  53.8 0.4 collective-permute-start.9
  54.3 0.3 collective-permute-start.10
  54.6 2.3 %collective-permute-done.10.refs_1_ = f32[16,256]{1,0:T(8,128)S(1)} collective-permute-done((f32[16,256]{1,0:T(8,128)S(1)}, f32[16,256]{1,0:T(8,128)S(1)}, u32[]{:S(2)}, u32[]{:S(2)}) %collective-permute-start.10) | collective-permute-done | bytes 16416 | tf_op jit(solution)/shard_map/ppermute | solution.py:536
  56.9 0.4 split_grads.1
  57.3 1.3 %collective-permute-start.11 = (bf16[64,2560]{1,0:T(8,128)(2,1)S(1)}, bf16[64,2560]{1,0:T(8,128)(2,1)S(1)}, u32[]{:S(2)}, u32[]{:S(2)}) collective-permute-start(bf16[64,2560]{1,0:T(8,128)(2,1)S(1)} %get-tuple-element.50), channel_id=1, source_target_pairs={{0,1},{1,0},{2,3},{3,2},{4,5},{5,4},{6,7},{7,6},{8,9},{9,8},{10,11... | collective-permute-start | bytes 983048 | tf_op jit(solution)/shard_map/ppermute | solution.py:536
  58.6 0.1 collective-permute-start.7
  58.7 0.4 collective-permute-start.8
  59.1 0.9 collective-permute-done.7.refs_1_
  60.0 0.2 collective-permute-done.8.refs_3_
  60.2 0.4 scatter_grads.1
  60.6 6.5 %collective-permute-start.12 = (bf16[16,6656]{1,0:T(8,128)(2,1)S(1)}, bf16[16,6656]{1,0:T(8,128)(2,1)S(1)}, u32[]{:S(2)}, u32[]{:S(2)}) collective-permute-start(bf16[16,6656]{1,0:T(8,128)(2,1)S(1)} %get-tuple-element.52), channel_id=1, source_target_pairs={{0,8},{4,12},{8,0},{12,4},{1,9},{5,13},{9,1},{13,5},{2,10},{6,14},... | collective-permute-start | bytes 638984 | tf_op jit(solution)/shard_map/ppermute | solution.py:541
  67.2 0.7 collective-permute-start.13
  67.9 1.1 %collective-permute-start.14 = (bf16[16,6656]{1,0:T(8,128)(2,1)S(1)}, bf16[16,6656]{1,0:T(8,128)(2,1)S(1)}, u32[]{:S(2)}, u32[]{:S(2)}) collective-permute-start(bf16[16,6656]{1,0:T(8,128)(2,1)S(1)} %get-tuple-element.54), channel_id=1, source_target_pairs={{0,12},{4,0},{8,4},{12,8},{1,13},{5,1},{9,5},{13,9},{2,14},{6,2},{... | collective-permute-start | bytes 638984 | tf_op jit(solution)/shard_map/ppermute | solution.py:541
  69.0 7.0 %collective-permute-done.12.refs_1_ = bf16[16,6656]{1,0:T(8,128)(2,1)S(1)} collective-permute-done((bf16[16,6656]{1,0:T(8,128)(2,1)S(1)}, bf16[16,6656]{1,0:T(8,128)(2,1)S(1)}, u32[]{:S(2)}, u32[]{:S(2)}) %collective-permute-start.12) | collective-permute-done | bytes 213024 | tf_op jit(solution)/shard_map/ppermute | solution.py:541
  76.0 9.1 %collective-permute-done.13.refs_2_ = bf16[16,6656]{1,0:T(8,128)(2,1)S(1)} collective-permute-done((bf16[16,6656]{1,0:T(8,128)(2,1)S(1)}, bf16[16,6656]{1,0:T(8,128)(2,1)S(1)}, u32[]{:S(2)}, u32[]{:S(2)}) %collective-permute-start.13) | collective-permute-done | bytes 213024 | tf_op jit(solution)/shard_map/ppermute | solution.py:541
  85.2 1.5 %collective-permute-done.14.refs_3_ = bf16[16,6656]{1,0:T(8,128)(2,1)S(1)} collective-permute-done((bf16[16,6656]{1,0:T(8,128)(2,1)S(1)}, bf16[16,6656]{1,0:T(8,128)(2,1)S(1)}, u32[]{:S(2)}, u32[]{:S(2)}) %collective-permute-start.14) | collective-permute-done | bytes 213024 | tf_op jit(solution)/shard_map/ppermute | solution.py:541
  86.7 0.1 sum_grads.1.refs_0_
  86.8 0.1 collective-permute-start.17
  86.9 0.8 collective-permute-start.16
  87.6 1.1 %collective-permute-start.15 = (bf16[16,6656]{1,0:T(8,128)(2,1)S(1)}, bf16[16,6656]{1,0:T(8,128)(2,1)S(1)}, u32[]{:S(2)}, u32[]{:S(2)}) collective-permute-start(bf16[16,6656]{1,0:T(8,128)(2,1)S(1)} %sum_grads.1.refs_0_), channel_id=1, source_target_pairs={{0,12},{4,0},{8,4},{12,8},{1,13},{5,1},{9,5},{13,9},{2,14},{6,2},{... | collective-permute-start | bytes 638984 | tf_op jit(solution)/shard_map/ppermute | solution.py:541
  88.7 7.0 %collective-permute-done.17.refs_3_ = bf16[16,6656]{1,0:T(8,128)(2,1)S(1)} collective-permute-done((bf16[16,6656]{1,0:T(8,128)(2,1)S(1)}, bf16[16,6656]{1,0:T(8,128)(2,1)S(1)}, u32[]{:S(2)}, u32[]{:S(2)}) %collective-permute-start.17) | collective-permute-done | bytes 213024 | tf_op jit(solution)/shard_map/ppermute | solution.py:541
  95.8 9.3 %collective-permute-done.16.refs_2_ = bf16[16,6656]{1,0:T(8,128)(2,1)S(1)} collective-permute-done((bf16[16,6656]{1,0:T(8,128)(2,1)S(1)}, bf16[16,6656]{1,0:T(8,128)(2,1)S(1)}, u32[]{:S(2)}, u32[]{:S(2)}) %collective-permute-start.16) | collective-permute-done | bytes 213024 | tf_op jit(solution)/shard_map/ppermute | solution.py:541
  105.0 0.6 collective-permute-done.15.refs_1_
  105.6 0.1 gather_grads.1.block
  105.7 1.9 %collective-permute-start.18 = (bf16[64,6656]{1,0:T(8,128)(2,1)S(1)}, bf16[64,6656]{1,0:T(8,128)(2,1)S(1)}, u32[]{:S(2)}, u32[]{:S(2)}) collective-permute-start(bf16[64,6656]{1,0:T(8,128)(2,1)S(1)} %gather_grads.1.block), channel_id=1, source_target_pairs={{0,1},{1,0},{2,3},{3,2},{4,5},{5,4},{6,7},{7,6},{8,9},{9,8},{10,11... | collective-permute-start | bytes 2555912 | tf_op jit(solution)/shard_map/ppermute | solution.py:536
  107.6 1.3 %finish_grads.2 = (f32[128,4096]{1,0:T(8,128)}, f32[128,2560]{1,0:T(8,128)}) custom-call(bf16[64,6656]{1,0:T(8,128)(2,1)S(1)} %gather_grads.1.block), custom_call_target="tpu_custom_call" | custom-call | flops 425984 | bytes 2555904 | tf_op jit(solution)/shard_map/finish_grads/pallas_call | solution.py:479
  108.9 0.7 collective-permute-done.18.block
  109.6 1.3 %finish_grads.3 = (f32[128,4096]{1,0:T(8,128)}, f32[128,2560]{1,0:T(8,128)}) custom-call(bf16[64,6656]{1,0:T(8,128)(2,1)S(1)} %collective-permute-done.18.block, f32[128,4096]{1,0:T(8,128)} %get-tuple-element.55.refs_0_, f32[128,2560]{1,0:T(8,128)} %get-tuple-element.56.refs_1_), custom_call_target="tpu_custom_call", output_to_operand_aliasing={{0}: (1, {}), {1}: (2, {})} | custom-call | flops 425984 | bytes 2555904 | tf_op jit(solution)/shard_map/finish_grads/pallas_call | solution.py:479
  (18 shorter events, 0.0 us)
Async XLA Ops:
  2.5 10.7 %copy-start = (bf16[272,512]{1,0:T(8,128)(2,1)S(1)}, bf16[272,512]{1,0:T(8,128)(2,1)}, u32[]{:S(2)}) copy-start(bf16[272,512]{1,0:T(8,128)(2,1)} %get-tuple-element.32.own.refs_3_.refs_4_.refs_11_) | copy-start | bytes 835588
  2.5 15.8 %copy-start.5 = (bf16[272,512]{1,0:T(8,128)(2,1)S(1)}, bf16[272,512]{1,0:T(8,128)(2,1)}, u32[]{:S(2)}) copy-start(bf16[272,512]{1,0:T(8,128)(2,1)} %get-tuple-element.31.own.refs_3_.refs_4_) | copy-start | bytes 835588
  2.5 10.7 %collective-permute-start.1 = (bf16[272,512]{1,0:T(8,128)(2,1)}, bf16[272,512]{1,0:T(8,128)(2,1)S(1)}, u32[]{:S(2)}, u32[]{:S(2)}) collective-permute-start(bf16[272,512]{1,0:T(8,128)(2,1)} %get-tuple-element.32.own.refs_3_.refs_4_.refs_11_), channel_id=1, source_target_pairs={{0,4},{4,8},{8,12},{1,5},{5,9},{9,13},{2,6},{6,10},{10,14},{3,7},{... | collective-permute-start | bytes 835592 | tf_op jit(solution)/shard_map/ppermute | solution.py:552
  9.3 3.2 %collective-permute-start.2 = (f32[24,256]{1,0:T(8,128)}, f32[24,256]{1,0:T(8,128)S(1)}, u32[]{:S(2)}, u32[]{:S(2)}) collective-permute-start(f32[24,256]{1,0:T(8,128)} %down_project.1.refs_0_.refs_1_), channel_id=1, source_target_pairs={{0,2},{2,0},{1,3},{3,1},{4,6},{6,4},{5,7},{7,5},{8,10},{10,8},{9,1... | collective-permute-start | bytes 73736 | tf_op jit(solution)/shard_map/ppermute | solution.py:536
  12.5 0.7 copy-start.6
  13.4 20.2 %copy-start.1 = (bf16[272,512]{1,0:T(8,128)(2,1)}, bf16[272,512]{1,0:T(8,128)(2,1)S(1)}, u32[]{:S(2)}) copy-start(bf16[272,512]{1,0:T(8,128)(2,1)S(1)} %get-tuple-element.33.refs_5_.refs_6_.refs_12_) | copy-start | bytes 835588
  13.4 8.4 %collective-permute-start.4 = (bf16[272,512]{1,0:T(8,128)(2,1)S(1)}, bf16[272,512]{1,0:T(8,128)(2,1)S(1)}, u32[]{:S(2)}, u32[]{:S(2)}) collective-permute-start(bf16[272,512]{1,0:T(8,128)(2,1)S(1)} %get-tuple-element.34), channel_id=1, source_target_pairs={{0,1},{1,4},{4,5},{5,8},{8,9},{9,12},{12,13},{2,3},{3,6},{6,7},{7,... | collective-permute-start | bytes 835592 | tf_op jit(solution)/shard_map/ppermute | solution.py:552
  18.3 3.5 %collective-permute-start.3 = (bf16[272,512]{1,0:T(8,128)(2,1)S(1)}, bf16[272,512]{1,0:T(8,128)(2,1)S(1)}, u32[]{:S(2)}, u32[]{:S(2)}) collective-permute-start(bf16[272,512]{1,0:T(8,128)(2,1)S(1)} %get-tuple-element.33.refs_5_.refs_6_.refs_12_), channel_id=1, source_target_pairs={{0,1},{1,0},{2,3},{3,2},{4,5},{5,4},{6,7},{7,6},{8,9},{9,8},{10,11... | collective-permute-start | bytes 835592 | tf_op jit(solution)/shard_map/ppermute | solution.py:536
  18.4 10.6 %collective-permute-start = (bf16[272,512]{1,0:T(8,128)(2,1)S(1)}, bf16[272,512]{1,0:T(8,128)(2,1)S(1)}, u32[]{:S(2)}, u32[]{:S(2)}) collective-permute-start(bf16[272,512]{1,0:T(8,128)(2,1)S(1)} %copy-done.5), channel_id=1, source_target_pairs={{0,4},{4,8},{8,12},{1,5},{5,9},{9,13},{2,6},{6,10},{10,14},{3,7},{... | collective-permute-start | bytes 835592 | tf_op jit(solution)/shard_map/ppermute | solution.py:552
  21.8 11.8 %copy-start.2 = (bf16[272,512]{1,0:T(8,128)(2,1)}, bf16[272,512]{1,0:T(8,128)(2,1)S(1)}, u32[]{:S(2)}) copy-start(bf16[272,512]{1,0:T(8,128)(2,1)S(1)} %collective-permute-done.4.refs_9_.refs_10_.refs_14_) | copy-start | bytes 835588
  21.8 11.8 %copy-start.3 = (bf16[272,512]{1,0:T(8,128)(2,1)}, bf16[272,512]{1,0:T(8,128)(2,1)S(1)}, u32[]{:S(2)}) copy-start(bf16[272,512]{1,0:T(8,128)(2,1)S(1)} %collective-permute-done.3.refs_7_.refs_8_.refs_13_) | copy-start | bytes 835588
  29.1 12.0 %collective-permute-start.6 = (bf16[272,512]{1,0:T(8,128)(2,1)S(1)}, bf16[272,512]{1,0:T(8,128)(2,1)S(1)}, u32[]{:S(2)}, u32[]{:S(2)}) collective-permute-start(bf16[272,512]{1,0:T(8,128)(2,1)S(1)} %get-tuple-element.37), channel_id=1, source_target_pairs={{0,1},{1,4},{4,5},{5,8},{8,9},{9,12},{12,13},{2,3},{3,6},{6,7},{7,... | collective-permute-start | bytes 835592 | tf_op jit(solution)/shard_map/ppermute | solution.py:552
  33.5 7.6 %collective-permute-start.5 = (bf16[272,512]{1,0:T(8,128)(2,1)S(1)}, bf16[272,512]{1,0:T(8,128)(2,1)S(1)}, u32[]{:S(2)}, u32[]{:S(2)}) collective-permute-start(bf16[272,512]{1,0:T(8,128)(2,1)S(1)} %get-tuple-element.36.refs_5_.refs_6_), channel_id=1, source_target_pairs={{0,1},{1,0},{2,3},{3,2},{4,5},{5,4},{6,7},{7,6},{8,9},{9,8},{10,11... | collective-permute-start | bytes 835592 | tf_op jit(solution)/shard_map/ppermute | solution.py:536
  41.1 15.8 %copy-start.4 = (bf16[256,2560]{1,0:T(8,128)(2,1)S(1)}, bf16[256,2560]{1,0:T(8,128)(2,1)}, u32[]{:S(2)}) copy-start(bf16[256,2560]{1,0:T(8,128)(2,1)} %refs_3_.1) | copy-start | bytes 3932164
  53.8 3.0 %collective-permute-start.9 = (bf16[64,2048]{1,0:T(8,128)(2,1)S(1)}, bf16[64,2048]{1,0:T(8,128)(2,1)S(1)}, u32[]{:S(2)}, u32[]{:S(2)}) collective-permute-start(bf16[64,2048]{1,0:T(8,128)(2,1)S(1)} %get-tuple-element.47), channel_id=1, source_target_pairs={{0,1},{1,0},{2,3},{3,2},{4,5},{5,4},{6,7},{7,6},{8,9},{9,8},{10,11... | collective-permute-start | bytes 786440 | tf_op jit(solution)/shard_map/ppermute | solution.py:536
  54.3 2.6 %collective-permute-start.10 = (f32[16,256]{1,0:T(8,128)S(1)}, f32[16,256]{1,0:T(8,128)S(1)}, u32[]{:S(2)}, u32[]{:S(2)}) collective-permute-start(f32[16,256]{1,0:T(8,128)S(1)} %get-tuple-element.48.refs_0_), channel_id=1, source_target_pairs={{0,2},{2,0},{1,3},{3,1},{4,6},{6,4},{5,7},{7,5},{8,10},{10,8},{9,1... | collective-permute-start | bytes 49160 | tf_op jit(solution)/shard_map/ppermute | solution.py:536
  57.3 2.9 %collective-permute-start.11 = (bf16[64,2560]{1,0:T(8,128)(2,1)S(1)}, bf16[64,2560]{1,0:T(8,128)(2,1)S(1)}, u32[]{:S(2)}, u32[]{:S(2)}) collective-permute-start(bf16[64,2560]{1,0:T(8,128)(2,1)S(1)} %get-tuple-element.50), channel_id=1, source_target_pairs={{0,1},{1,0},{2,3},{3,2},{4,5},{5,4},{6,7},{7,6},{8,9},{9,8},{10,11... | collective-permute-start | bytes 983048 | tf_op jit(solution)/shard_map/ppermute | solution.py:536
  58.6 1.4 %collective-permute-start.7 = (bf16[64,1024]{1,0:T(8,128)(2,1)S(1)}, bf16[64,1024]{1,0:T(8,128)(2,1)S(1)}, u32[]{:S(2)}, u32[]{:S(2)}) collective-permute-start(bf16[64,1024]{1,0:T(8,128)(2,1)S(1)} %get-tuple-element.43), channel_id=1, source_target_pairs={{0,1},{1,0},{2,3},{3,2},{4,5},{5,4},{6,7},{7,6},{8,9},{9,8},{10,11... | collective-permute-start | bytes 393224 | tf_op jit(solution)/shard_map/ppermute | solution.py:536
  58.7 1.6 %collective-permute-start.8 = (bf16[64,1024]{1,0:T(8,128)(2,1)S(1)}, bf16[64,1024]{1,0:T(8,128)(2,1)S(1)}, u32[]{:S(2)}, u32[]{:S(2)}) collective-permute-start(bf16[64,1024]{1,0:T(8,128)(2,1)S(1)} %get-tuple-element.45), channel_id=1, source_target_pairs={{0,1},{1,0},{2,3},{3,2},{4,5},{5,4},{6,7},{7,6},{8,9},{9,8},{10,11... | collective-permute-start | bytes 393224 | tf_op jit(solution)/shard_map/ppermute | solution.py:536
  60.6 15.4 %collective-permute-start.12 = (bf16[16,6656]{1,0:T(8,128)(2,1)S(1)}, bf16[16,6656]{1,0:T(8,128)(2,1)S(1)}, u32[]{:S(2)}, u32[]{:S(2)}) collective-permute-start(bf16[16,6656]{1,0:T(8,128)(2,1)S(1)} %get-tuple-element.52), channel_id=1, source_target_pairs={{0,8},{4,12},{8,0},{12,4},{1,9},{5,13},{9,1},{13,5},{2,10},{6,14},... | collective-permute-start | bytes 638984 | tf_op jit(solution)/shard_map/ppermute | solution.py:541
  67.2 18.0 %collective-permute-start.13 = (bf16[16,6656]{1,0:T(8,128)(2,1)S(1)}, bf16[16,6656]{1,0:T(8,128)(2,1)S(1)}, u32[]{:S(2)}, u32[]{:S(2)}) collective-permute-start(bf16[16,6656]{1,0:T(8,128)(2,1)S(1)} %get-tuple-element.53), channel_id=1, source_target_pairs={{0,4},{4,8},{8,12},{12,0},{1,5},{5,9},{9,13},{13,1},{2,6},{6,10},{... | collective-permute-start | bytes 638984 | tf_op jit(solution)/shard_map/ppermute | solution.py:541
  67.9 18.8 %collective-permute-start.14 = (bf16[16,6656]{1,0:T(8,128)(2,1)S(1)}, bf16[16,6656]{1,0:T(8,128)(2,1)S(1)}, u32[]{:S(2)}, u32[]{:S(2)}) collective-permute-start(bf16[16,6656]{1,0:T(8,128)(2,1)S(1)} %get-tuple-element.54), channel_id=1, source_target_pairs={{0,12},{4,0},{8,4},{12,8},{1,13},{5,1},{9,5},{13,9},{2,14},{6,2},{... | collective-permute-start | bytes 638984 | tf_op jit(solution)/shard_map/ppermute | solution.py:541
  86.8 9.0 %collective-permute-start.17 = (bf16[16,6656]{1,0:T(8,128)(2,1)S(1)}, bf16[16,6656]{1,0:T(8,128)(2,1)S(1)}, u32[]{:S(2)}, u32[]{:S(2)}) collective-permute-start(bf16[16,6656]{1,0:T(8,128)(2,1)S(1)} %sum_grads.1.refs_0_), channel_id=1, source_target_pairs={{0,8},{4,12},{8,0},{12,4},{1,9},{5,13},{9,1},{13,5},{2,10},{6,14},... | collective-permute-start | bytes 638984 | tf_op jit(solution)/shard_map/ppermute | solution.py:541
  86.9 18.2 %collective-permute-start.16 = (bf16[16,6656]{1,0:T(8,128)(2,1)S(1)}, bf16[16,6656]{1,0:T(8,128)(2,1)S(1)}, u32[]{:S(2)}, u32[]{:S(2)}) collective-permute-start(bf16[16,6656]{1,0:T(8,128)(2,1)S(1)} %sum_grads.1.refs_0_), channel_id=1, source_target_pairs={{0,4},{4,8},{8,12},{12,0},{1,5},{5,9},{9,13},{13,1},{2,6},{6,10},{... | collective-permute-start | bytes 638984 | tf_op jit(solution)/shard_map/ppermute | solution.py:541
  87.6 18.0 %collective-permute-start.15 = (bf16[16,6656]{1,0:T(8,128)(2,1)S(1)}, bf16[16,6656]{1,0:T(8,128)(2,1)S(1)}, u32[]{:S(2)}, u32[]{:S(2)}) collective-permute-start(bf16[16,6656]{1,0:T(8,128)(2,1)S(1)} %sum_grads.1.refs_0_), channel_id=1, source_target_pairs={{0,12},{4,0},{8,4},{12,8},{1,13},{5,1},{9,5},{13,9},{2,14},{6,2},{... | collective-permute-start | bytes 638984 | tf_op jit(solution)/shard_map/ppermute | solution.py:541
  105.7 3.9 %collective-permute-start.18 = (bf16[64,6656]{1,0:T(8,128)(2,1)S(1)}, bf16[64,6656]{1,0:T(8,128)(2,1)S(1)}, u32[]{:S(2)}, u32[]{:S(2)}) collective-permute-start(bf16[64,6656]{1,0:T(8,128)(2,1)S(1)} %gather_grads.1.block), channel_id=1, source_target_pairs={{0,1},{1,0},{2,3},{3,2},{4,5},{5,4},{6,7},{7,6},{8,9},{9,8},{10,11... | collective-permute-start | bytes 2555912 | tf_op jit(solution)/shard_map/ppermute | solution.py:536
